TPU v7x, 512 devices: a whole 4x8x8 slice. The times are simulated.
512 devices in a mesh: dp: 16 (over x, y_lo), pipe: 8 (over z), expert: 4 (over y_hi, core).
Axes of the slice: x: 4, y: 8 (y_hi: 2, y_lo: 4; y = y_hi * 4 + y_lo), z: 8, core: 2. Of those that a mesh axis runs over, the one named last changes fastest.
Arguments:
- activations: bfloat16 [16, 8, 2, 384, 7168], P('dp', 'pipe', None, None, 'expert'), may hold values from -6 to 6
- out_grads: bfloat16 [16, 8, 2, 384, 576], P('dp', 'pipe', None, 'expert'), may hold values from -0.119628906 to 0.119628906
- counts: int32 [16, 8, 2], P('dp', 'pipe'), may hold values from 96 to 384, as said below
- first_moment: float32 [8, 4, 1792, 576], P('pipe', 'expert', 'dp'), may hold values from -1.8 to 1.8
- second_moment: float32 [8, 4, 1792, 576], P('pipe', 'expert', 'dp'), may hold values from 0.05 to 2
Outputs:
- new_first: float32 [8, 4, 1792, 576], P('pipe', 'expert', 'dp')
- new_second: float32 [8, 4, 1792, 576], P('pipe', 'expert', 'dp')
- direction: float32 [8, 4, 1792, 576], P('pipe', 'expert', 'dp')
Inputs may be any that keep to these rules, and one draw needn't show every extreme that they name: `counts`: some span holds 384 live tokens and some span 384 / 4.
All inputs are finite; a program needn't handle non-finite values.
Results may differ from a plain program's by a relative error of at most 0.0003.
Values may be sent and summed in bfloat16 or wider, within the bound.
No kernel may reach another device: no remote copies, remote signals or barrier semaphores. Data moves between devices by JAX's collectives and lax.ppermute only.
A program may use at most 64 MiB of HBM per device.

v0:
```python
import jax
import jax.numpy as jnp
from jax import lax
from jax.sharding import PartitionSpec as P


def from_partner(shard, axis, apart):
    return lax.ppermute(shard, axis, [(i, i ^ 1 << apart) for i in range(lax.axis_size(axis))])


def local(activations, out_grads, counts, first_moment, second_moment):
    inputs = activations[0, 0]
    grads_out = out_grads[0, 0]
    local_rows = grads_out.shape[1]
    first_slot = lax.axis_index("expert") * local_rows
    position = first_slot + lax.broadcasted_iota(jnp.int32, (2, local_rows, 1), 1)
    live = position < counts[0, 0][:, None, None]
    masked = jnp.where(live, grads_out, jnp.zeros_like(grads_out))
    summed = jnp.einsum(
        "ctd,ctf->cdf",
        inputs,
        lax.all_gather(masked, "expert", axis=1, tiled=True),
        preferred_element_type=jnp.float32,
    )
    own_grad = summed[0]
    other_grad = summed[1]
    levels = lax.axis_size("pipe").bit_length() - 1
    for level in range(levels):
        other_grad = from_partner(other_grad, "pipe", level)
    combined = own_grad + other_grad
    grad_rows = lax.psum_scatter(combined, "dp", scatter_dimension=0, tiled=True)
    grad_rows = grad_rows[None, None]
    new_first = 0.9 * first_moment + 0.1 * grad_rows
    new_second = 0.95 * second_moment + 0.05 * grad_rows * grad_rows
    direction = new_first / (jnp.sqrt(new_second) + 1e-08)
    return (new_first, new_second, direction)


def solution(mesh):
    return jax.shard_map(
        local,
        mesh=mesh,
        in_specs=(
            P("dp", "pipe", None, None, "expert"),
            P("dp", "pipe", None, "expert", None),
            P("dp", "pipe", None),
            P("pipe", "expert", "dp", None),
            P("pipe", "expert", "dp", None),
        ),
        out_specs=(
            P("pipe", "expert", "dp", None),
            P("pipe", "expert", "dp", None),
            P("pipe", "expert", "dp", None),
        ),
        check_vma=False,
    )
```

profile of v0, /device:TPU:6, one launch (start us, length us, event | category | flops | bytes accessed | tf_op | source)
XLA Modules:
  0.0 627.7 jit_solution(13152129516587636190)
XLA Ops:
  7.2 0.0 copy-start
  7.2 0.0 reduce-scatter.4.cloned.1.call-start
  7.2 0.9 broadcast_compare_fusion
  8.1 1.0 bitcast_select_fusion
  9.2 16.3 %all_gather.3 = bf16[2,384,576]{2,1,0:T(8,128)(2,1)S(1)} all-gather(bf16[2,96,576]{2,1,0:T(8,128)(2,1)S(1)} %bitcast_select_fusion), channel_id=1, replica_groups=mesh['dp'=16,'pipe'=8,'expert'=4] {'expert'}, dimensions={1}, use_global_device_ids=true | all-gather | bytes 1105920 | tf_op jit(solution)/shard_map/all_gather | solution.py:22
  25.5 0.0 copy-done
  25.5 2.4 convolution_bitcast_fusion
  27.9 0.3 slice_bitcast_fusion
  28.1 4.3 collective-permute-start
  32.4 89.7 %collective-permute-done = f32[1792,576]{0,1:T(8,128)S(1)} collective-permute-done((f32[1792,576]{0,1:T(8,128)S(1)}, f32[1792,576]{0,1:T(8,128)S(1)}, u32[]{:S(2)}, u32[]{:S(2)}) %collective-permute-start) | collective-permute-done | bytes 4128800 | tf_op jit(solution)/shard_map/ppermute | solution.py:8
  122.1 6.1 collective-permute-start.1
  128.2 177.6 %collective-permute-done.1 = f32[1792,576]{0,1:T(8,128)S(1)} collective-permute-done((f32[1792,576]{0,1:T(8,128)S(1)}, f32[1792,576]{0,1:T(8,128)S(1)}, u32[]{:S(2)}, u32[]{:S(2)}) %collective-permute-start.1) | collective-permute-done | bytes 4128800 | tf_op jit(solution)/shard_map/ppermute | solution.py:8
  305.7 8.5 %collective-permute-start.2 = (f32[1792,576]{0,1:T(8,128)S(1)}, f32[1792,576]{0,1:T(8,128)S(1)}, u32[]{:S(2)}, u32[]{:S(2)}) collective-permute-start(f32[1792,576]{0,1:T(8,128)S(1)} %collective-permute-done.1), channel_id=1, source_target_pairs={{0,16},{4,20},{8,24},{12,28},{16,0},{20,4},{24,8},{28,12},{1,17},{... | collective-permute-start | bytes 12386312 | tf_op jit(solution)/shard_map/ppermute | solution.py:8
  314.2 177.7 %collective-permute-done.2 = f32[1792,576]{0,1:T(8,128)S(1)} collective-permute-done((f32[1792,576]{0,1:T(8,128)S(1)}, f32[1792,576]{0,1:T(8,128)S(1)}, u32[]{:S(2)}, u32[]{:S(2)}) %collective-permute-start.2) | collective-permute-done | bytes 4128800 | tf_op jit(solution)/shard_map/ppermute | solution.py:8
  492.0 2.5 fusion
  494.5 5.6 copy.18
  500.1 0.0 copy-start.1
  500.1 0.0 reduce-scatter.4.cloned.1.call-update
  500.1 0.9 copy-done.1
  501.0 0.1 copy.13
  501.2 1.1 copy.14
  502.3 109.3 %reduce-scatter.4.cloned.1.call-done = f32[112,576]{1,0:T(8,128)} async-done(((f32[1792,576]{1,0:T(8,128)}), f32[112,576]{1,0:T(8,128)}) %reduce-scatter.4.cloned.1.call-update) | async-done | bytes 258064
  611.6 1.8 copy.19
  613.4 1.9 add_divide_fusion
  615.4 1.8 copy.15
  617.2 1.8 copy.16
  619.0 1.8 copy.17
  (1 shorter events, 0.0 us)
Async XLA Ops:
  7.2 18.3 %copy-start = (bf16[1,1,2,384,1792]{4,3,2,1,0:T(8,128)(2,1)S(1)}, bf16[1,1,2,384,1792]{4,3,2,1,0:T(8,128)(2,1)}, u32[]{:S(2)}) copy-start(bf16[1,1,2,384,1792]{4,3,2,1,0:T(8,128)(2,1)} %param.5) | copy-start | bytes 8257540
  7.2 604.4 %reduce-scatter.4.cloned.1.call-start = ((), (), s32[]{:S(2)}) async-start(), calls=%async_computation.1 | async-start | bytes 4874240
  28.1 94.0 %collective-permute-start = (f32[1792,576]{0,1:T(8,128)S(1)}, f32[1792,576]{0,1:T(8,128)S(1)}, u32[]{:S(2)}, u32[]{:S(2)}) collective-permute-start(f32[1792,576]{0,1:T(8,128)S(1)} %slice_bitcast_fusion), channel_id=1, source_target_pairs={{0,4},{4,0},{8,12},{12,8},{16,20},{20,16},{24,28},{28,24},{1,5},{5... | collective-permute-start | bytes 12386312 | tf_op jit(solution)/shard_map/ppermute | solution.py:8
  122.1 183.7 %collective-permute-start.1 = (f32[1792,576]{0,1:T(8,128)S(1)}, f32[1792,576]{0,1:T(8,128)S(1)}, u32[]{:S(2)}, u32[]{:S(2)}) collective-permute-start(f32[1792,576]{0,1:T(8,128)S(1)} %collective-permute-done), channel_id=1, source_target_pairs={{0,8},{4,12},{8,0},{12,4},{16,24},{20,28},{24,16},{28,20},{1,9},{5... | collective-permute-start | bytes 12386312 | tf_op jit(solution)/shard_map/ppermute | solution.py:8
  305.7 186.3 %collective-permute-start.2 = (f32[1792,576]{0,1:T(8,128)S(1)}, f32[1792,576]{0,1:T(8,128)S(1)}, u32[]{:S(2)}, u32[]{:S(2)}) collective-permute-start(f32[1792,576]{0,1:T(8,128)S(1)} %collective-permute-done.1), channel_id=1, source_target_pairs={{0,16},{4,20},{8,24},{12,28},{16,0},{20,4},{24,8},{28,12},{1,17},{... | collective-permute-start | bytes 12386312 | tf_op jit(solution)/shard_map/ppermute | solution.py:8
  500.1 1.0 copy-start.1
Sparse Core Ops, SparseCore 0:
  500.2 111.3 reduce-scatter.3
where the time goes:
time: 631 us; the launch traced here: 628 us
  waiting for transfers between devices  554 us (88%)
  starting transfers between devices  18.9 us (3%)
  blocking collectives  16.3 us (3%)
  local copies, waits for them, and re-layouts  15.4 us (2%)
  between operations  14.1 us (2%)
  other arithmetic  6.35 us (1%)
    ppermute x3, waiting for transfers between devices, from_partner(): lax.ppermute(shard, axis, [(i, i ^ 1 << apart) for i in range(lax.axis_si...  445 us
    unnamed x2, waiting for transfers between devices  109 us
    ppermute x3, starting transfers between devices, from_partner(): lax.ppermute(shard, axis, [(i, i ^ 1 << apart) for i in range(lax.axis_si...  18.9 us
    all_gather x1, blocking collectives, local(): lax.all_gather(masked, 'expert', axis=1, tiled=True)  16.3 us
    unnamed x11, local copies, waits for them, and re-layouts  15.1 us
  transfers between devices with their start and end apart: 4, of which 4 were waited for; matrix products, arithmetic and copies ran while one was open for 0% of the time, Pallas kernels for 0%

commit v1 on v0

v1 whole, which is shorter than its diff:
```python
import jax
import jax.numpy as jnp
from jax import lax
from jax.experimental import pallas as pl
from jax.experimental.pallas import tpu as pltpu
from jax.sharding import PartitionSpec as P

AXES = ("dp", "pipe", "expert")
NX, NY = 4, 4
TILE = 256
X_SCALE, Z_SCALE, Y_SCALE = 64.0, 32.0, 16.0


def over_x(step):
    return lambda dp, pipe, expert: ((dp // NY + step) % NX * NY + dp % NY, pipe, expert)


def over_y(bits):
    return lambda dp, pipe, expert: (dp ^ bits, pipe, expert)


def mirrored(dp, pipe, expert):
    return dp, lax.axis_size("pipe") - 1 - pipe, expert


def send(block, to, core):
    sizes = [lax.axis_size(name) for name in AXES]

    def flat(dp, pipe, expert):
        return (dp * sizes[1] + pipe) * sizes[2] + expert

    pairs = [
        (flat(d, p, e), flat(*to(d, p, e)))
        for d in range(sizes[0])
        for p in range(sizes[1])
        for e in range(sizes[2])
        if e % 2 == core
    ]
    return lax.ppermute(block, AXES, pairs)


def transposed_dot(a, b):
    return lax.dot_general(a, b, (((0,), (0,)), ((), ())), preferred_element_type=jnp.float32)


def spans_kernel(counts, acts, grads, own, other, masked_other, masked):
    @pl.when(pl.program_id(0) == 0)
    def _():
        slots = lax.broadcasted_iota(jnp.int32, masked.shape[1:], 0)
        for span in range(2):
            live = slots < counts[span]
            kept = jnp.where(live, grads[span].astype(jnp.float32), 0.0).astype(masked.dtype)
            masked[span] = kept
        masked_other[...] = masked[1]

    own[...] = transposed_dot(acts[0, 0, 0], masked[0])
    other[...] = transposed_dot(acts[0, 0, 1], masked[1])


def both_spans(counts, activations, grads):
    _, _, spans, slots, rows = activations.shape
    width = grads.shape[-1]
    part = jax.ShapeDtypeStruct((rows, width), jnp.float32)
    return pl.pallas_call(
        spans_kernel,
        grid_spec=pltpu.PrefetchScalarGridSpec(
            num_scalar_prefetch=1,
            grid=(rows // TILE,),
            in_specs=[
                pl.BlockSpec((1, 1, spans, slots, TILE), lambda i, c: (0, 0, 0, 0, i)),
                pl.BlockSpec((spans, slots, width), lambda i, c: (0, 0, 0)),
            ],
            out_specs=[
                pl.BlockSpec((TILE, width), lambda i, c: (i, 0)),
                pl.BlockSpec((TILE, width), lambda i, c: (i, 0)),
                pl.BlockSpec((slots, width), lambda i, c: (0, 0)),
            ],
            scratch_shapes=[pltpu.VMEM((spans, slots, width), grads.dtype)],
        ),
        out_shape=[part, part, jax.ShapeDtypeStruct((slots, width), grads.dtype)],
        compiler_params=pltpu.CompilerParams(vmem_limit_bytes=32 << 20),
        cost_estimate=pl.CostEstimate(
            flops=4 * slots * rows * width, bytes_accessed=12 << 20, transcendentals=0
        ),
    )(counts, activations, grads)


def mirror_kernel(acts, grads, base, total):
    total[...] = base[...] + transposed_dot(acts[...], grads[...])


def add_mirror(acts, grads, base):
    slots, rows = acts.shape
    width = grads.shape[-1]
    return pl.pallas_call(
        mirror_kernel,
        grid=(rows // TILE,),
        in_specs=[
            pl.BlockSpec((slots, TILE), lambda i: (0, i)),
            pl.BlockSpec((slots, width), lambda i: (0, 0)),
            pl.BlockSpec((TILE, width), lambda i: (i, 0)),
        ],
        out_specs=pl.BlockSpec((TILE, width), lambda i: (i, 0)),
        out_shape=jax.ShapeDtypeStruct((rows, width), jnp.float32),
        compiler_params=pltpu.CompilerParams(vmem_limit_bytes=32 << 20),
        cost_estimate=pl.CostEstimate(
            flops=2 * slots * rows * width, bytes_accessed=11 << 20, transcendentals=0
        ),
    )(acts, grads, base)


def piece(array, index, pieces):
    rows = array.shape[0] // pieces
    return lax.dynamic_slice_in_dim(array, index * rows, rows, 0)


def narrow(values, scale):
    return (values * scale).astype(jnp.float16)


def widen(values, scale):
    return values.astype(jnp.float32) * (1.0 / scale)


def exchange_x(part, x, core):
    return [
        send(narrow(piece(part, (x + k) % NX, NX), X_SCALE), over_x(k), core)
        for k in range(1, NX)
    ]


def exchange_y(part, y, core):
    return [
        send(narrow(piece(part, y ^ k, NY), Y_SCALE), over_y(k), core) for k in range(1, NY)
    ]


def collect(own, received, scale):
    for block in received:
        own = own + widen(block, scale)
    return own


def local(activations, out_grads, counts, first_moment, second_moment):
    dp = lax.axis_index("dp")
    core = lax.axis_index("expert") % 2
    x, y = dp // NY, dp % NY
    mirror_acts = send(activations[0, 0, 1], mirrored, 0)
    grads = lax.all_gather(out_grads[0, 0], "expert", axis=1, tiled=True)
    own, other, masked_other = both_spans(counts[0, 0], activations, grads)
    mirror_grads = send(masked_other, mirrored, 0)

    other_x = collect(piece(other, x, NX), exchange_x(other, x, 1), X_SCALE)
    own_in = exchange_x(own, x, 1)
    other_z = send(narrow(other_x, Z_SCALE), mirrored, 1)
    quarter_1 = collect(piece(own, x, NX), own_in, X_SCALE) + widen(other_z, Z_SCALE)
    last_1 = exchange_y(quarter_1, y, 1)

    both = add_mirror(mirror_acts, mirror_grads, own)
    quarter_0 = collect(piece(both, x, NX), exchange_x(both, x, 0), X_SCALE)
    last_0 = exchange_y(quarter_0, y, 0)

    rows_1 = collect(piece(quarter_1, y, NY), last_1, Y_SCALE)
    rows_0 = collect(piece(quarter_0, y, NY), last_0, Y_SCALE)
    grad = jnp.where(core == 1, rows_1, rows_0)[None, None]
    new_first = 0.9 * first_moment + 0.1 * grad
    new_second = 0.95 * second_moment + 0.05 * grad * grad
    direction = new_first / (jnp.sqrt(new_second) + 1e-08)
    return (new_first, new_second, direction)


def solution(mesh):
    state = P("pipe", "expert", "dp", None)
    return jax.shard_map(
        local,
        mesh=mesh,
        in_specs=(
            P("dp", "pipe", None, None, "expert"),
            P("dp", "pipe", None, "expert", None),
            P("dp", "pipe", None),
            state,
            state,
        ),
        out_specs=(state, state, state),
        check_vma=False,
    )
```

time: 631 us -> 118 us (0.19)
  waiting for transfers between devices: 554 us -> 18.3 us
  starting transfers between devices: 18.9 us -> 44.3 us
  between operations: 14.1 us -> 0.95 us
  other arithmetic: 6.35 us -> 17 us
  Pallas kernels: 0 us -> 8.02 us
  local copies, waits for them, and re-layouts: 15.4 us -> 8.16 us
    ppermute x3 -> x18, waiting for transfers between devices: 445 us -> 18.3 us  [send(): return lax.ppermute(block, AXES, pairs)]
    unnamed x2 -> x0, waiting for transfers between devices: 109 us -> none
    ppermute x3 -> x18, starting transfers between devices: 18.9 us -> 44.3 us  [send(): return lax.ppermute(block, AXES, pairs)]
    convert_element_type x0 -> x6, other arithmetic: none -> 10.2 us  [narrow(): return (values * scale).astype(jnp.float16)]
    unnamed x11 -> x20, local copies, waits for them, and re-layouts: 15.1 us -> 5.57 us
    pallas_call x0 -> x2, Pallas kernels: none -> 8.02 us  [the longest x1 5.16 us: both_spans(): pl.pallas_call(spans_kernel, grid_spec=pltpu.PrefetchScalarGridSpec(num_s...]
  transfers between devices with their start and end apart: 4 -> 18, of which waited for: 4 -> 4; matrix products, arithmetic and copies ran while one was open for 0% -> 13% of each run, Pallas kernels for 0% -> 7%
where the time goes in v1:
time: 118 us; the launch traced here: 116 us
  starting transfers between devices  44.3 us (38%)
  blocking collectives  19.3 us (16%)
  waiting for transfers between devices  18.3 us (16%)
  other arithmetic  17 us (14%)
  local copies, waits for them, and re-layouts  8.16 us (7%)
  Pallas kernels  8.02 us (7%)
    ppermute x18, starting transfers between devices, send(): return lax.ppermute(block, AXES, pairs)  44.3 us
    all_gather x1, blocking collectives, local(): grads = lax.all_gather(out_grads[0, 0], 'expert', axis=1, tiled=True)  19.3 us
    ppermute x18, waiting for transfers between devices, send(): return lax.ppermute(block, AXES, pairs)  18.3 us
    convert_element_type x6, other arithmetic, narrow(): return (values * scale).astype(jnp.float16)  10.2 us
    unnamed x20, local copies, waits for them, and re-layouts  5.57 us
    pallas_call x1, Pallas kernels, both_spans(): pl.pallas_call(spans_kernel, grid_spec=pltpu.PrefetchScalarGridSpec(num_s...  5.16 us
    pallas_call x1, Pallas kernels, add_mirror(): pl.pallas_call(mirror_kernel, grid=(rows // TILE,), in_specs=[pl.BlockSpe...  2.85 us
    squeeze x1, local copies, waits for them, and re-layouts, local(): mirror_acts = send(activations[0, 0, 1], mirrored, 0)  2.58 us
  transfers between devices with their start and end apart: 18, of which 4 were waited for; matrix products, arithmetic and copies ran while one was open for 13% of the time, Pallas kernels for 7%

profile of v1, /device:TPU:6, one launch (start us, length us, event | category | flops | bytes accessed | tf_op | source)
XLA Modules:
  0.0 116.0 jit_solution(13610276112530835163)
XLA Ops:
  0.6 0.0 copy-start.8
  0.6 2.6 %slice_bitcast_fusion = bf16[384,1792]{1,0:T(8,128)(2,1)} fusion(bf16[1,1,2,384,1792]{4,3,2,1,0:T(8,128)(2,1)} %acts.1), kind=kLoop, calls=%fused_computation | loop fusion | bytes 2752512 | tf_op jit(solution)/shard_map/squeeze | solution.py:148
  3.2 11.1 %collective-permute-start.10 = (bf16[384,1792]{1,0:T(8,128)(2,1)}, bf16[384,1792]{1,0:T(8,128)(2,1)S(1)}, u32[]{:S(2)}, u32[]{:S(2)}) collective-permute-start(bf16[384,1792]{1,0:T(8,128)(2,1)} %slice_bitcast_fusion), channel_id=1, source_target_pairs={{0,28},{2,30},{4,24},{6,26},{8,20},{10,22},{12,16},{14,18},{16,12}... | collective-permute-start | bytes 4128776 | tf_op jit(solution)/shard_map/ppermute | solution.py:39
  14.3 0.0 copy-done.8
  14.3 19.3 %all-gather = bf16[1,1,2,384,576]{4,3,2,1,0:T(8,128)(2,1)S(1)} all-gather(bf16[1,1,2,96,576]{4,3,2,1,0:T(8,128)(2,1)S(1)} %copy-done.8), channel_id=2, replica_groups=mesh['dp'=16,'pipe'=8,'expert'=4] {'expert'}, dimensions={3}, use_global_device_ids=true | all-gather | bytes 1105920 | tf_op jit(solution)/shard_map/all_gather | solution.py:149
  33.6 0.0 copy-done.5
  33.6 1.8 %copy-done.4 = bf16[1,1,2,384,1792]{4,3,2,1,0:T(8,128)(2,1)S(1)} copy-done((bf16[1,1,2,384,1792]{4,3,2,1,0:T(8,128)(2,1)S(1)}, bf16[1,1,2,384,1792]{4,3,2,1,0:T(8,128)(2,1)}, u32[]{:S(2)}) %copy-start.4) | copy-done | bytes 2752536
  35.4 5.2 %shard_map.76 = (f32[1792,576]{1,0:T(8,128)S(1)}, f32[1792,576]{1,0:T(8,128)S(1)}, bf16[384,576]{1,0:T(8,128)(2,1)S(1)}) custom-call(s32[2]{0:T(128)S(1)} %bitcast.13, bf16[1,1,2,384,1792]{4,3,2,1,0:T(8,128)(2,1)S(1)} %copy-done.4, bf16[2,384,576]{2,1,0:T(8,128)(2,1)S(1)} %bitcast.12), custom_call_target="tpu_custom_call" | custom-call | flops 1585446912 | bytes 12582912 | tf_op jit(solution)/shard_map/pallas_call | solution.py:64
  40.6 0.0 copy-start
  40.6 0.0 copy-start.3
  40.6 1.6 %multiply_convert_fusion.6 = (f16[448,576]{1,0:T(8,128)(2,1)S(1)}, f16[448,576]{1,0:T(8,128)(2,1)}, f16[448,576]{1,0:T(8,128)(2,1)}) fusion(f32[1792,576]{1,0:T(8,128)S(1)} %get-tuple-element.7, s32[]{:T(128)S(6)} %select_n.88, s32[]{:T(128)S(6)} %select_n.92, s32[]{:T(128)S(6)} %select_n.90), kind=kLoop, calls=%fused_computation.9 | loop fusion | flops 1548288 | bytes 4644876 | tf_op jit(solution)/shard_map/convert_element_type | solution.py:118
  42.2 0.8 copy-done
  43.0 1.5 %copy-done.3 = f32[1792,576]{1,0:T(8,128)} copy-done((f32[1792,576]{1,0:T(8,128)}, f32[1792,576]{1,0:T(8,128)S(1)}, u32[]{:S(2)}) %copy-start.3) | copy-done | bytes 4128792
  44.5 1.5 %collective-permute-start.3 = (f16[448,576]{1,0:T(8,128)(2,1)S(1)}, f16[448,576]{1,0:T(8,128)(2,1)}, u32[]{:S(2)}, u32[]{:S(2)}) collective-permute-start(f16[448,576]{1,0:T(8,128)(2,1)S(1)} %get-tuple-element.15), channel_id=1, source_target_pairs={{1,129},{3,131},{5,133},{7,135},{9,137},{11,139},{13,141},{15,143}... | collective-permute-start | bytes 1548296 | tf_op jit(solution)/shard_map/ppermute | solution.py:39
  46.0 1.5 %collective-permute-start.5 = (f16[448,576]{1,0:T(8,128)(2,1)}, f16[448,576]{1,0:T(8,128)(2,1)}, u32[]{:S(2)}, u32[]{:S(2)}) collective-permute-start(f16[448,576]{1,0:T(8,128)(2,1)} %get-tuple-element.16), channel_id=1, source_target_pairs={{1,385},{3,387},{5,389},{7,391},{9,393},{11,395},{13,397},{15,399}... | collective-permute-start | bytes 1548296 | tf_op jit(solution)/shard_map/ppermute | solution.py:39
  47.5 1.5 %collective-permute-start.4 = (f16[448,576]{1,0:T(8,128)(2,1)}, f16[448,576]{1,0:T(8,128)(2,1)}, u32[]{:S(2)}, u32[]{:S(2)}) collective-permute-start(f16[448,576]{1,0:T(8,128)(2,1)} %get-tuple-element.17), channel_id=1, source_target_pairs={{1,257},{3,259},{5,261},{7,263},{9,265},{11,267},{13,269},{15,271}... | collective-permute-start | bytes 1548296 | tf_op jit(solution)/shard_map/ppermute | solution.py:39
  48.9 1.9 %collective-permute-start.11 = (bf16[384,576]{1,0:T(8,128)(2,1)S(1)}, bf16[384,576]{1,0:T(8,128)(2,1)S(1)}, u32[]{:S(2)}, u32[]{:S(2)}) collective-permute-start(bf16[384,576]{1,0:T(8,128)(2,1)S(1)} %get-tuple-element.8), channel_id=1, source_target_pairs={{0,28},{2,30},{4,24},{6,26},{8,20},{10,22},{12,16},{14,18},{16,12}... | collective-permute-start | bytes 1327112 | tf_op jit(solution)/shard_map/ppermute | solution.py:39
  50.9 0.0 copy-start.1
  50.9 3.3 %multiply_convert_fusion.9 = (f16[448,576]{1,0:T(8,128)(2,1)S(1)}, f16[448,576]{1,0:T(8,128)(2,1)S(1)}, f16[448,576]{1,0:T(8,128)(2,1)}) fusion(f32[1792,576]{1,0:T(8,128)} %copy-done, s32[]{:T(128)S(6)} %select_n.88, s32[]{:T(128)S(6)} %select_n.92, s32[]{:T(128)S(6)} %select_n.90), kind=kLoop, calls=%fused_computation.12 | loop fusion | flops 1548288 | bytes 4644876 | tf_op jit(solution)/shard_map/convert_element_type | solution.py:118
  54.2 0.0 collective-permute-done.3
  54.2 0.7 collective-permute-start
  54.9 0.0 collective-permute-done.5
  54.9 1.5 %collective-permute-start.2 = (f16[448,576]{1,0:T(8,128)(2,1)S(1)}, f16[448,576]{1,0:T(8,128)(2,1)}, u32[]{:S(2)}, u32[]{:S(2)}) collective-permute-start(f16[448,576]{1,0:T(8,128)(2,1)S(1)} %get-tuple-element.13), channel_id=1, source_target_pairs={{1,385},{3,387},{5,389},{7,391},{9,393},{11,395},{13,397},{15,399}... | collective-permute-start | bytes 1548296 | tf_op jit(solution)/shard_map/ppermute | solution.py:39
  56.3 0.0 collective-permute-done.4
  56.3 1.5 %collective-permute-start.1 = (f16[448,576]{1,0:T(8,128)(2,1)}, f16[448,576]{1,0:T(8,128)(2,1)}, u32[]{:S(2)}, u32[]{:S(2)}) collective-permute-start(f16[448,576]{1,0:T(8,128)(2,1)} %get-tuple-element.14), channel_id=1, source_target_pairs={{1,257},{3,259},{5,261},{7,263},{9,265},{11,267},{13,269},{15,271}... | collective-permute-start | bytes 1548296 | tf_op jit(solution)/shard_map/ppermute | solution.py:39
  57.8 3.0 %multiply_convert_fusion.3 = f16[448,576]{1,0:T(8,128)(2,1)} fusion(f16[448,576]{1,0:T(8,128)(2,1)} %collective-permute-done.5, f16[448,576]{1,0:T(8,128)(2,1)} %collective-permute-done.4, f16[448,576]{1,0:T(8,128)(2,1)} %collective-permute-done.3, f32[1792,576]{1,0:T(8,128)} %copy-done.3, s32[]{:T(128)S(6)} %select_n.86), kind=kLoop, calls=%fused_computation.6 | loop fusion | flops 2838528 | bytes 3096580 | tf_op jit(solution)/shard_map/convert_element_type | solution.py:118
  60.9 5.3 %collective-permute-done.11.grads = bf16[384,576]{1,0:T(8,128)(2,1)S(1)} collective-permute-done((bf16[384,576]{1,0:T(8,128)(2,1)S(1)}, bf16[384,576]{1,0:T(8,128)(2,1)S(1)}, u32[]{:S(2)}, u32[]{:S(2)}) %collective-permute-start.11) | collective-permute-done | bytes 442400 | tf_op jit(solution)/shard_map/ppermute | solution.py:39
  66.1 1.5 %collective-permute-start.6 = (f16[448,576]{1,0:T(8,128)(2,1)}, f16[448,576]{1,0:T(8,128)(2,1)}, u32[]{:S(2)}, u32[]{:S(2)}) collective-permute-start(f16[448,576]{1,0:T(8,128)(2,1)} %multiply_convert_fusion.3), channel_id=1, source_target_pairs={{1,29},{3,31},{5,25},{7,27},{9,21},{11,23},{13,17},{15,19},{17,13}... | collective-permute-start | bytes 1548296 | tf_op jit(solution)/shard_map/ppermute | solution.py:39
  67.6 0.0 collective-permute-done.10.acts
  67.6 0.0 copy-done.1
  67.6 2.9 %shard_map.77 = f32[1792,576]{1,0:T(8,128)S(1)} custom-call(bf16[384,1792]{1,0:T(8,128)(2,1)S(1)} %collective-permute-done.10.acts, bf16[384,576]{1,0:T(8,128)(2,1)S(1)} %collective-permute-done.11.grads, f32[1792,576]{1,0:T(8,128)S(1)} %copy-done.1), custom_call_target="tpu_custom_call" | custom-call | flops 792723456 | bytes 11534336 | tf_op jit(solution)/shard_map/pallas_call | solution.py:95
  70.5 0.0 copy-start.2
  70.5 1.4 %multiply_convert_fusion.2 = (f16[448,576]{1,0:T(8,128)(2,1)}, f16[448,576]{1,0:T(8,128)(2,1)S(1)}, f16[448,576]{1,0:T(8,128)(2,1)S(1)}) fusion(f32[1792,576]{1,0:T(8,128)S(1)} %shard_map.77, s32[]{:T(128)S(6)} %select_n.88, s32[]{:T(128)S(6)} %select_n.92, s32[]{:T(128)S(6)} %select_n.90), kind=kLoop, calls=%fused_computation.4 | loop fusion | flops 1548288 | bytes 4644876 | tf_op jit(solution)/shard_map/convert_element_type | solution.py:118
  71.9 0.9 copy-done.2
  72.8 2.4 %collective-permute-start.12 = (f16[448,576]{1,0:T(8,128)(2,1)}, f16[448,576]{1,0:T(8,128)(2,1)}, u32[]{:S(2)}, u32[]{:S(2)}) collective-permute-start(f16[448,576]{1,0:T(8,128)(2,1)} %get-tuple-element.18), channel_id=1, source_target_pairs={{0,128},{2,130},{4,132},{6,134},{8,136},{10,138},{12,140},{14,142}... | collective-permute-start | bytes 1548296 | tf_op jit(solution)/shard_map/ppermute | solution.py:39
  75.2 0.0 collective-permute-done
  75.2 3.5 %collective-permute-start.14 = (f16[448,576]{1,0:T(8,128)(2,1)S(1)}, f16[448,576]{1,0:T(8,128)(2,1)}, u32[]{:S(2)}, u32[]{:S(2)}) collective-permute-start(f16[448,576]{1,0:T(8,128)(2,1)S(1)} %get-tuple-element.19), channel_id=1, source_target_pairs={{0,384},{2,386},{4,388},{6,390},{8,392},{10,394},{12,396},{14,398}... | collective-permute-start | bytes 1548296 | tf_op jit(solution)/shard_map/ppermute | solution.py:39
  78.6 0.0 collective-permute-done.2
  78.6 3.3 %collective-permute-start.13 = (f16[448,576]{1,0:T(8,128)(2,1)S(1)}, f16[448,576]{1,0:T(8,128)(2,1)}, u32[]{:S(2)}, u32[]{:S(2)}) collective-permute-start(f16[448,576]{1,0:T(8,128)(2,1)S(1)} %get-tuple-element.20), channel_id=1, source_target_pairs={{0,256},{2,258},{4,260},{6,262},{8,264},{10,266},{12,268},{14,270}... | collective-permute-start | bytes 1548296 | tf_op jit(solution)/shard_map/ppermute | solution.py:39
  82.0 0.0 collective-permute-done.1
  82.0 0.0 collective-permute-done.6
  82.0 2.2 %multiply_add_fusion.1 = f32[448,576]{1,0:T(8,128)S(1)} fusion(f16[448,576]{1,0:T(8,128)(2,1)} %collective-permute-done.6, f16[448,576]{1,0:T(8,128)(2,1)} %collective-permute-done.2, f16[448,576]{1,0:T(8,128)(2,1)} %collective-permute-done.1, f16[448,576]{1,0:T(8,128)(2,1)S(1)} %collective-permute-done, f32[1792,576]{1,0:T(8,128)} %copy-done, s32[]{:T(128)S(6)} %select_n.86), kind=kLoop, calls=%fused_computation.5 | loop fusion | flops 3096576 | bytes 4128772 | tf_op jit(solution)/shard_map/add | solution.py:156
  84.3 0.1 multiply_convert_fusion.15
  84.4 0.7 collective-permute-start.7
  85.0 1.3 %collective-permute-start.9 = (f16[112,576]{1,0:T(8,128)(2,1)S(1)}, f16[112,576]{1,0:T(8,128)(2,1)}, u32[]{:S(2)}, u32[]{:S(2)}) collective-permute-start(f16[112,576]{1,0:T(8,128)(2,1)S(1)} %get-tuple-element.22), channel_id=1, source_target_pairs={{1,97},{3,99},{5,101},{7,103},{9,105},{11,107},{13,109},{15,111},{... | collective-permute-start | bytes 387080 | tf_op jit(solution)/shard_map/ppermute | solution.py:39
  86.4 0.0 collective-permute-done.12
  86.4 1.3 %collective-permute-start.8 = (f16[112,576]{1,0:T(8,128)(2,1)S(1)}, f16[112,576]{1,0:T(8,128)(2,1)}, u32[]{:S(2)}, u32[]{:S(2)}) collective-permute-start(f16[112,576]{1,0:T(8,128)(2,1)S(1)} %get-tuple-element.23), channel_id=1, source_target_pairs={{1,65},{3,67},{5,69},{7,71},{9,73},{11,75},{13,77},{15,79},{17,81}... | collective-permute-start | bytes 387080 | tf_op jit(solution)/shard_map/ppermute | solution.py:39
  87.7 7.9 %collective-permute-done.14 = f16[448,576]{1,0:T(8,128)(2,1)} collective-permute-done((f16[448,576]{1,0:T(8,128)(2,1)S(1)}, f16[448,576]{1,0:T(8,128)(2,1)}, u32[]{:S(2)}, u32[]{:S(2)}) %collective-permute-start.14) | collective-permute-done | bytes 516128 | tf_op jit(solution)/shard_map/ppermute | solution.py:39
  95.6 0.0 collective-permute-done.13
  95.6 2.1 %multiply_add_fusion = f32[448,576]{1,0:T(8,128)S(1)} fusion(f16[448,576]{1,0:T(8,128)(2,1)} %collective-permute-done.14, f16[448,576]{1,0:T(8,128)(2,1)} %collective-permute-done.13, f16[448,576]{1,0:T(8,128)(2,1)} %collective-permute-done.12, f32[1792,576]{1,0:T(8,128)} %copy-done.2, s32[]{:T(128)S(6)} %select_n.86), kind=kLoop, calls=%fused_computation.1 | loop fusion | flops 2322432 | bytes 3612676 | tf_op jit(solution)/shard_map/add | solution.py:140
  97.7 0.0 copy-start.6
  97.8 0.0 copy-start.7
  97.8 0.8 multiply_convert_fusion.12
  98.5 2.6 %collective-permute-start.15 = (f16[112,576]{1,0:T(8,128)(2,1)}, f16[112,576]{1,0:T(8,128)(2,1)}, u32[]{:S(2)}, u32[]{:S(2)}) collective-permute-start(f16[112,576]{1,0:T(8,128)(2,1)} %get-tuple-element.24), channel_id=1, source_target_pairs={{0,32},{2,34},{4,36},{6,38},{8,40},{10,42},{12,44},{14,46},{16,48}... | collective-permute-start | bytes 387080 | tf_op jit(solution)/shard_map/ppermute | solution.py:39
  101.1 2.3 %collective-permute-start.17 = (f16[112,576]{1,0:T(8,128)(2,1)S(1)}, f16[112,576]{1,0:T(8,128)(2,1)}, u32[]{:S(2)}, u32[]{:S(2)}) collective-permute-start(f16[112,576]{1,0:T(8,128)(2,1)S(1)} %get-tuple-element.25), channel_id=1, source_target_pairs={{0,96},{2,98},{4,100},{6,102},{8,104},{10,106},{12,108},{14,110},{... | collective-permute-start | bytes 387080 | tf_op jit(solution)/shard_map/ppermute | solution.py:39
  103.4 0.0 collective-permute-done.7
  103.4 0.6 copy-done.9
  104.1 4.3 %collective-permute-start.16 = (f16[112,576]{1,0:T(8,128)(2,1)S(1)}, f16[112,576]{1,0:T(8,128)(2,1)}, u32[]{:S(2)}, u32[]{:S(2)}) collective-permute-start(f16[112,576]{1,0:T(8,128)(2,1)S(1)} %get-tuple-element.26), channel_id=1, source_target_pairs={{0,64},{2,66},{4,68},{6,70},{8,72},{10,74},{12,76},{14,78},{16,80}... | collective-permute-start | bytes 387080 | tf_op jit(solution)/shard_map/ppermute | solution.py:39
  108.4 0.0 collective-permute-done.9
  108.4 0.0 collective-permute-done.8
  108.4 0.0 collective-permute-done.15
  108.5 1.6 %collective-permute-done.17 = f16[112,576]{1,0:T(8,128)(2,1)} collective-permute-done((f16[112,576]{1,0:T(8,128)(2,1)S(1)}, f16[112,576]{1,0:T(8,128)(2,1)}, u32[]{:S(2)}, u32[]{:S(2)}) %collective-permute-start.17) | collective-permute-done | bytes 129056 | tf_op jit(solution)/shard_map/ppermute | solution.py:39
  110.1 3.5 %collective-permute-done.16 = f16[112,576]{1,0:T(8,128)(2,1)} collective-permute-done((f16[112,576]{1,0:T(8,128)(2,1)S(1)}, f16[112,576]{1,0:T(8,128)(2,1)}, u32[]{:S(2)}, u32[]{:S(2)}) %collective-permute-start.16) | collective-permute-done | bytes 129056 | tf_op jit(solution)/shard_map/ppermute | solution.py:39
  113.6 2.4 %add_divide_fusion = (f32[1,1,112,576]{3,2,1,0:T(8,128)}, f32[1,1,112,576]{3,2,1,0:T(8,128)}, f32[1,1,112,576]{3,2,1,0:T(8,128)}) fusion(f32[1,1,112,576]{3,2,1,0:T(8,128)S(1)} %copy-done.6, f32[1,1,112,576]{3,2,1,0:T(8,128)S(1)} %copy-done.7, f16[112,576]{1,0:T(8,128)(2,1)} %collective-permute-done.17, f16[112,576]{1,0:T(8,128)(2,1)} %collective-permute-done.16, ...), kind=kLoop, calls=%fused_computation.17 | loop fusion | flops 1806336 | bytes 2580485 | tf_op jit(solution)/shard_map/div | solution.py:168
  (5 shorter events, 0.0 us)
Async XLA Ops:
  0.6 13.7 %copy-start.8 = (bf16[1,1,2,96,576]{4,3,2,1,0:T(8,128)(2,1)S(1)}, bf16[1,1,2,96,576]{4,3,2,1,0:T(8,128)(2,1)}, u32[]{:S(2)}) copy-start(bf16[1,1,2,96,576]{4,3,2,1,0:T(8,128)(2,1)} %param.6) | copy-start | bytes 663556
  3.2 30.4 %copy-start.5 = (s32[1,1,2]{2,1,0:T(1,128)S(1)}, s32[1,1,2]{2,1,0:T(1,128)}, u32[]{:S(2)}) copy-start(s32[1,1,2]{2,1,0:T(1,128)} %param.7) | copy-start | bytes 28
  3.2 64.4 %collective-permute-start.10 = (bf16[384,1792]{1,0:T(8,128)(2,1)}, bf16[384,1792]{1,0:T(8,128)(2,1)S(1)}, u32[]{:S(2)}, u32[]{:S(2)}) collective-permute-start(bf16[384,1792]{1,0:T(8,128)(2,1)} %slice_bitcast_fusion), channel_id=1, source_target_pairs={{0,28},{2,30},{4,24},{6,26},{8,20},{10,22},{12,16},{14,18},{16,12}... | collective-permute-start | bytes 4128776 | tf_op jit(solution)/shard_map/ppermute | solution.py:39
  33.6 1.8 %copy-start.4 = (bf16[1,1,2,384,1792]{4,3,2,1,0:T(8,128)(2,1)S(1)}, bf16[1,1,2,384,1792]{4,3,2,1,0:T(8,128)(2,1)}, u32[]{:S(2)}) copy-start(bf16[1,1,2,384,1792]{4,3,2,1,0:T(8,128)(2,1)} %acts.1) | copy-start | bytes 8257540
  40.6 2.4 %copy-start = (f32[1792,576]{1,0:T(8,128)}, f32[1792,576]{1,0:T(8,128)S(1)}, u32[]{:S(2)}) copy-start(f32[1792,576]{1,0:T(8,128)S(1)} %get-tuple-element.6.base) | copy-start | bytes 12386308
  40.6 3.9 %copy-start.3 = (f32[1792,576]{1,0:T(8,128)}, f32[1792,576]{1,0:T(8,128)S(1)}, u32[]{:S(2)}) copy-start(f32[1792,576]{1,0:T(8,128)S(1)} %get-tuple-element.7) | copy-start | bytes 12386308
  44.5 9.7 %collective-permute-start.3 = (f16[448,576]{1,0:T(8,128)(2,1)S(1)}, f16[448,576]{1,0:T(8,128)(2,1)}, u32[]{:S(2)}, u32[]{:S(2)}) collective-permute-start(f16[448,576]{1,0:T(8,128)(2,1)S(1)} %get-tuple-element.15), channel_id=1, source_target_pairs={{1,129},{3,131},{5,133},{7,135},{9,137},{11,139},{13,141},{15,143}... | collective-permute-start | bytes 1548296 | tf_op jit(solution)/shard_map/ppermute | solution.py:39
  46.0 8.9 %collective-permute-start.5 = (f16[448,576]{1,0:T(8,128)(2,1)}, f16[448,576]{1,0:T(8,128)(2,1)}, u32[]{:S(2)}, u32[]{:S(2)}) collective-permute-start(f16[448,576]{1,0:T(8,128)(2,1)} %get-tuple-element.16), channel_id=1, source_target_pairs={{1,385},{3,387},{5,389},{7,391},{9,393},{11,395},{13,397},{15,399}... | collective-permute-start | bytes 1548296 | tf_op jit(solution)/shard_map/ppermute | solution.py:39
  47.5 8.9 %collective-permute-start.4 = (f16[448,576]{1,0:T(8,128)(2,1)}, f16[448,576]{1,0:T(8,128)(2,1)}, u32[]{:S(2)}, u32[]{:S(2)}) collective-permute-start(f16[448,576]{1,0:T(8,128)(2,1)} %get-tuple-element.17), channel_id=1, source_target_pairs={{1,257},{3,259},{5,261},{7,263},{9,265},{11,267},{13,269},{15,271}... | collective-permute-start | bytes 1548296 | tf_op jit(solution)/shard_map/ppermute | solution.py:39
  48.9 17.2 %collective-permute-start.11 = (bf16[384,576]{1,0:T(8,128)(2,1)S(1)}, bf16[384,576]{1,0:T(8,128)(2,1)S(1)}, u32[]{:S(2)}, u32[]{:S(2)}) collective-permute-start(bf16[384,576]{1,0:T(8,128)(2,1)S(1)} %get-tuple-element.8), channel_id=1, source_target_pairs={{0,28},{2,30},{4,24},{6,26},{8,20},{10,22},{12,16},{14,18},{16,12}... | collective-permute-start | bytes 1327112 | tf_op jit(solution)/shard_map/ppermute | solution.py:39
  50.9 16.7 %copy-start.1 = (f32[1792,576]{1,0:T(8,128)S(1)}, f32[1792,576]{1,0:T(8,128)}, u32[]{:S(2)}) copy-start(f32[1792,576]{1,0:T(8,128)} %copy-done) | copy-start | bytes 12386308
  54.2 21.0 %collective-permute-start = (f16[448,576]{1,0:T(8,128)(2,1)S(1)}, f16[448,576]{1,0:T(8,128)(2,1)S(1)}, u32[]{:S(2)}, u32[]{:S(2)}) collective-permute-start(f16[448,576]{1,0:T(8,128)(2,1)S(1)} %get-tuple-element.12), channel_id=1, source_target_pairs={{1,129},{3,131},{5,133},{7,135},{9,137},{11,139},{13,141},{15,143}... | collective-permute-start | bytes 1548296 | tf_op jit(solution)/shard_map/ppermute | solution.py:39
  54.9 23.8 %collective-permute-start.2 = (f16[448,576]{1,0:T(8,128)(2,1)S(1)}, f16[448,576]{1,0:T(8,128)(2,1)}, u32[]{:S(2)}, u32[]{:S(2)}) collective-permute-start(f16[448,576]{1,0:T(8,128)(2,1)S(1)} %get-tuple-element.13), channel_id=1, source_target_pairs={{1,385},{3,387},{5,389},{7,391},{9,393},{11,395},{13,397},{15,399}... | collective-permute-start | bytes 1548296 | tf_op jit(solution)/shard_map/ppermute | solution.py:39
  56.3 25.7 %collective-permute-start.1 = (f16[448,576]{1,0:T(8,128)(2,1)}, f16[448,576]{1,0:T(8,128)(2,1)}, u32[]{:S(2)}, u32[]{:S(2)}) collective-permute-start(f16[448,576]{1,0:T(8,128)(2,1)} %get-tuple-element.14), channel_id=1, source_target_pairs={{1,257},{3,259},{5,261},{7,263},{9,265},{11,267},{13,269},{15,271}... | collective-permute-start | bytes 1548296 | tf_op jit(solution)/shard_map/ppermute | solution.py:39
  66.1 15.9 %collective-permute-start.6 = (f16[448,576]{1,0:T(8,128)(2,1)}, f16[448,576]{1,0:T(8,128)(2,1)}, u32[]{:S(2)}, u32[]{:S(2)}) collective-permute-start(f16[448,576]{1,0:T(8,128)(2,1)} %multiply_convert_fusion.3), channel_id=1, source_target_pairs={{1,29},{3,31},{5,25},{7,27},{9,21},{11,23},{13,17},{15,19},{17,13}... | collective-permute-start | bytes 1548296 | tf_op jit(solution)/shard_map/ppermute | solution.py:39
  70.5 2.3 %copy-start.2 = (f32[1792,576]{1,0:T(8,128)}, f32[1792,576]{1,0:T(8,128)S(1)}, u32[]{:S(2)}) copy-start(f32[1792,576]{1,0:T(8,128)S(1)} %shard_map.77) | copy-start | bytes 12386308
  72.8 13.6 %collective-permute-start.12 = (f16[448,576]{1,0:T(8,128)(2,1)}, f16[448,576]{1,0:T(8,128)(2,1)}, u32[]{:S(2)}, u32[]{:S(2)}) collective-permute-start(f16[448,576]{1,0:T(8,128)(2,1)} %get-tuple-element.18), channel_id=1, source_target_pairs={{0,128},{2,130},{4,132},{6,134},{8,136},{10,138},{12,140},{14,142}... | collective-permute-start | bytes 1548296 | tf_op jit(solution)/shard_map/ppermute | solution.py:39
  75.2 20.4 %collective-permute-start.14 = (f16[448,576]{1,0:T(8,128)(2,1)S(1)}, f16[448,576]{1,0:T(8,128)(2,1)}, u32[]{:S(2)}, u32[]{:S(2)}) collective-permute-start(f16[448,576]{1,0:T(8,128)(2,1)S(1)} %get-tuple-element.19), channel_id=1, source_target_pairs={{0,384},{2,386},{4,388},{6,390},{8,392},{10,394},{12,396},{14,398}... | collective-permute-start | bytes 1548296 | tf_op jit(solution)/shard_map/ppermute | solution.py:39
  78.6 17.0 %collective-permute-start.13 = (f16[448,576]{1,0:T(8,128)(2,1)S(1)}, f16[448,576]{1,0:T(8,128)(2,1)}, u32[]{:S(2)}, u32[]{:S(2)}) collective-permute-start(f16[448,576]{1,0:T(8,128)(2,1)S(1)} %get-tuple-element.20), channel_id=1, source_target_pairs={{0,256},{2,258},{4,260},{6,262},{8,264},{10,266},{12,268},{14,270}... | collective-permute-start | bytes 1548296 | tf_op jit(solution)/shard_map/ppermute | solution.py:39
  84.4 19.1 %collective-permute-start.7 = (f16[112,576]{1,0:T(8,128)(2,1)S(1)}, f16[112,576]{1,0:T(8,128)(2,1)S(1)}, u32[]{:S(2)}, u32[]{:S(2)}) collective-permute-start(f16[112,576]{1,0:T(8,128)(2,1)S(1)} %get-tuple-element.21), channel_id=1, source_target_pairs={{1,33},{3,35},{5,37},{7,39},{9,41},{11,43},{13,45},{15,47},{17,49}... | collective-permute-start | bytes 387080 | tf_op jit(solution)/shard_map/ppermute | solution.py:39
  85.0 23.4 %collective-permute-start.9 = (f16[112,576]{1,0:T(8,128)(2,1)S(1)}, f16[112,576]{1,0:T(8,128)(2,1)}, u32[]{:S(2)}, u32[]{:S(2)}) collective-permute-start(f16[112,576]{1,0:T(8,128)(2,1)S(1)} %get-tuple-element.22), channel_id=1, source_target_pairs={{1,97},{3,99},{5,101},{7,103},{9,105},{11,107},{13,109},{15,111},{... | collective-permute-start | bytes 387080 | tf_op jit(solution)/shard_map/ppermute | solution.py:39
  86.4 22.0 %collective-permute-start.8 = (f16[112,576]{1,0:T(8,128)(2,1)S(1)}, f16[112,576]{1,0:T(8,128)(2,1)}, u32[]{:S(2)}, u32[]{:S(2)}) collective-permute-start(f16[112,576]{1,0:T(8,128)(2,1)S(1)} %get-tuple-element.23), channel_id=1, source_target_pairs={{1,65},{3,67},{5,69},{7,71},{9,73},{11,75},{13,77},{15,79},{17,81}... | collective-permute-start | bytes 387080 | tf_op jit(solution)/shard_map/ppermute | solution.py:39
  97.7 15.9 %copy-start.6 = (f32[1,1,112,576]{3,2,1,0:T(8,128)S(1)}, f32[1,1,112,576]{3,2,1,0:T(8,128)}, u32[]{:S(2)}) copy-start(f32[1,1,112,576]{3,2,1,0:T(8,128)} %param.9) | copy-start | bytes 774148
  97.8 15.9 %copy-start.7 = (f32[1,1,112,576]{3,2,1,0:T(8,128)S(1)}, f32[1,1,112,576]{3,2,1,0:T(8,128)}, u32[]{:S(2)}) copy-start(f32[1,1,112,576]{3,2,1,0:T(8,128)} %param.8) | copy-start | bytes 774148
  98.5 9.9 %collective-permute-start.15 = (f16[112,576]{1,0:T(8,128)(2,1)}, f16[112,576]{1,0:T(8,128)(2,1)}, u32[]{:S(2)}, u32[]{:S(2)}) collective-permute-start(f16[112,576]{1,0:T(8,128)(2,1)} %get-tuple-element.24), channel_id=1, source_target_pairs={{0,32},{2,34},{4,36},{6,38},{8,40},{10,42},{12,44},{14,46},{16,48}... | collective-permute-start | bytes 387080 | tf_op jit(solution)/shard_map/ppermute | solution.py:39
  101.1 9.0 %collective-permute-start.17 = (f16[112,576]{1,0:T(8,128)(2,1)S(1)}, f16[112,576]{1,0:T(8,128)(2,1)}, u32[]{:S(2)}, u32[]{:S(2)}) collective-permute-start(f16[112,576]{1,0:T(8,128)(2,1)S(1)} %get-tuple-element.25), channel_id=1, source_target_pairs={{0,96},{2,98},{4,100},{6,102},{8,104},{10,106},{12,108},{14,110},{... | collective-permute-start | bytes 387080 | tf_op jit(solution)/shard_map/ppermute | solution.py:39
  103.4 0.7 copy-start.9
  104.1 9.5 %collective-permute-start.16 = (f16[112,576]{1,0:T(8,128)(2,1)S(1)}, f16[112,576]{1,0:T(8,128)(2,1)}, u32[]{:S(2)}, u32[]{:S(2)}) collective-permute-start(f16[112,576]{1,0:T(8,128)(2,1)S(1)} %get-tuple-element.26), channel_id=1, source_target_pairs={{0,64},{2,66},{4,68},{6,70},{8,72},{10,74},{12,76},{14,78},{16,80}... | collective-permute-start | bytes 387080 | tf_op jit(solution)/shard_map/ppermute | solution.py:39

commit v2 on v0

v2 whole, which is shorter than its diff:
```python
import functools

import jax
import jax.numpy as jnp
from jax import lax
from jax.experimental import pallas as pl
from jax.experimental.pallas import tpu as pltpu
from jax.sharding import PartitionSpec as P

AXES = ("dp", "pipe", "expert")
NX, NY = 4, 4
X_SCALE, Y_SCALE, Z_SCALE = 64.0, 32.0, 8.0
VMEM_BYTES = 32 << 20


def first_step(expert):
    return 1 + 2 * (expert % 2)


def over_x_first(dp, pipe, expert):
    return dp ^ first_step(expert) * NY, pipe, expert


def over_x_second(dp, pipe, expert):
    return dp ^ (4 - first_step(expert)) * NY, pipe, expert


def over_y(bits):
    return lambda dp, pipe, expert: (dp ^ bits, pipe, expert)


def mirrored(dp, pipe, expert):
    return dp, lax.axis_size("pipe") - 1 - pipe, expert


def send(block, to):
    sizes = [lax.axis_size(name) for name in AXES]

    def flat(dp, pipe, expert):
        return (dp * sizes[1] + pipe) * sizes[2] + expert

    pairs = [
        (flat(d, p, e), flat(*to(d, p, e)))
        for d in range(sizes[0])
        for p in range(sizes[1])
        for e in range(sizes[2])
    ]
    return lax.ppermute(block, AXES, pairs)


def transposed_dot(a, b):
    return lax.dot_general(a, b, (((0,), (0,)), ((), ())), preferred_element_type=jnp.float32)


def cost(flops, read_and_written):
    return pl.CostEstimate(flops=flops, bytes_accessed=read_and_written, transcendentals=0)


def span_kernel(span, counts, acts, grads, part, masked):
    @pl.when(pl.program_id(0) == 0)
    def _():
        live = lax.broadcasted_iota(jnp.int32, masked.shape, 0) < counts[span]
        masked[...] = jnp.where(live, grads[0].astype(jnp.float32), 0.0).astype(masked.dtype)

    product = transposed_dot(acts[0, 0, 0], masked[...])
    x = lax.axis_index("dp") // NY
    first = first_step(lax.axis_index("expert"))
    rows = part.shape[1]
    for i in range(2):
        apart = jnp.bitwise_xor(2 * pl.program_id(0) + i, x)
        slot = jnp.where(apart == 0, 0, jnp.where(apart == 2, 3, jnp.where(apart == first, 2, 1)))
        part[slot] = product[i * rows : (i + 1) * rows]


def multiply_span(span, counts, activations, grads):
    _, _, _, slots, rows = activations.shape
    width = grads.shape[-1]
    part = (NX, rows // NX, width)
    return pl.pallas_call(
        functools.partial(span_kernel, span),
        grid_spec=pltpu.PrefetchScalarGridSpec(
            num_scalar_prefetch=1,
            grid=(2,),
            in_specs=[
                pl.BlockSpec((1, 1, 1, slots, rows // 2), lambda i, c: (0, 0, span, 0, i)),
                pl.BlockSpec((1, slots, width), lambda i, c: (span, 0, 0)),
            ],
            out_specs=pl.BlockSpec(part, lambda i, c: (0, 0, 0)),
            scratch_shapes=[pltpu.VMEM((slots, width), grads.dtype)],
        ),
        out_shape=jax.ShapeDtypeStruct(part, jnp.float32),
        compiler_params=pltpu.CompilerParams(vmem_limit_bytes=VMEM_BYTES),
        cost_estimate=cost(2 * slots * rows * width, 6 << 20),
    )(counts, activations, grads)


def narrow(values, scale):
    return (values * scale).astype(jnp.float16)


def widen(values, scale):
    return values.astype(jnp.float32) * (1.0 / scale)


def after(value, *earlier):
    return lax.optimization_barrier((value, *earlier))[0]


def piece(array, index):
    rows = array.shape[0] // NY
    return lax.dynamic_slice_in_dim(array, index * rows, rows, 0)


def exchange_y(quarter, y):
    out = [narrow(piece(quarter, y ^ k), Y_SCALE) for k in range(1, NY)]
    return out, [send(block, over_y(k)) for k, block in enumerate(out, 1)]


def local(activations, out_grads, counts, first_moment, second_moment):
    y = lax.axis_index("dp") % NY
    live = counts[0, 0]
    grads = lax.all_gather(out_grads[0, 0], "expert", axis=1, tiled=True)

    other = multiply_span(1, live, activations, grads)
    other_half = narrow(other[2:], X_SCALE)
    other_got = send(other_half, over_x_first)
    own = multiply_span(0, live, activations, after(grads, other_half))
    own_half = narrow(own[2:], X_SCALE)
    own_got = send(own_half, over_x_first)
    other_pass = narrow(after(other[1], own_half) + widen(other_got[1], X_SCALE), X_SCALE)
    other_last = send(other_pass, over_x_second)
    own_pass = narrow(after(own[1], other_pass) + widen(own_got[1], X_SCALE), X_SCALE)
    own_last = send(own_pass, over_x_second)

    other_x = after(other[0], own_pass) + widen(other_got[0], X_SCALE) + widen(other_last, X_SCALE)
    other_out, other_in = exchange_y(other_x, y)
    own_x = after(own[0], *other_out) + widen(own_got[0], X_SCALE) + widen(own_last, X_SCALE)
    own_out, own_in = exchange_y(own_x, y)
    other_rows = piece(after(other_x, *own_out), y) + sum(widen(block, Y_SCALE) for block in other_in)
    mirror_rows = send(narrow(other_rows, Z_SCALE), mirrored)
    grad = piece(own_x, y) + sum(widen(block, Y_SCALE) for block in own_in)
    grad = (grad + widen(mirror_rows, Z_SCALE))[None, None]
    new_first = 0.9 * first_moment + 0.1 * grad
    new_second = 0.95 * second_moment + 0.05 * grad * grad
    direction = new_first / (jnp.sqrt(new_second) + 1e-08)
    return (new_first, new_second, direction)


def solution(mesh):
    state = P("pipe", "expert", "dp", None)
    return jax.shard_map(
        local,
        mesh=mesh,
        in_specs=(
            P("dp", "pipe", None, None, "expert"),
            P("dp", "pipe", None, "expert", None),
            P("dp", "pipe", None),
            state,
            state,
        ),
        out_specs=(state, state, state),
        check_vma=False,
    )
```

time: 631 us -> 107 us (0.17)
  waiting for transfers between devices: 554 us -> 22.6 us
  starting transfers between devices: 18.9 us -> 51.4 us
  local copies, waits for them, and re-layouts: 15.4 us -> 2.1 us
  between operations: 14.1 us -> 0.91 us
    ppermute x3 -> x11, waiting for transfers between devices: 445 us -> 22.6 us  [send(): return lax.ppermute(block, AXES, pairs)]
    unnamed x2 -> x0, waiting for transfers between devices: 109 us -> none
    ppermute x3 -> x11, starting transfers between devices: 18.9 us -> 51.4 us  [send(): return lax.ppermute(block, AXES, pairs)]
    unnamed x11 -> x10, local copies, waits for them, and re-layouts: 15.1 us -> 1.8 us
  transfers between devices with their start and end apart: 4 -> 11, of which waited for: 4 -> 3; matrix products, arithmetic and copies ran while one was open for 0% -> 6% of each run, Pallas kernels for 0% -> 2%
where the time goes in v2:
time: 107 us; the launch traced here: 105 us
  starting transfers between devices  51.4 us (48%)
  waiting for transfers between devices  22.6 us (21%)
  blocking collectives  16.5 us (15%)
  other arithmetic  6.79 us (6%)
  Pallas kernels  5.02 us (5%)
  local copies, waits for them, and re-layouts  2.1 us (2%)
    ppermute x11, starting transfers between devices, send(): return lax.ppermute(block, AXES, pairs)  51.4 us
    ppermute x11, waiting for transfers between devices, send(): return lax.ppermute(block, AXES, pairs)  22.6 us
    all_gather x1, blocking collectives, local(): grads = lax.all_gather(out_grads[0, 0], 'expert', axis=1, tiled=True)  16.5 us
    pallas_call x2, Pallas kernels, multiply_span(): pl.pallas_call(functools.partial(span_kernel, span), grid_spec=pltpu.Pref...  5.02 us
    convert_element_type x7, other arithmetic, narrow(): return (values * scale).astype(jnp.float16)  2.97 us
  transfers between devices with their start and end apart: 11, of which 3 were waited for; matrix products, arithmetic and copies ran while one was open for 6% of the time, Pallas kernels for 2%

profile of v2, /device:TPU:6, one launch (start us, length us, event | category | flops | bytes accessed | tf_op | source)
XLA Modules:
  0.0 105.3 jit_solution(11803748435355587501)
XLA Ops:
  0.6 0.0 copy-start.1
  0.6 16.5 %all-gather = bf16[1,1,2,384,576]{4,3,2,1,0:T(8,128)(2,1)S(1)} all-gather(bf16[1,1,2,96,576]{4,3,2,1,0:T(8,128)(2,1)} %param.6), channel_id=2, replica_groups=mesh['dp'=16,'pipe'=8,'expert'=4] {'expert'}, dimensions={3}, use_global_device_ids=true | all-gather | bytes 1105920 | tf_op jit(solution)/shard_map/all_gather | solution.py:122
  17.1 0.0 copy-done.1
  17.1 0.0 copy-start
  17.1 1.8 %copy-done = bf16[1,1,2,384,1792]{4,3,2,1,0:T(8,128)(2,1)S(1)} copy-done((bf16[1,1,2,384,1792]{4,3,2,1,0:T(8,128)(2,1)S(1)}, bf16[1,1,2,384,1792]{4,3,2,1,0:T(8,128)(2,1)}, u32[]{:S(2)}) %copy-start) | copy-done | bytes 2752536
  18.9 2.5 %shard_map.76 = f32[4,448,576]{2,1,0:T(8,128)S(1)} custom-call(s32[2]{0:T(128)S(1)} %bitcast.40, bf16[1,1,2,384,1792]{4,3,2,1,0:T(8,128)(2,1)S(1)} %copy-done, bf16[2,384,576]{2,1,0:T(8,128)(2,1)S(1)} %bitcast.38), custom_call_target="tpu_custom_call" | custom-call | flops 792723456 | bytes 6291456 | tf_op jit(solution)/shard_map/pallas_call | solution.py:79
  21.4 0.2 fusion.1
  21.7 2.7 %collective-permute-start = (f16[2,448,576]{2,1,0:T(8,128)(2,1)S(1)}, f16[2,448,576]{2,1,0:T(8,128)(2,1)S(1)}, u32[]{:S(2)}, u32[]{:S(2)}) collective-permute-start(f16[2,448,576]{2,1,0:T(8,128)(2,1)S(1)} %fusion.1), channel_id=1, source_target_pairs={{0,128},{1,385},{2,130},{3,387},{4,132},{5,389},{6,134},{7,391},{8... | collective-permute-start | bytes 3096584 | tf_op jit(solution)/shard_map/ppermute | solution.py:48
  24.4 2.5 %shard_map.77 = f32[4,448,576]{2,1,0:T(8,128)S(1)} custom-call(s32[2]{0:T(128)S(1)} %bitcast.41, bf16[1,1,2,384,1792]{4,3,2,1,0:T(8,128)(2,1)S(1)} %copy-done, bf16[2,384,576]{2,1,0:T(8,128)(2,1)S(1)} %bitcast.39), custom_call_target="tpu_custom_call" | custom-call | flops 792723456 | bytes 6291456 | tf_op jit(solution)/shard_map/pallas_call | solution.py:79
  26.9 0.2 fusion
  27.1 3.1 %collective-permute-start.1 = (f16[2,448,576]{2,1,0:T(8,128)(2,1)S(1)}, f16[2,448,576]{2,1,0:T(8,128)(2,1)S(1)}, u32[]{:S(2)}, u32[]{:S(2)}) collective-permute-start(f16[2,448,576]{2,1,0:T(8,128)(2,1)S(1)} %fusion), channel_id=1, source_target_pairs={{0,128},{1,385},{2,130},{3,387},{4,132},{5,389},{6,134},{7,391},{8... | collective-permute-start | bytes 3096584 | tf_op jit(solution)/shard_map/ppermute | solution.py:48
  30.3 0.1 slice_bitcast_fusion
  30.4 9.0 %collective-permute-done = f16[2,448,576]{2,1,0:T(8,128)(2,1)S(1)} collective-permute-done((f16[2,448,576]{2,1,0:T(8,128)(2,1)S(1)}, f16[2,448,576]{2,1,0:T(8,128)(2,1)S(1)}, u32[]{:S(2)}, u32[]{:S(2)}) %collective-permute-start) | collective-permute-done | bytes 1032224 | tf_op jit(solution)/shard_map/ppermute | solution.py:48
  39.4 0.0 copy-start.2
  39.4 1.2 %fusion.7 = f16[448,576]{1,0:T(8,128)(2,1)} fusion(f32[448,576]{1,0:T(8,128)S(1)} %get-tuple-element.10, f16[2,448,576]{2,1,0:T(8,128)(2,1)S(1)} %collective-permute-done), kind=kLoop, calls=%fused_computation.17 | loop fusion | flops 1290240 | bytes 2064384 | tf_op jit(solution)/shard_map/convert_element_type | solution.py:98
  40.6 0.0 copy-done.2
  40.6 6.3 %collective-permute-start.2 = (f16[448,576]{1,0:T(8,128)(2,1)}, f16[448,576]{1,0:T(8,128)(2,1)}, u32[]{:S(2)}, u32[]{:S(2)}) collective-permute-start(f16[448,576]{1,0:T(8,128)(2,1)} %fusion.7), channel_id=1, source_target_pairs={{0,384},{1,129},{2,386},{3,131},{4,388},{5,133},{6,390},{7,135},{8... | collective-permute-start | bytes 1548296 | tf_op jit(solution)/shard_map/ppermute | solution.py:48
  46.9 0.1 slice_bitcast_fusion.3
  47.1 9.1 %collective-permute-done.1 = f16[2,448,576]{2,1,0:T(8,128)(2,1)S(1)} collective-permute-done((f16[2,448,576]{2,1,0:T(8,128)(2,1)S(1)}, f16[2,448,576]{2,1,0:T(8,128)(2,1)S(1)}, u32[]{:S(2)}, u32[]{:S(2)}) %collective-permute-start.1) | collective-permute-done | bytes 1032224 | tf_op jit(solution)/shard_map/ppermute | solution.py:48
  56.1 1.1 %fusion.5 = f16[448,576]{1,0:T(8,128)(2,1)} fusion(f32[448,576]{1,0:T(8,128)S(1)} %get-tuple-element.11, f16[2,448,576]{2,1,0:T(8,128)(2,1)S(1)} %collective-permute-done.1), kind=kLoop, calls=%fused_computation.14 | loop fusion | flops 1290240 | bytes 2064384 | tf_op jit(solution)/shard_map/convert_element_type | solution.py:98
  57.2 7.8 %collective-permute-start.3 = (f16[448,576]{1,0:T(8,128)(2,1)}, f16[448,576]{1,0:T(8,128)(2,1)}, u32[]{:S(2)}, u32[]{:S(2)}) collective-permute-start(f16[448,576]{1,0:T(8,128)(2,1)} %fusion.5), channel_id=1, source_target_pairs={{0,384},{1,129},{2,386},{3,131},{4,388},{5,133},{6,390},{7,135},{8... | collective-permute-start | bytes 1548296 | tf_op jit(solution)/shard_map/ppermute | solution.py:48
  65.0 0.0 collective-permute-done.2
  65.0 1.5 %fusion.3 = f32[448,576]{1,0:T(8,128)S(1)} fusion(f32[448,576]{1,0:T(8,128)S(1)} %get-tuple-element.12, f16[448,576]{1,0:T(8,128)(2,1)} %collective-permute-done.2, f16[2,448,576]{2,1,0:T(8,128)(2,1)} %copy-done.2), kind=kLoop, calls=%fused_computation.11 | loop fusion | flops 1548288 | bytes 3096576 | tf_op jit(solution)/shard_map/add | solution.py:135
  66.5 0.1 multiply_convert_fusion.6
  66.6 3.4 %collective-permute-start.9 = (f16[112,576]{1,0:T(8,128)(2,1)S(1)}, f16[112,576]{1,0:T(8,128)(2,1)S(1)}, u32[]{:S(2)}, u32[]{:S(2)}) collective-permute-start(f16[112,576]{1,0:T(8,128)(2,1)S(1)} %get-tuple-element.26), channel_id=1, source_target_pairs={{0,96},{1,97},{2,98},{3,99},{4,100},{5,101},{6,102},{7,103},{8,104... | collective-permute-start | bytes 387080 | tf_op jit(solution)/shard_map/ppermute | solution.py:48
  70.0 1.9 %collective-permute-start.8 = (f16[112,576]{1,0:T(8,128)(2,1)S(1)}, f16[112,576]{1,0:T(8,128)(2,1)S(1)}, u32[]{:S(2)}, u32[]{:S(2)}) collective-permute-start(f16[112,576]{1,0:T(8,128)(2,1)S(1)} %get-tuple-element.27), channel_id=1, source_target_pairs={{0,64},{1,65},{2,66},{3,67},{4,68},{5,69},{6,70},{7,71},{8,72},{9,... | collective-permute-start | bytes 387080 | tf_op jit(solution)/shard_map/ppermute | solution.py:48
  71.9 4.8 %collective-permute-start.7 = (f16[112,576]{1,0:T(8,128)(2,1)S(1)}, f16[112,576]{1,0:T(8,128)(2,1)S(1)}, u32[]{:S(2)}, u32[]{:S(2)}) collective-permute-start(f16[112,576]{1,0:T(8,128)(2,1)S(1)} %get-tuple-element.25), channel_id=1, source_target_pairs={{0,32},{1,33},{2,34},{3,35},{4,36},{5,37},{6,38},{7,39},{8,40},{9,... | collective-permute-start | bytes 387080 | tf_op jit(solution)/shard_map/ppermute | solution.py:48
  76.7 0.0 collective-permute-done.3
  76.7 1.3 %fusion.2 = f32[448,576]{1,0:T(8,128)S(1)} fusion(f32[448,576]{1,0:T(8,128)S(1)} %get-tuple-element.13, f16[448,576]{1,0:T(8,128)(2,1)} %collective-permute-done.3, f16[2,448,576]{2,1,0:T(8,128)(2,1)S(1)} %collective-permute-done.1), kind=kLoop, calls=%fused_computation.9 | loop fusion | flops 1548288 | bytes 3096576 | tf_op jit(solution)/shard_map/add | solution.py:137
  78.0 0.0 copy-start.3
  78.0 0.0 copy-start.4
  78.0 0.1 multiply_convert_fusion.1
  78.1 3.5 %collective-permute-start.6 = (f16[112,576]{1,0:T(8,128)(2,1)S(1)}, f16[112,576]{1,0:T(8,128)(2,1)S(1)}, u32[]{:S(2)}, u32[]{:S(2)}) collective-permute-start(f16[112,576]{1,0:T(8,128)(2,1)S(1)} %get-tuple-element.22), channel_id=1, source_target_pairs={{0,96},{1,97},{2,98},{3,99},{4,100},{5,101},{6,102},{7,103},{8,104... | collective-permute-start | bytes 387080 | tf_op jit(solution)/shard_map/ppermute | solution.py:48
  81.6 1.9 %collective-permute-start.5 = (f16[112,576]{1,0:T(8,128)(2,1)S(1)}, f16[112,576]{1,0:T(8,128)(2,1)S(1)}, u32[]{:S(2)}, u32[]{:S(2)}) collective-permute-start(f16[112,576]{1,0:T(8,128)(2,1)S(1)} %get-tuple-element.23), channel_id=1, source_target_pairs={{0,64},{1,65},{2,66},{3,67},{4,68},{5,69},{6,70},{7,71},{8,72},{9,... | collective-permute-start | bytes 387080 | tf_op jit(solution)/shard_map/ppermute | solution.py:48
  83.6 0.0 collective-permute-done.9
  83.6 4.8 %collective-permute-start.4 = (f16[112,576]{1,0:T(8,128)(2,1)S(1)}, f16[112,576]{1,0:T(8,128)(2,1)S(1)}, u32[]{:S(2)}, u32[]{:S(2)}) collective-permute-start(f16[112,576]{1,0:T(8,128)(2,1)S(1)} %get-tuple-element.24), channel_id=1, source_target_pairs={{0,32},{1,33},{2,34},{3,35},{4,36},{5,37},{6,38},{7,39},{8,40},{9,... | collective-permute-start | bytes 387080 | tf_op jit(solution)/shard_map/ppermute | solution.py:48
  88.4 0.0 collective-permute-done.8
  88.4 0.0 collective-permute-done.7
  88.4 0.1 multiply_convert_fusion
  88.5 11.1 %collective-permute-start.10 = (f16[112,576]{1,0:T(8,128)(2,1)S(1)}, f16[112,576]{1,0:T(8,128)(2,1)S(1)}, u32[]{:S(2)}, u32[]{:S(2)}) collective-permute-start(f16[112,576]{1,0:T(8,128)(2,1)S(1)} %multiply_convert_fusion), channel_id=1, source_target_pairs={{0,28},{1,29},{2,30},{3,31},{4,24},{5,25},{6,26},{7,27},{8,20},{9,... | collective-permute-start | bytes 387080 | tf_op jit(solution)/shard_map/ppermute | solution.py:48
  99.7 0.0 collective-permute-done.6
  99.7 0.0 collective-permute-done.5
  99.7 0.0 collective-permute-done.4
  99.7 4.5 %collective-permute-done.10 = f16[112,576]{1,0:T(8,128)(2,1)S(1)} collective-permute-done((f16[112,576]{1,0:T(8,128)(2,1)S(1)}, f16[112,576]{1,0:T(8,128)(2,1)S(1)}, u32[]{:S(2)}, u32[]{:S(2)}) %collective-permute-start.10) | collective-permute-done | bytes 129056 | tf_op jit(solution)/shard_map/ppermute | solution.py:48
  104.2 0.0 copy-done.3
  104.2 0.0 copy-done.4
  104.2 1.1 %add_divide_fusion = (f32[1,1,112,576]{3,2,1,0:T(8,128)}, f32[1,1,112,576]{3,2,1,0:T(8,128)}, f32[1,1,112,576]{3,2,1,0:T(8,128)}) fusion(f32[1,1,112,576]{3,2,1,0:T(8,128)S(1)} %copy-done.3, f32[1,1,112,576]{3,2,1,0:T(8,128)S(1)} %copy-done.4, f16[112,576]{1,0:T(8,128)(2,1)S(1)} %collective-permute-done.10, f16[112,576]{1,0:T(8,128)(2,1)S(1)} %collective-permute-done.6, ...), kind=kLoop, calls=%fused_computation.22 | loop fusion | flops 1225728 | bytes 2064388 | tf_op jit(solution)/shard_map/div | solution.py:145
Async XLA Ops:
  0.6 16.5 %copy-start.1 = (s32[1,1,2]{2,1,0:T(1,128)S(1)}, s32[1,1,2]{2,1,0:T(1,128)}, u32[]{:S(2)}) copy-start(s32[1,1,2]{2,1,0:T(1,128)} %param.7) | copy-start | bytes 28
  17.1 1.8 %copy-start = (bf16[1,1,2,384,1792]{4,3,2,1,0:T(8,128)(2,1)S(1)}, bf16[1,1,2,384,1792]{4,3,2,1,0:T(8,128)(2,1)}, u32[]{:S(2)}) copy-start(bf16[1,1,2,384,1792]{4,3,2,1,0:T(8,128)(2,1)} %acts.3) | copy-start | bytes 8257540
  21.7 17.7 %collective-permute-start = (f16[2,448,576]{2,1,0:T(8,128)(2,1)S(1)}, f16[2,448,576]{2,1,0:T(8,128)(2,1)S(1)}, u32[]{:S(2)}, u32[]{:S(2)}) collective-permute-start(f16[2,448,576]{2,1,0:T(8,128)(2,1)S(1)} %fusion.1), channel_id=1, source_target_pairs={{0,128},{1,385},{2,130},{3,387},{4,132},{5,389},{6,134},{7,391},{8... | collective-permute-start | bytes 3096584 | tf_op jit(solution)/shard_map/ppermute | solution.py:48
  27.1 29.0 %collective-permute-start.1 = (f16[2,448,576]{2,1,0:T(8,128)(2,1)S(1)}, f16[2,448,576]{2,1,0:T(8,128)(2,1)S(1)}, u32[]{:S(2)}, u32[]{:S(2)}) collective-permute-start(f16[2,448,576]{2,1,0:T(8,128)(2,1)S(1)} %fusion), channel_id=1, source_target_pairs={{0,128},{1,385},{2,130},{3,387},{4,132},{5,389},{6,134},{7,391},{8... | collective-permute-start | bytes 3096584 | tf_op jit(solution)/shard_map/ppermute | solution.py:48
  39.4 1.2 %copy-start.2 = (f16[2,448,576]{2,1,0:T(8,128)(2,1)}, f16[2,448,576]{2,1,0:T(8,128)(2,1)S(1)}, u32[]{:S(2)}) copy-start(f16[2,448,576]{2,1,0:T(8,128)(2,1)S(1)} %collective-permute-done) | copy-start | bytes 3096580
  40.6 24.4 %collective-permute-start.2 = (f16[448,576]{1,0:T(8,128)(2,1)}, f16[448,576]{1,0:T(8,128)(2,1)}, u32[]{:S(2)}, u32[]{:S(2)}) collective-permute-start(f16[448,576]{1,0:T(8,128)(2,1)} %fusion.7), channel_id=1, source_target_pairs={{0,384},{1,129},{2,386},{3,131},{4,388},{5,133},{6,390},{7,135},{8... | collective-permute-start | bytes 1548296 | tf_op jit(solution)/shard_map/ppermute | solution.py:48
  57.2 19.5 %collective-permute-start.3 = (f16[448,576]{1,0:T(8,128)(2,1)}, f16[448,576]{1,0:T(8,128)(2,1)}, u32[]{:S(2)}, u32[]{:S(2)}) collective-permute-start(f16[448,576]{1,0:T(8,128)(2,1)} %fusion.5), channel_id=1, source_target_pairs={{0,384},{1,129},{2,386},{3,131},{4,388},{5,133},{6,390},{7,135},{8... | collective-permute-start | bytes 1548296 | tf_op jit(solution)/shard_map/ppermute | solution.py:48
  66.6 17.0 %collective-permute-start.9 = (f16[112,576]{1,0:T(8,128)(2,1)S(1)}, f16[112,576]{1,0:T(8,128)(2,1)S(1)}, u32[]{:S(2)}, u32[]{:S(2)}) collective-permute-start(f16[112,576]{1,0:T(8,128)(2,1)S(1)} %get-tuple-element.26), channel_id=1, source_target_pairs={{0,96},{1,97},{2,98},{3,99},{4,100},{5,101},{6,102},{7,103},{8,104... | collective-permute-start | bytes 387080 | tf_op jit(solution)/shard_map/ppermute | solution.py:48
  70.0 18.5 %collective-permute-start.8 = (f16[112,576]{1,0:T(8,128)(2,1)S(1)}, f16[112,576]{1,0:T(8,128)(2,1)S(1)}, u32[]{:S(2)}, u32[]{:S(2)}) collective-permute-start(f16[112,576]{1,0:T(8,128)(2,1)S(1)} %get-tuple-element.27), channel_id=1, source_target_pairs={{0,64},{1,65},{2,66},{3,67},{4,68},{5,69},{6,70},{7,71},{8,72},{9,... | collective-permute-start | bytes 387080 | tf_op jit(solution)/shard_map/ppermute | solution.py:48
  71.9 16.6 %collective-permute-start.7 = (f16[112,576]{1,0:T(8,128)(2,1)S(1)}, f16[112,576]{1,0:T(8,128)(2,1)S(1)}, u32[]{:S(2)}, u32[]{:S(2)}) collective-permute-start(f16[112,576]{1,0:T(8,128)(2,1)S(1)} %get-tuple-element.25), channel_id=1, source_target_pairs={{0,32},{1,33},{2,34},{3,35},{4,36},{5,37},{6,38},{7,39},{8,40},{9,... | collective-permute-start | bytes 387080 | tf_op jit(solution)/shard_map/ppermute | solution.py:48
  78.0 26.2 %copy-start.3 = (f32[1,1,112,576]{3,2,1,0:T(8,128)S(1)}, f32[1,1,112,576]{3,2,1,0:T(8,128)}, u32[]{:S(2)}) copy-start(f32[1,1,112,576]{3,2,1,0:T(8,128)} %param.9) | copy-start | bytes 774148
  78.0 26.2 %copy-start.4 = (f32[1,1,112,576]{3,2,1,0:T(8,128)S(1)}, f32[1,1,112,576]{3,2,1,0:T(8,128)}, u32[]{:S(2)}) copy-start(f32[1,1,112,576]{3,2,1,0:T(8,128)} %param.8) | copy-start | bytes 774148
  78.1 21.5 %collective-permute-start.6 = (f16[112,576]{1,0:T(8,128)(2,1)S(1)}, f16[112,576]{1,0:T(8,128)(2,1)S(1)}, u32[]{:S(2)}, u32[]{:S(2)}) collective-permute-start(f16[112,576]{1,0:T(8,128)(2,1)S(1)} %get-tuple-element.22), channel_id=1, source_target_pairs={{0,96},{1,97},{2,98},{3,99},{4,100},{5,101},{6,102},{7,103},{8,104... | collective-permute-start | bytes 387080 | tf_op jit(solution)/shard_map/ppermute | solution.py:48
  81.6 18.0 %collective-permute-start.5 = (f16[112,576]{1,0:T(8,128)(2,1)S(1)}, f16[112,576]{1,0:T(8,128)(2,1)S(1)}, u32[]{:S(2)}, u32[]{:S(2)}) collective-permute-start(f16[112,576]{1,0:T(8,128)(2,1)S(1)} %get-tuple-element.23), channel_id=1, source_target_pairs={{0,64},{1,65},{2,66},{3,67},{4,68},{5,69},{6,70},{7,71},{8,72},{9,... | collective-permute-start | bytes 387080 | tf_op jit(solution)/shard_map/ppermute | solution.py:48
  83.6 16.1 %collective-permute-start.4 = (f16[112,576]{1,0:T(8,128)(2,1)S(1)}, f16[112,576]{1,0:T(8,128)(2,1)S(1)}, u32[]{:S(2)}, u32[]{:S(2)}) collective-permute-start(f16[112,576]{1,0:T(8,128)(2,1)S(1)} %get-tuple-element.24), channel_id=1, source_target_pairs={{0,32},{1,33},{2,34},{3,35},{4,36},{5,37},{6,38},{7,39},{8,40},{9,... | collective-permute-start | bytes 387080 | tf_op jit(solution)/shard_map/ppermute | solution.py:48
  88.5 15.7 %collective-permute-start.10 = (f16[112,576]{1,0:T(8,128)(2,1)S(1)}, f16[112,576]{1,0:T(8,128)(2,1)S(1)}, u32[]{:S(2)}, u32[]{:S(2)}) collective-permute-start(f16[112,576]{1,0:T(8,128)(2,1)S(1)} %multiply_convert_fusion), channel_id=1, source_target_pairs={{0,28},{1,29},{2,30},{3,31},{4,24},{5,25},{6,26},{7,27},{8,20},{9,... | collective-permute-start | bytes 387080 | tf_op jit(solution)/shard_map/ppermute | solution.py:48

commit v3 on v2

v3 whole, which is shorter than its diff:
```python
import functools

import jax
import jax.numpy as jnp
from jax import lax
from jax.experimental import pallas as pl
from jax.experimental.pallas import tpu as pltpu
from jax.sharding import PartitionSpec as P

AXES = ("dp", "pipe", "expert")
NX, NY = 4, 4
X_SCALE, Y_SCALE, Z_SCALE = 64.0, 32.0, 8.0
VMEM_BYTES = 32 << 20


def x_steps(expert):
    first = 1 + 2 * (expert % 2)
    return first, 4 - first


def over_x(step):
    return lambda dp, pipe, expert: (dp ^ x_steps(expert)[step] * NY, pipe, expert)


def over_y(bits):
    return lambda dp, pipe, expert: (dp ^ bits, pipe, expert)


def mirrored(dp, pipe, expert):
    return dp, lax.axis_size("pipe") - 1 - pipe, expert


def send(block, to):
    sizes = [lax.axis_size(name) for name in AXES]

    def flat(dp, pipe, expert):
        return (dp * sizes[1] + pipe) * sizes[2] + expert

    pairs = [
        (flat(d, p, e), flat(*to(d, p, e)))
        for d in range(sizes[0])
        for p in range(sizes[1])
        for e in range(sizes[2])
    ]
    return lax.ppermute(block, AXES, pairs)


def transposed_dot(a, b):
    return lax.dot_general(a, b, (((0,), (0,)), ((), ())), preferred_element_type=jnp.float32)


def cost(flops, read_and_written):
    return pl.CostEstimate(flops=flops, bytes_accessed=read_and_written, transcendentals=0)


def span_kernel(span, counts, acts, grads, part):
    live = lax.broadcasted_iota(jnp.int32, grads.shape[1:], 0) < counts[span]
    masked = jnp.where(live, grads[span].astype(jnp.float32), 0.0).astype(grads.dtype)
    dp = lax.axis_index("dp")
    x, y = dp // NY, lax.rem(dp, NY)
    first, _ = x_steps(lax.axis_index("expert"))
    rows = part.shape[2]
    for pair in range(NX // 2):
        columns = slice(pair * 4 * NY * rows, (pair + 1) * 4 * NY * rows)
        product = transposed_dot(acts[0, 0, span, :, columns], masked)
        for i in range(2):
            apart = jnp.bitwise_xor(2 * pair + i, x)
            slot = jnp.where(
                apart == 0, 0, jnp.where(apart == 2, 3, jnp.where(apart == first, 2, 1))
            )
            for j in range(NY):
                start = (i * NY + j) * 2 * rows
                halves = [product[start + k * rows : start + (k + 1) * rows] for k in range(2)]
                part[slot, jnp.bitwise_xor(j, y)] = jnp.concatenate(halves, axis=1)


def multiply_span(span, counts, activations, grads):
    _, _, _, slots, rows = activations.shape
    width = grads.shape[-1]
    vmem = pl.BlockSpec(memory_space=pltpu.VMEM)
    return pl.pallas_call(
        functools.partial(span_kernel, span),
        in_specs=[pl.BlockSpec(memory_space=pltpu.SMEM), vmem, vmem],
        out_specs=vmem,
        out_shape=jax.ShapeDtypeStruct((NX, NY, rows // (2 * NX * NY), 2 * width), jnp.float32),
        compiler_params=pltpu.CompilerParams(vmem_limit_bytes=VMEM_BYTES),
        cost_estimate=cost(2 * slots * rows * width, 6 << 20),
    )(counts, activations, grads)


def narrow(values, scale):
    return (values * scale).astype(jnp.float16)


def widen(values, scale):
    return values.astype(jnp.float32) * (1.0 / scale)


def after(value, *earlier):
    return lax.optimization_barrier((value, *earlier))[0]


def local(activations, out_grads, counts, first_moment, second_moment):
    live = counts[0, 0]
    grads = lax.all_gather(out_grads[0, 0], "expert", axis=1, tiled=True)

    other = multiply_span(1, live, activations, grads)
    other_out = narrow(other[2:], X_SCALE)
    other_in = send(other_out, over_x(0))
    own = multiply_span(0, live, activations, after(grads, other_out))
    own_out = narrow(own[2:], X_SCALE)
    own_in = send(own_out, over_x(0))
    other_pass = narrow(after(other[1], own_out) + widen(other_in[1], X_SCALE), X_SCALE)
    other_last = send(other_pass, over_x(1))
    own_pass = narrow(after(own[1], other_pass) + widen(own_in[1], X_SCALE), X_SCALE)
    own_last = send(own_pass, over_x(1))

    other = after(other[0], own_pass) + widen(other_in[0], X_SCALE) + widen(other_last, X_SCALE)
    other_out = [narrow(other[k], Y_SCALE) for k in range(1, NY)]
    other_in = [send(block, over_y(k)) for k, block in enumerate(other_out, 1)]
    own = after(own[0], *other_out) + widen(own_in[0], X_SCALE) + widen(own_last, X_SCALE)
    own_out = [narrow(own[k], Y_SCALE) for k in range(1, NY)]
    own_in = [send(block, over_y(k)) for k, block in enumerate(own_out, 1)]
    other = after(other[0], *own_out) + sum(widen(block, Y_SCALE) for block in other_in)
    from_mirror = send(narrow(other, Z_SCALE), mirrored)
    grad = own[0] + sum(widen(block, Y_SCALE) for block in own_in) + widen(from_mirror, Z_SCALE)
    width = out_grads.shape[-1]
    grad = jnp.concatenate([grad[:, :width], grad[:, width:]])[None, None]
    new_first = 0.9 * first_moment + 0.1 * grad
    new_second = 0.95 * second_moment + 0.05 * grad * grad
    direction = new_first / (jnp.sqrt(new_second) + 1e-08)
    return (new_first, new_second, direction)


def solution(mesh):
    state = P("pipe", "expert", "dp", None)
    return jax.shard_map(
        local,
        mesh=mesh,
        in_specs=(
            P("dp", "pipe", None, None, "expert"),
            P("dp", "pipe", None, "expert", None),
            P("dp", "pipe", None),
            state,
            state,
        ),
        out_specs=(state, state, state),
        check_vma=False,
    )
```

time: 107 us -> 101 us (0.944)
  the two profiles are of different devices: /device:TPU:6 before, /device:TPU:61 now
where the time goes in v3:
time: 101 us
  starting transfers between devices  42.3 us (42%)
  waiting for transfers between devices  29.2 us (29%)
  blocking collectives  18.5 us (18%)
  Pallas kernels  4.74 us (5%)
  local copies, waits for them, and re-layouts  2.81 us (3%)
  other arithmetic  2.54 us (3%)
    ppermute x11, starting transfers between devices, send(): return lax.ppermute(block, AXES, pairs)  42.3 us
    ppermute x11, waiting for transfers between devices, send(): return lax.ppermute(block, AXES, pairs)  29.2 us
    all_gather x1, blocking collectives, local(): grads = lax.all_gather(out_grads[0, 0], 'expert', axis=1, tiled=True)  18.5 us
    pallas_call x2, Pallas kernels, multiply_span(): pl.pallas_call(functools.partial(span_kernel, span), in_specs=[pl.BlockSp...  4.74 us
    unnamed x8, local copies, waits for them, and re-layouts  2.45 us
  transfers between devices with their start and end apart: 11, of which 4 were waited for; matrix products, arithmetic and copies ran while one was open for 2% of the time, Pallas kernels for 2%

profile of v3, /device:TPU:61, one launch (start us, length us, event | category | flops | bytes accessed | tf_op | source)
XLA Modules:
  0.0 101.0 jit_solution(12794478990951146627)
XLA Ops:
  0.6 18.5 %all-gather = bf16[1,1,2,384,576]{4,3,2,1,0:T(8,128)(2,1)S(1)} all-gather(bf16[1,1,2,96,576]{4,3,2,1,0:T(8,128)(2,1)} %param.6), channel_id=2, replica_groups=mesh['dp'=16,'pipe'=8,'expert'=4] {'expert'}, dimensions={3}, use_global_device_ids=true | all-gather | bytes 1105920 | tf_op jit(solution)/shard_map/all_gather | solution.py:105
  19.1 0.0 copy-start
  19.1 1.8 %copy-done = bf16[1,1,2,384,1792]{4,3,2,1,0:T(8,128)(2,1)S(1)} copy-done((bf16[1,1,2,384,1792]{4,3,2,1,0:T(8,128)(2,1)S(1)}, bf16[1,1,2,384,1792]{4,3,2,1,0:T(8,128)(2,1)}, u32[]{:S(2)}) %copy-start) | copy-done | bytes 2752536
  20.9 0.0 copy-start.1
  20.9 0.7 copy-done.1
  21.6 2.4 %shard_map.76 = f32[4,4,56,1152]{3,2,1,0:T(8,128)S(1)} custom-call(s32[2]{0:T(128)S(1)} %bitcast.56, bf16[1,1,2,384,1792]{4,3,2,1,0:T(8,128)(2,1)S(1)} %copy-done, bf16[2,384,576]{2,1,0:T(8,128)(2,1)S(1)} %bitcast.54), custom_call_target="tpu_custom_call" | custom-call | flops 792723456 | bytes 6291456 | tf_op jit(solution)/shard_map/pallas_call | solution.py:81
  23.9 0.2 fusion.1
  24.1 2.2 %collective-permute-start = (f16[2,4,56,1152]{3,2,1,0:T(8,128)(2,1)S(1)}, f16[2,4,56,1152]{3,2,1,0:T(8,128)(2,1)S(1)}, u32[]{:S(2)}, u32[]{:S(2)}) collective-permute-start(f16[2,4,56,1152]{3,2,1,0:T(8,128)(2,1)S(1)} %fusion.1), channel_id=1, source_target_pairs={{0,128},{1,385},{2,130},{3,387},{4,132},{5,389},{6,134},{7,391},{8... | collective-permute-start | bytes 3096584 | tf_op jit(solution)/shard_map/ppermute | solution.py:45
  26.3 2.4 %shard_map.77 = f32[4,4,56,1152]{3,2,1,0:T(8,128)S(1)} custom-call(s32[2]{0:T(128)S(1)} %bitcast.57, bf16[1,1,2,384,1792]{4,3,2,1,0:T(8,128)(2,1)S(1)} %copy-done, bf16[2,384,576]{2,1,0:T(8,128)(2,1)S(1)} %bitcast.55), custom_call_target="tpu_custom_call" | custom-call | flops 792723456 | bytes 6291456 | tf_op jit(solution)/shard_map/pallas_call | solution.py:81
  28.7 0.2 fusion
  28.9 3.1 %collective-permute-start.1 = (f16[2,4,56,1152]{3,2,1,0:T(8,128)(2,1)S(1)}, f16[2,4,56,1152]{3,2,1,0:T(8,128)(2,1)S(1)}, u32[]{:S(2)}, u32[]{:S(2)}) collective-permute-start(f16[2,4,56,1152]{3,2,1,0:T(8,128)(2,1)S(1)} %fusion), channel_id=1, source_target_pairs={{0,128},{1,385},{2,130},{3,387},{4,132},{5,389},{6,134},{7,391},{8... | collective-permute-start | bytes 3096584 | tf_op jit(solution)/shard_map/ppermute | solution.py:45
  32.0 0.1 slice_bitcast_fusion
  32.1 0.1 slice_bitcast_fusion.1
  32.3 7.5 %collective-permute-done = f16[2,4,56,1152]{3,2,1,0:T(8,128)(2,1)S(1)} collective-permute-done((f16[2,4,56,1152]{3,2,1,0:T(8,128)(2,1)S(1)}, f16[2,4,56,1152]{3,2,1,0:T(8,128)(2,1)S(1)}, u32[]{:S(2)}, u32[]{:S(2)}) %collective-permute-start) | collective-permute-done | bytes 1032224 | tf_op jit(solution)/shard_map/ppermute | solution.py:45
  39.8 0.2 fusion.7
  40.0 3.7 %collective-permute-start.2 = (f16[4,56,1152]{2,1,0:T(8,128)(2,1)S(1)}, f16[4,56,1152]{2,1,0:T(8,128)(2,1)S(1)}, u32[]{:S(2)}, u32[]{:S(2)}) collective-permute-start(f16[4,56,1152]{2,1,0:T(8,128)(2,1)S(1)} %fusion.7), channel_id=1, source_target_pairs={{0,384},{1,129},{2,386},{3,131},{4,388},{5,133},{6,390},{7,135},{8... | collective-permute-start | bytes 1548296 | tf_op jit(solution)/shard_map/ppermute | solution.py:45
  43.7 11.8 %collective-permute-done.1 = f16[2,4,56,1152]{3,2,1,0:T(8,128)(2,1)S(1)} collective-permute-done((f16[2,4,56,1152]{3,2,1,0:T(8,128)(2,1)S(1)}, f16[2,4,56,1152]{3,2,1,0:T(8,128)(2,1)S(1)}, u32[]{:S(2)}, u32[]{:S(2)}) %collective-permute-start.1) | collective-permute-done | bytes 1032224 | tf_op jit(solution)/shard_map/ppermute | solution.py:45
  55.5 0.2 fusion.5
  55.7 4.0 %collective-permute-start.3 = (f16[4,56,1152]{2,1,0:T(8,128)(2,1)S(1)}, f16[4,56,1152]{2,1,0:T(8,128)(2,1)S(1)}, u32[]{:S(2)}, u32[]{:S(2)}) collective-permute-start(f16[4,56,1152]{2,1,0:T(8,128)(2,1)S(1)} %fusion.5), channel_id=1, source_target_pairs={{0,384},{1,129},{2,386},{3,131},{4,388},{5,133},{6,390},{7,135},{8... | collective-permute-start | bytes 1548296 | tf_op jit(solution)/shard_map/ppermute | solution.py:45
  59.8 0.0 collective-permute-done.2
  59.8 0.2 fusion.3
  60.0 0.1 slice_bitcast_fusion.4
  60.1 2.7 %collective-permute-start.9 = (f16[56,1152]{1,0:T(8,128)(2,1)S(1)}, f16[56,1152]{1,0:T(8,128)(2,1)S(1)}, u32[]{:S(2)}, u32[]{:S(2)}) collective-permute-start(f16[56,1152]{1,0:T(8,128)(2,1)S(1)} %get-tuple-element.26), channel_id=1, source_target_pairs={{0,96},{1,97},{2,98},{3,99},{4,100},{5,101},{6,102},{7,103},{8,104... | collective-permute-start | bytes 387080 | tf_op jit(solution)/shard_map/ppermute | solution.py:45
  62.9 4.0 %collective-permute-start.8 = (f16[56,1152]{1,0:T(8,128)(2,1)S(1)}, f16[56,1152]{1,0:T(8,128)(2,1)S(1)}, u32[]{:S(2)}, u32[]{:S(2)}) collective-permute-start(f16[56,1152]{1,0:T(8,128)(2,1)S(1)} %get-tuple-element.27), channel_id=1, source_target_pairs={{0,64},{1,65},{2,66},{3,67},{4,68},{5,69},{6,70},{7,71},{8,72},{9,... | collective-permute-start | bytes 387080 | tf_op jit(solution)/shard_map/ppermute | solution.py:45
  66.9 2.5 %collective-permute-start.7 = (f16[56,1152]{1,0:T(8,128)(2,1)S(1)}, f16[56,1152]{1,0:T(8,128)(2,1)S(1)}, u32[]{:S(2)}, u32[]{:S(2)}) collective-permute-start(f16[56,1152]{1,0:T(8,128)(2,1)S(1)} %get-tuple-element.28), channel_id=1, source_target_pairs={{0,32},{1,33},{2,34},{3,35},{4,36},{5,37},{6,38},{7,39},{8,40},{9,... | collective-permute-start | bytes 387080 | tf_op jit(solution)/shard_map/ppermute | solution.py:45
  69.4 0.0 copy-start.2
  69.4 0.0 copy-start.3
  69.4 0.0 collective-permute-done.3
  69.4 0.2 fusion.2
  69.7 0.1 fusion.22
  69.8 3.3 %collective-permute-start.6 = (f16[56,1152]{1,0:T(8,128)(2,1)S(1)}, f16[56,1152]{1,0:T(8,128)(2,1)S(1)}, u32[]{:S(2)}, u32[]{:S(2)}) collective-permute-start(f16[56,1152]{1,0:T(8,128)(2,1)S(1)} %get-tuple-element.22), channel_id=1, source_target_pairs={{0,96},{1,97},{2,98},{3,99},{4,100},{5,101},{6,102},{7,103},{8,104... | collective-permute-start | bytes 387080 | tf_op jit(solution)/shard_map/ppermute | solution.py:45
  73.0 2.6 %collective-permute-start.5 = (f16[56,1152]{1,0:T(8,128)(2,1)S(1)}, f16[56,1152]{1,0:T(8,128)(2,1)S(1)}, u32[]{:S(2)}, u32[]{:S(2)}) collective-permute-start(f16[56,1152]{1,0:T(8,128)(2,1)S(1)} %get-tuple-element.23), channel_id=1, source_target_pairs={{0,64},{1,65},{2,66},{3,67},{4,68},{5,69},{6,70},{7,71},{8,72},{9,... | collective-permute-start | bytes 387080 | tf_op jit(solution)/shard_map/ppermute | solution.py:45
  75.6 0.0 collective-permute-done.9
  75.6 3.4 %collective-permute-start.4 = (f16[56,1152]{1,0:T(8,128)(2,1)S(1)}, f16[56,1152]{1,0:T(8,128)(2,1)S(1)}, u32[]{:S(2)}, u32[]{:S(2)}) collective-permute-start(f16[56,1152]{1,0:T(8,128)(2,1)S(1)} %get-tuple-element.24), channel_id=1, source_target_pairs={{0,32},{1,33},{2,34},{3,35},{4,36},{5,37},{6,38},{7,39},{8,40},{9,... | collective-permute-start | bytes 387080 | tf_op jit(solution)/shard_map/ppermute | solution.py:45
  79.1 3.3 %collective-permute-done.8 = f16[56,1152]{1,0:T(8,128)(2,1)S(1)} collective-permute-done((f16[56,1152]{1,0:T(8,128)(2,1)S(1)}, f16[56,1152]{1,0:T(8,128)(2,1)S(1)}, u32[]{:S(2)}, u32[]{:S(2)}) %collective-permute-start.8) | collective-permute-done | bytes 129056 | tf_op jit(solution)/shard_map/ppermute | solution.py:45
  82.3 0.0 collective-permute-done.7
  82.3 0.1 multiply_convert_fusion
  82.4 10.7 %collective-permute-start.10 = (f16[56,1152]{1,0:T(8,128)(2,1)S(1)}, f16[56,1152]{1,0:T(8,128)(2,1)S(1)}, u32[]{:S(2)}, u32[]{:S(2)}) collective-permute-start(f16[56,1152]{1,0:T(8,128)(2,1)S(1)} %multiply_convert_fusion), channel_id=1, source_target_pairs={{0,28},{1,29},{2,30},{3,31},{4,24},{5,25},{6,26},{7,27},{8,20},{9,... | collective-permute-start | bytes 387080 | tf_op jit(solution)/shard_map/ppermute | solution.py:45
  93.2 0.0 collective-permute-done.6
  93.2 0.0 collective-permute-done.5
  93.2 0.0 collective-permute-done.4
  93.2 6.6 %collective-permute-done.10 = f16[56,1152]{1,0:T(8,128)(2,1)S(1)} collective-permute-done((f16[56,1152]{1,0:T(8,128)(2,1)S(1)}, f16[56,1152]{1,0:T(8,128)(2,1)S(1)}, u32[]{:S(2)}, u32[]{:S(2)}) %collective-permute-start.10) | collective-permute-done | bytes 129056 | tf_op jit(solution)/shard_map/ppermute | solution.py:45
  99.8 0.1 fusion.13
  99.9 0.1 slice_bitcast_fusion.7
  100.0 0.0 copy-done.2
  100.0 0.0 copy-done.3
  100.0 1.0 add_divide_fusion
Async XLA Ops:
  19.1 1.8 %copy-start = (bf16[1,1,2,384,1792]{4,3,2,1,0:T(8,128)(2,1)S(1)}, bf16[1,1,2,384,1792]{4,3,2,1,0:T(8,128)(2,1)}, u32[]{:S(2)}) copy-start(bf16[1,1,2,384,1792]{4,3,2,1,0:T(8,128)(2,1)} %acts.3) | copy-start | bytes 8257540
  20.9 0.7 copy-start.1
  24.1 15.7 %collective-permute-start = (f16[2,4,56,1152]{3,2,1,0:T(8,128)(2,1)S(1)}, f16[2,4,56,1152]{3,2,1,0:T(8,128)(2,1)S(1)}, u32[]{:S(2)}, u32[]{:S(2)}) collective-permute-start(f16[2,4,56,1152]{3,2,1,0:T(8,128)(2,1)S(1)} %fusion.1), channel_id=1, source_target_pairs={{0,128},{1,385},{2,130},{3,387},{4,132},{5,389},{6,134},{7,391},{8... | collective-permute-start | bytes 3096584 | tf_op jit(solution)/shard_map/ppermute | solution.py:45
  28.9 26.7 %collective-permute-start.1 = (f16[2,4,56,1152]{3,2,1,0:T(8,128)(2,1)S(1)}, f16[2,4,56,1152]{3,2,1,0:T(8,128)(2,1)S(1)}, u32[]{:S(2)}, u32[]{:S(2)}) collective-permute-start(f16[2,4,56,1152]{3,2,1,0:T(8,128)(2,1)S(1)} %fusion), channel_id=1, source_target_pairs={{0,128},{1,385},{2,130},{3,387},{4,132},{5,389},{6,134},{7,391},{8... | collective-permute-start | bytes 3096584 | tf_op jit(solution)/shard_map/ppermute | solution.py:45
  40.0 19.8 %collective-permute-start.2 = (f16[4,56,1152]{2,1,0:T(8,128)(2,1)S(1)}, f16[4,56,1152]{2,1,0:T(8,128)(2,1)S(1)}, u32[]{:S(2)}, u32[]{:S(2)}) collective-permute-start(f16[4,56,1152]{2,1,0:T(8,128)(2,1)S(1)} %fusion.7), channel_id=1, source_target_pairs={{0,384},{1,129},{2,386},{3,131},{4,388},{5,133},{6,390},{7,135},{8... | collective-permute-start | bytes 1548296 | tf_op jit(solution)/shard_map/ppermute | solution.py:45
  55.7 13.7 %collective-permute-start.3 = (f16[4,56,1152]{2,1,0:T(8,128)(2,1)S(1)}, f16[4,56,1152]{2,1,0:T(8,128)(2,1)S(1)}, u32[]{:S(2)}, u32[]{:S(2)}) collective-permute-start(f16[4,56,1152]{2,1,0:T(8,128)(2,1)S(1)} %fusion.5), channel_id=1, source_target_pairs={{0,384},{1,129},{2,386},{3,131},{4,388},{5,133},{6,390},{7,135},{8... | collective-permute-start | bytes 1548296 | tf_op jit(solution)/shard_map/ppermute | solution.py:45
  60.1 15.5 %collective-permute-start.9 = (f16[56,1152]{1,0:T(8,128)(2,1)S(1)}, f16[56,1152]{1,0:T(8,128)(2,1)S(1)}, u32[]{:S(2)}, u32[]{:S(2)}) collective-permute-start(f16[56,1152]{1,0:T(8,128)(2,1)S(1)} %get-tuple-element.26), channel_id=1, source_target_pairs={{0,96},{1,97},{2,98},{3,99},{4,100},{5,101},{6,102},{7,103},{8,104... | collective-permute-start | bytes 387080 | tf_op jit(solution)/shard_map/ppermute | solution.py:45
  62.9 19.5 %collective-permute-start.8 = (f16[56,1152]{1,0:T(8,128)(2,1)S(1)}, f16[56,1152]{1,0:T(8,128)(2,1)S(1)}, u32[]{:S(2)}, u32[]{:S(2)}) collective-permute-start(f16[56,1152]{1,0:T(8,128)(2,1)S(1)} %get-tuple-element.27), channel_id=1, source_target_pairs={{0,64},{1,65},{2,66},{3,67},{4,68},{5,69},{6,70},{7,71},{8,72},{9,... | collective-permute-start | bytes 387080 | tf_op jit(solution)/shard_map/ppermute | solution.py:45
  66.9 15.5 %collective-permute-start.7 = (f16[56,1152]{1,0:T(8,128)(2,1)S(1)}, f16[56,1152]{1,0:T(8,128)(2,1)S(1)}, u32[]{:S(2)}, u32[]{:S(2)}) collective-permute-start(f16[56,1152]{1,0:T(8,128)(2,1)S(1)} %get-tuple-element.28), channel_id=1, source_target_pairs={{0,32},{1,33},{2,34},{3,35},{4,36},{5,37},{6,38},{7,39},{8,40},{9,... | collective-permute-start | bytes 387080 | tf_op jit(solution)/shard_map/ppermute | solution.py:45
  69.4 30.6 %copy-start.2 = (f32[1,1,112,576]{3,2,1,0:T(8,128)S(1)}, f32[1,1,112,576]{3,2,1,0:T(8,128)}, u32[]{:S(2)}) copy-start(f32[1,1,112,576]{3,2,1,0:T(8,128)} %param.9) | copy-start | bytes 774148
  69.4 30.6 %copy-start.3 = (f32[1,1,112,576]{3,2,1,0:T(8,128)S(1)}, f32[1,1,112,576]{3,2,1,0:T(8,128)}, u32[]{:S(2)}) copy-start(f32[1,1,112,576]{3,2,1,0:T(8,128)} %param.8) | copy-start | bytes 774148
  69.8 23.4 %collective-permute-start.6 = (f16[56,1152]{1,0:T(8,128)(2,1)S(1)}, f16[56,1152]{1,0:T(8,128)(2,1)S(1)}, u32[]{:S(2)}, u32[]{:S(2)}) collective-permute-start(f16[56,1152]{1,0:T(8,128)(2,1)S(1)} %get-tuple-element.22), channel_id=1, source_target_pairs={{0,96},{1,97},{2,98},{3,99},{4,100},{5,101},{6,102},{7,103},{8,104... | collective-permute-start | bytes 387080 | tf_op jit(solution)/shard_map/ppermute | solution.py:45
  73.0 20.1 %collective-permute-start.5 = (f16[56,1152]{1,0:T(8,128)(2,1)S(1)}, f16[56,1152]{1,0:T(8,128)(2,1)S(1)}, u32[]{:S(2)}, u32[]{:S(2)}) collective-permute-start(f16[56,1152]{1,0:T(8,128)(2,1)S(1)} %get-tuple-element.23), channel_id=1, source_target_pairs={{0,64},{1,65},{2,66},{3,67},{4,68},{5,69},{6,70},{7,71},{8,72},{9,... | collective-permute-start | bytes 387080 | tf_op jit(solution)/shard_map/ppermute | solution.py:45
  75.6 17.5 %collective-permute-start.4 = (f16[56,1152]{1,0:T(8,128)(2,1)S(1)}, f16[56,1152]{1,0:T(8,128)(2,1)S(1)}, u32[]{:S(2)}, u32[]{:S(2)}) collective-permute-start(f16[56,1152]{1,0:T(8,128)(2,1)S(1)} %get-tuple-element.24), channel_id=1, source_target_pairs={{0,32},{1,33},{2,34},{3,35},{4,36},{5,37},{6,38},{7,39},{8,40},{9,... | collective-permute-start | bytes 387080 | tf_op jit(solution)/shard_map/ppermute | solution.py:45
  82.4 17.4 %collective-permute-start.10 = (f16[56,1152]{1,0:T(8,128)(2,1)S(1)}, f16[56,1152]{1,0:T(8,128)(2,1)S(1)}, u32[]{:S(2)}, u32[]{:S(2)}) collective-permute-start(f16[56,1152]{1,0:T(8,128)(2,1)S(1)} %multiply_convert_fusion), channel_id=1, source_target_pairs={{0,28},{1,29},{2,30},{3,31},{4,24},{5,25},{6,26},{7,27},{8,20},{9,... | collective-permute-start | bytes 387080 | tf_op jit(solution)/shard_map/ppermute | solution.py:45

commit v4 on v3

--- a/solution.py
+++ b/solution.py
@@ -53,16 +53,28 @@
     return pl.CostEstimate(flops=flops, bytes_accessed=read_and_written, transcendentals=0)
 
 
-def span_kernel(span, counts, acts, grads, part):
-    live = lax.broadcasted_iota(jnp.int32, grads.shape[1:], 0) < counts[span]
-    masked = jnp.where(live, grads[span].astype(jnp.float32), 0.0).astype(grads.dtype)
+def pair_columns(rows):
+    width = 2 * rows // NX
+    return [slice(start, start + width) for start in range(0, rows, width)]
+
+
+def span_kernel(span, counts, acts, grads, part, acts_here, sems):
+    fetches = []
+    for pair, columns in enumerate(pair_columns(acts.shape[-1])):
+        source = acts.at[0, 0, span, :, columns]
+        fetches.append(pltpu.make_async_copy(source, acts_here.at[:, columns], sems.at[pair]))
+        fetches[-1].start()
+    shards, _, slots, width = grads.shape
+    mine = grads[:, span].reshape(shards * slots, width)
+    live = lax.broadcasted_iota(jnp.int32, mine.shape, 0) < counts[span]
+    masked = jnp.where(live, mine.astype(jnp.float32), 0.0).astype(mine.dtype)
     dp = lax.axis_index("dp")
     x, y = dp // NY, lax.rem(dp, NY)
     first, _ = x_steps(lax.axis_index("expert"))
     rows = part.shape[2]
-    for pair in range(NX // 2):
-        columns = slice(pair * 4 * NY * rows, (pair + 1) * 4 * NY * rows)
-        product = transposed_dot(acts[0, 0, span, :, columns], masked)
+    for pair, columns in enumerate(pair_columns(acts.shape[-1])):
+        fetches[pair].wait()
+        product = transposed_dot(acts_here[:, columns], masked)
         for i in range(2):
             apart = jnp.bitwise_xor(2 * pair + i, x)
             slot = jnp.where(
@@ -74,18 +86,30 @@
                 part[slot, jnp.bitwise_xor(j, y)] = jnp.concatenate(halves, axis=1)
 
 
+def in_hbm(array):
+    return pltpu.with_memory_space_constraint(array, pltpu.HBM)
+
+
 def multiply_span(span, counts, activations, grads):
     _, _, _, slots, rows = activations.shape
     width = grads.shape[-1]
     vmem = pl.BlockSpec(memory_space=pltpu.VMEM)
     return pl.pallas_call(
         functools.partial(span_kernel, span),
-        in_specs=[pl.BlockSpec(memory_space=pltpu.SMEM), vmem, vmem],
-        out_specs=vmem,
+        grid_spec=pltpu.PrefetchScalarGridSpec(
+            num_scalar_prefetch=1,
+            grid=(),
+            in_specs=[pl.BlockSpec(memory_space=pltpu.HBM), vmem],
+            out_specs=vmem,
+            scratch_shapes=[
+                pltpu.VMEM((slots, rows), activations.dtype),
+                pltpu.SemaphoreType.DMA((NX // 2,)),
+            ],
+        ),
         out_shape=jax.ShapeDtypeStruct((NX, NY, rows // (2 * NX * NY), 2 * width), jnp.float32),
         compiler_params=pltpu.CompilerParams(vmem_limit_bytes=VMEM_BYTES),
         cost_estimate=cost(2 * slots * rows * width, 6 << 20),
-    )(counts, activations, grads)
+    )(counts, in_hbm(activations), grads)
 
 
 def narrow(values, scale):
@@ -101,8 +125,8 @@
 
 
 def local(activations, out_grads, counts, first_moment, second_moment):
-    live = counts[0, 0]
-    grads = lax.all_gather(out_grads[0, 0], "expert", axis=1, tiled=True)
+    live = in_hbm(counts[0, 0])
+    grads = lax.all_gather(out_grads[0, 0], "expert")
 
     other = multiply_span(1, live, activations, grads)
     other_out = narrow(other[2:], X_SCALE)

time: 101 us -> 100 us (0.990)
  Pallas kernels: 4.74 us -> 7.5 us
  local copies, waits for them, and re-layouts: 2.81 us -> 0.38 us
  waiting for transfers between devices: 29.2 us -> 27.9 us
    pallas_call x2, Pallas kernels: 4.74 us -> 7.5 us  [multiply_span(): pl.pallas_call(functools.partial(span_kernel, span), grid_spec=pltpu.Pref...]
    unnamed x8 -> x4, local copies, waits for them, and re-layouts: 2.45 us -> 0.01 us
    ppermute x11, waiting for transfers between devices: 29.2 us -> 27.9 us  [send(): return lax.ppermute(block, AXES, pairs)]
  transfers between devices with their start and end apart: 11 -> 11, of which waited for: 4 -> 4; matrix products, arithmetic and copies ran while one was open for 2% -> 2% of each run, Pallas kernels for 2% -> 4%
where the time goes in v4:
time: 100 us; the launch traced here: 99.9 us
  starting transfers between devices  42.3 us (42%)
  waiting for transfers between devices  27.9 us (28%)
  blocking collectives  18.5 us (18%)
  Pallas kernels  7.5 us (8%)
  other arithmetic  2.54 us (3%)
    ppermute x11, starting transfers between devices, send(): return lax.ppermute(block, AXES, pairs)  42.3 us
    ppermute x11, waiting for transfers between devices, send(): return lax.ppermute(block, AXES, pairs)  27.9 us
    all_gather x1, blocking collectives, local(): grads = lax.all_gather(out_grads[0, 0], 'expert')  18.5 us
    pallas_call x2, Pallas kernels, multiply_span(): pl.pallas_call(functools.partial(span_kernel, span), grid_spec=pltpu.Pref...  7.5 us
  transfers between devices with their start and end apart: 11, of which 4 were waited for; matrix products, arithmetic and copies ran while one was open for 2% of the time, Pallas kernels for 4%

profile of v4, /device:TPU:61, one launch (start us, length us, event | category | flops | bytes accessed | tf_op | source)
XLA Modules:
  0.0 99.9 jit_solution(8814571536877584324)
XLA Ops:
  0.6 18.5 %all-gather = bf16[4,1,2,96,576]{4,3,2,1,0:T(8,128)(2,1)S(1)} all-gather(bf16[1,1,2,96,576]{4,3,2,1,0:T(8,128)(2,1)} %param.6), channel_id=2, replica_groups=mesh['dp'=16,'pipe'=8,'expert'=4] {'expert'}, dimensions={0}, use_global_device_ids=true | all-gather | bytes 1105920 | tf_op jit(solution)/shard_map/all_gather | solution.py:129
  19.1 3.8 %shard_map.76 = f32[4,4,56,1152]{3,2,1,0:T(8,128)S(1)} custom-call(s32[2]{0:T(128)} %bitcast.56, bf16[1,1,2,384,1792]{4,3,2,1,0:T(8,128)(2,1)} %acts.3, bf16[4,2,96,576]{3,2,1,0:T(8,128)(2,1)S(1)} %bitcast.54), custom_call_target="tpu_custom_call" | custom-call | flops 792723456 | bytes 6291456 | tf_op jit(solution)/shard_map/pallas_call | solution.py:97
  22.9 0.2 fusion.1
  23.1 2.2 %collective-permute-start = (f16[2,4,56,1152]{3,2,1,0:T(8,128)(2,1)S(1)}, f16[2,4,56,1152]{3,2,1,0:T(8,128)(2,1)S(1)}, u32[]{:S(2)}, u32[]{:S(2)}) collective-permute-start(f16[2,4,56,1152]{3,2,1,0:T(8,128)(2,1)S(1)} %fusion.1), channel_id=1, source_target_pairs={{0,128},{1,385},{2,130},{3,387},{4,132},{5,389},{6,134},{7,391},{8... | collective-permute-start | bytes 3096584 | tf_op jit(solution)/shard_map/ppermute | solution.py:45
  25.2 3.8 %shard_map.77 = f32[4,4,56,1152]{3,2,1,0:T(8,128)S(1)} custom-call(s32[2]{0:T(128)} %bitcast.57, bf16[1,1,2,384,1792]{4,3,2,1,0:T(8,128)(2,1)} %acts.3, bf16[4,2,96,576]{3,2,1,0:T(8,128)(2,1)S(1)} %bitcast.55), custom_call_target="tpu_custom_call" | custom-call | flops 792723456 | bytes 6291456 | tf_op jit(solution)/shard_map/pallas_call | solution.py:97
  29.0 0.2 fusion
  29.2 3.1 %collective-permute-start.1 = (f16[2,4,56,1152]{3,2,1,0:T(8,128)(2,1)S(1)}, f16[2,4,56,1152]{3,2,1,0:T(8,128)(2,1)S(1)}, u32[]{:S(2)}, u32[]{:S(2)}) collective-permute-start(f16[2,4,56,1152]{3,2,1,0:T(8,128)(2,1)S(1)} %fusion), channel_id=1, source_target_pairs={{0,128},{1,385},{2,130},{3,387},{4,132},{5,389},{6,134},{7,391},{8... | collective-permute-start | bytes 3096584 | tf_op jit(solution)/shard_map/ppermute | solution.py:45
  32.3 0.1 slice_bitcast_fusion
  32.5 0.1 slice_bitcast_fusion.1
  32.6 6.1 %collective-permute-done = f16[2,4,56,1152]{3,2,1,0:T(8,128)(2,1)S(1)} collective-permute-done((f16[2,4,56,1152]{3,2,1,0:T(8,128)(2,1)S(1)}, f16[2,4,56,1152]{3,2,1,0:T(8,128)(2,1)S(1)}, u32[]{:S(2)}, u32[]{:S(2)}) %collective-permute-start) | collective-permute-done | bytes 1032224 | tf_op jit(solution)/shard_map/ppermute | solution.py:45
  38.7 0.2 fusion.7
  38.9 3.7 %collective-permute-start.2 = (f16[4,56,1152]{2,1,0:T(8,128)(2,1)S(1)}, f16[4,56,1152]{2,1,0:T(8,128)(2,1)S(1)}, u32[]{:S(2)}, u32[]{:S(2)}) collective-permute-start(f16[4,56,1152]{2,1,0:T(8,128)(2,1)S(1)} %fusion.7), channel_id=1, source_target_pairs={{0,384},{1,129},{2,386},{3,131},{4,388},{5,133},{6,390},{7,135},{8... | collective-permute-start | bytes 1548296 | tf_op jit(solution)/shard_map/ppermute | solution.py:45
  42.7 11.8 %collective-permute-done.1 = f16[2,4,56,1152]{3,2,1,0:T(8,128)(2,1)S(1)} collective-permute-done((f16[2,4,56,1152]{3,2,1,0:T(8,128)(2,1)S(1)}, f16[2,4,56,1152]{3,2,1,0:T(8,128)(2,1)S(1)}, u32[]{:S(2)}, u32[]{:S(2)}) %collective-permute-start.1) | collective-permute-done | bytes 1032224 | tf_op jit(solution)/shard_map/ppermute | solution.py:45
  54.5 0.2 fusion.5
  54.7 4.0 %collective-permute-start.3 = (f16[4,56,1152]{2,1,0:T(8,128)(2,1)S(1)}, f16[4,56,1152]{2,1,0:T(8,128)(2,1)S(1)}, u32[]{:S(2)}, u32[]{:S(2)}) collective-permute-start(f16[4,56,1152]{2,1,0:T(8,128)(2,1)S(1)} %fusion.5), channel_id=1, source_target_pairs={{0,384},{1,129},{2,386},{3,131},{4,388},{5,133},{6,390},{7,135},{8... | collective-permute-start | bytes 1548296 | tf_op jit(solution)/shard_map/ppermute | solution.py:45
  58.7 0.0 collective-permute-done.2
  58.7 0.2 fusion.3
  59.0 0.1 slice_bitcast_fusion.4
  59.0 2.8 %collective-permute-start.9 = (f16[56,1152]{1,0:T(8,128)(2,1)S(1)}, f16[56,1152]{1,0:T(8,128)(2,1)S(1)}, u32[]{:S(2)}, u32[]{:S(2)}) collective-permute-start(f16[56,1152]{1,0:T(8,128)(2,1)S(1)} %get-tuple-element.26), channel_id=1, source_target_pairs={{0,96},{1,97},{2,98},{3,99},{4,100},{5,101},{6,102},{7,103},{8,104... | collective-permute-start | bytes 387080 | tf_op jit(solution)/shard_map/ppermute | solution.py:45
  61.8 4.0 %collective-permute-start.8 = (f16[56,1152]{1,0:T(8,128)(2,1)S(1)}, f16[56,1152]{1,0:T(8,128)(2,1)S(1)}, u32[]{:S(2)}, u32[]{:S(2)}) collective-permute-start(f16[56,1152]{1,0:T(8,128)(2,1)S(1)} %get-tuple-element.27), channel_id=1, source_target_pairs={{0,64},{1,65},{2,66},{3,67},{4,68},{5,69},{6,70},{7,71},{8,72},{9,... | collective-permute-start | bytes 387080 | tf_op jit(solution)/shard_map/ppermute | solution.py:45
  65.8 2.5 %collective-permute-start.7 = (f16[56,1152]{1,0:T(8,128)(2,1)S(1)}, f16[56,1152]{1,0:T(8,128)(2,1)S(1)}, u32[]{:S(2)}, u32[]{:S(2)}) collective-permute-start(f16[56,1152]{1,0:T(8,128)(2,1)S(1)} %get-tuple-element.28), channel_id=1, source_target_pairs={{0,32},{1,33},{2,34},{3,35},{4,36},{5,37},{6,38},{7,39},{8,40},{9,... | collective-permute-start | bytes 387080 | tf_op jit(solution)/shard_map/ppermute | solution.py:45
  68.3 0.0 copy-start
  68.3 0.0 copy-start.1
  68.4 0.0 collective-permute-done.3
  68.4 0.2 fusion.2
  68.6 0.1 fusion.22
  68.7 3.3 %collective-permute-start.6 = (f16[56,1152]{1,0:T(8,128)(2,1)S(1)}, f16[56,1152]{1,0:T(8,128)(2,1)S(1)}, u32[]{:S(2)}, u32[]{:S(2)}) collective-permute-start(f16[56,1152]{1,0:T(8,128)(2,1)S(1)} %get-tuple-element.22), channel_id=1, source_target_pairs={{0,96},{1,97},{2,98},{3,99},{4,100},{5,101},{6,102},{7,103},{8,104... | collective-permute-start | bytes 387080 | tf_op jit(solution)/shard_map/ppermute | solution.py:45
  72.0 2.6 %collective-permute-start.5 = (f16[56,1152]{1,0:T(8,128)(2,1)S(1)}, f16[56,1152]{1,0:T(8,128)(2,1)S(1)}, u32[]{:S(2)}, u32[]{:S(2)}) collective-permute-start(f16[56,1152]{1,0:T(8,128)(2,1)S(1)} %get-tuple-element.23), channel_id=1, source_target_pairs={{0,64},{1,65},{2,66},{3,67},{4,68},{5,69},{6,70},{7,71},{8,72},{9,... | collective-permute-start | bytes 387080 | tf_op jit(solution)/shard_map/ppermute | solution.py:45
  74.6 0.0 collective-permute-done.9
  74.6 3.4 %collective-permute-start.4 = (f16[56,1152]{1,0:T(8,128)(2,1)S(1)}, f16[56,1152]{1,0:T(8,128)(2,1)S(1)}, u32[]{:S(2)}, u32[]{:S(2)}) collective-permute-start(f16[56,1152]{1,0:T(8,128)(2,1)S(1)} %get-tuple-element.24), channel_id=1, source_target_pairs={{0,32},{1,33},{2,34},{3,35},{4,36},{5,37},{6,38},{7,39},{8,40},{9,... | collective-permute-start | bytes 387080 | tf_op jit(solution)/shard_map/ppermute | solution.py:45
  78.0 3.3 %collective-permute-done.8 = f16[56,1152]{1,0:T(8,128)(2,1)S(1)} collective-permute-done((f16[56,1152]{1,0:T(8,128)(2,1)S(1)}, f16[56,1152]{1,0:T(8,128)(2,1)S(1)}, u32[]{:S(2)}, u32[]{:S(2)}) %collective-permute-start.8) | collective-permute-done | bytes 129056 | tf_op jit(solution)/shard_map/ppermute | solution.py:45
  81.3 0.0 collective-permute-done.7
  81.3 0.1 multiply_convert_fusion
  81.4 10.7 %collective-permute-start.10 = (f16[56,1152]{1,0:T(8,128)(2,1)S(1)}, f16[56,1152]{1,0:T(8,128)(2,1)S(1)}, u32[]{:S(2)}, u32[]{:S(2)}) collective-permute-start(f16[56,1152]{1,0:T(8,128)(2,1)S(1)} %multiply_convert_fusion), channel_id=1, source_target_pairs={{0,28},{1,29},{2,30},{3,31},{4,24},{5,25},{6,26},{7,27},{8,20},{9,... | collective-permute-start | bytes 387080 | tf_op jit(solution)/shard_map/ppermute | solution.py:45
  92.1 0.0 collective-permute-done.6
  92.1 0.0 collective-permute-done.5
  92.1 0.0 collective-permute-done.4
  92.1 6.6 %collective-permute-done.10 = f16[56,1152]{1,0:T(8,128)(2,1)S(1)} collective-permute-done((f16[56,1152]{1,0:T(8,128)(2,1)S(1)}, f16[56,1152]{1,0:T(8,128)(2,1)S(1)}, u32[]{:S(2)}, u32[]{:S(2)}) %collective-permute-start.10) | collective-permute-done | bytes 129056 | tf_op jit(solution)/shard_map/ppermute | solution.py:45
  98.7 0.1 fusion.13
  98.8 0.1 slice_bitcast_fusion.7
  98.9 0.0 copy-done
  98.9 0.0 copy-done.1
  99.0 1.0 add_divide_fusion
Async XLA Ops:
  23.1 15.7 %collective-permute-start = (f16[2,4,56,1152]{3,2,1,0:T(8,128)(2,1)S(1)}, f16[2,4,56,1152]{3,2,1,0:T(8,128)(2,1)S(1)}, u32[]{:S(2)}, u32[]{:S(2)}) collective-permute-start(f16[2,4,56,1152]{3,2,1,0:T(8,128)(2,1)S(1)} %fusion.1), channel_id=1, source_target_pairs={{0,128},{1,385},{2,130},{3,387},{4,132},{5,389},{6,134},{7,391},{8... | collective-permute-start | bytes 3096584 | tf_op jit(solution)/shard_map/ppermute | solution.py:45
  29.2 25.3 %collective-permute-start.1 = (f16[2,4,56,1152]{3,2,1,0:T(8,128)(2,1)S(1)}, f16[2,4,56,1152]{3,2,1,0:T(8,128)(2,1)S(1)}, u32[]{:S(2)}, u32[]{:S(2)}) collective-permute-start(f16[2,4,56,1152]{3,2,1,0:T(8,128)(2,1)S(1)} %fusion), channel_id=1, source_target_pairs={{0,128},{1,385},{2,130},{3,387},{4,132},{5,389},{6,134},{7,391},{8... | collective-permute-start | bytes 3096584 | tf_op jit(solution)/shard_map/ppermute | solution.py:45
  38.9 19.8 %collective-permute-start.2 = (f16[4,56,1152]{2,1,0:T(8,128)(2,1)S(1)}, f16[4,56,1152]{2,1,0:T(8,128)(2,1)S(1)}, u32[]{:S(2)}, u32[]{:S(2)}) collective-permute-start(f16[4,56,1152]{2,1,0:T(8,128)(2,1)S(1)} %fusion.7), channel_id=1, source_target_pairs={{0,384},{1,129},{2,386},{3,131},{4,388},{5,133},{6,390},{7,135},{8... | collective-permute-start | bytes 1548296 | tf_op jit(solution)/shard_map/ppermute | solution.py:45
  54.7 13.7 %collective-permute-start.3 = (f16[4,56,1152]{2,1,0:T(8,128)(2,1)S(1)}, f16[4,56,1152]{2,1,0:T(8,128)(2,1)S(1)}, u32[]{:S(2)}, u32[]{:S(2)}) collective-permute-start(f16[4,56,1152]{2,1,0:T(8,128)(2,1)S(1)} %fusion.5), channel_id=1, source_target_pairs={{0,384},{1,129},{2,386},{3,131},{4,388},{5,133},{6,390},{7,135},{8... | collective-permute-start | bytes 1548296 | tf_op jit(solution)/shard_map/ppermute | solution.py:45
  59.0 15.5 %collective-permute-start.9 = (f16[56,1152]{1,0:T(8,128)(2,1)S(1)}, f16[56,1152]{1,0:T(8,128)(2,1)S(1)}, u32[]{:S(2)}, u32[]{:S(2)}) collective-permute-start(f16[56,1152]{1,0:T(8,128)(2,1)S(1)} %get-tuple-element.26), channel_id=1, source_target_pairs={{0,96},{1,97},{2,98},{3,99},{4,100},{5,101},{6,102},{7,103},{8,104... | collective-permute-start | bytes 387080 | tf_op jit(solution)/shard_map/ppermute | solution.py:45
  61.8 19.5 %collective-permute-start.8 = (f16[56,1152]{1,0:T(8,128)(2,1)S(1)}, f16[56,1152]{1,0:T(8,128)(2,1)S(1)}, u32[]{:S(2)}, u32[]{:S(2)}) collective-permute-start(f16[56,1152]{1,0:T(8,128)(2,1)S(1)} %get-tuple-element.27), channel_id=1, source_target_pairs={{0,64},{1,65},{2,66},{3,67},{4,68},{5,69},{6,70},{7,71},{8,72},{9,... | collective-permute-start | bytes 387080 | tf_op jit(solution)/shard_map/ppermute | solution.py:45
  65.8 15.5 %collective-permute-start.7 = (f16[56,1152]{1,0:T(8,128)(2,1)S(1)}, f16[56,1152]{1,0:T(8,128)(2,1)S(1)}, u32[]{:S(2)}, u32[]{:S(2)}) collective-permute-start(f16[56,1152]{1,0:T(8,128)(2,1)S(1)} %get-tuple-element.28), channel_id=1, source_target_pairs={{0,32},{1,33},{2,34},{3,35},{4,36},{5,37},{6,38},{7,39},{8,40},{9,... | collective-permute-start | bytes 387080 | tf_op jit(solution)/shard_map/ppermute | solution.py:45
  68.3 30.6 %copy-start = (f32[1,1,112,576]{3,2,1,0:T(8,128)S(1)}, f32[1,1,112,576]{3,2,1,0:T(8,128)}, u32[]{:S(2)}) copy-start(f32[1,1,112,576]{3,2,1,0:T(8,128)} %param.9) | copy-start | bytes 774148
  68.3 30.6 %copy-start.1 = (f32[1,1,112,576]{3,2,1,0:T(8,128)S(1)}, f32[1,1,112,576]{3,2,1,0:T(8,128)}, u32[]{:S(2)}) copy-start(f32[1,1,112,576]{3,2,1,0:T(8,128)} %param.8) | copy-start | bytes 774148
  68.7 23.4 %collective-permute-start.6 = (f16[56,1152]{1,0:T(8,128)(2,1)S(1)}, f16[56,1152]{1,0:T(8,128)(2,1)S(1)}, u32[]{:S(2)}, u32[]{:S(2)}) collective-permute-start(f16[56,1152]{1,0:T(8,128)(2,1)S(1)} %get-tuple-element.22), channel_id=1, source_target_pairs={{0,96},{1,97},{2,98},{3,99},{4,100},{5,101},{6,102},{7,103},{8,104... | collective-permute-start | bytes 387080 | tf_op jit(solution)/shard_map/ppermute | solution.py:45
  72.0 20.1 %collective-permute-start.5 = (f16[56,1152]{1,0:T(8,128)(2,1)S(1)}, f16[56,1152]{1,0:T(8,128)(2,1)S(1)}, u32[]{:S(2)}, u32[]{:S(2)}) collective-permute-start(f16[56,1152]{1,0:T(8,128)(2,1)S(1)} %get-tuple-element.23), channel_id=1, source_target_pairs={{0,64},{1,65},{2,66},{3,67},{4,68},{5,69},{6,70},{7,71},{8,72},{9,... | collective-permute-start | bytes 387080 | tf_op jit(solution)/shard_map/ppermute | solution.py:45
  74.6 17.5 %collective-permute-start.4 = (f16[56,1152]{1,0:T(8,128)(2,1)S(1)}, f16[56,1152]{1,0:T(8,128)(2,1)S(1)}, u32[]{:S(2)}, u32[]{:S(2)}) collective-permute-start(f16[56,1152]{1,0:T(8,128)(2,1)S(1)} %get-tuple-element.24), channel_id=1, source_target_pairs={{0,32},{1,33},{2,34},{3,35},{4,36},{5,37},{6,38},{7,39},{8,40},{9,... | collective-permute-start | bytes 387080 | tf_op jit(solution)/shard_map/ppermute | solution.py:45
  81.4 17.3 %collective-permute-start.10 = (f16[56,1152]{1,0:T(8,128)(2,1)S(1)}, f16[56,1152]{1,0:T(8,128)(2,1)S(1)}, u32[]{:S(2)}, u32[]{:S(2)}) collective-permute-start(f16[56,1152]{1,0:T(8,128)(2,1)S(1)} %multiply_convert_fusion), channel_id=1, source_target_pairs={{0,28},{1,29},{2,30},{3,31},{4,24},{5,25},{6,26},{7,27},{8,20},{9,... | collective-permute-start | bytes 387080 | tf_op jit(solution)/shard_map/ppermute | solution.py:45

commit v5 on v4

--- a/solution.py
+++ b/solution.py
@@ -9,21 +9,19 @@
 
 AXES = ("dp", "pipe", "expert")
 NX, NY = 4, 4
-X_SCALE, Y_SCALE, Z_SCALE = 64.0, 32.0, 8.0
+SCALES = (64.0, 64.0, 32.0, 16.0, 8.0)
 VMEM_BYTES = 32 << 20
 
 
-def x_steps(expert):
-    first = 1 + 2 * (expert % 2)
-    return first, 4 - first
+X_1, X_3, Y_1, LAST = 1 * NY, 3 * NY, 1, 2
+ORDERS = (((X_3, Y_1, X_1), (Y_1, X_1, X_3)), ((X_1, Y_1, X_3), (X_3, X_1, Y_1)))
 
 
-def over_x(step):
-    return lambda dp, pipe, expert: (dp ^ x_steps(expert)[step] * NY, pipe, expert)
+def step(span, number):
+    def to(dp, pipe, expert):
+        return dp ^ (*ORDERS[span][expert % 2], LAST)[number], pipe, expert
 
-
-def over_y(bits):
-    return lambda dp, pipe, expert: (dp ^ bits, pipe, expert)
+    return to
 
 
 def mirrored(dp, pipe, expert):
@@ -68,22 +66,26 @@
     mine = grads[:, span].reshape(shards * slots, width)
     live = lax.broadcasted_iota(jnp.int32, mine.shape, 0) < counts[span]
     masked = jnp.where(live, mine.astype(jnp.float32), 0.0).astype(mine.dtype)
-    dp = lax.axis_index("dp")
+    dp, expert = lax.axis_index("dp"), lax.axis_index("expert")
     x, y = dp // NY, lax.rem(dp, NY)
-    first, _ = x_steps(lax.axis_index("expert"))
-    rows = part.shape[2]
+    core_0, core_1 = ([8 >> order.index(part) for part in (X_1, X_3, Y_1)] for order in ORDERS[span])
+    x_1, x_3, y_1 = (jnp.where(lax.rem(expert, 2) == 0, p, q) for p, q in zip(core_0, core_1))
+    x_places, y_places = [], []
+    for i in range(NX):
+        apart = jnp.bitwise_xor(i, x)
+        x_place = jnp.where((apart == 1) | (apart == 2), x_1, 0)
+        x_places.append(x_place + jnp.where((apart == 3) | (apart == 2), x_3, 0))
+        apart = jnp.bitwise_xor(i, y)
+        y_places.append(lax.rem(apart, 2) * y_1 + apart // 2)
+    rows = part.shape[1]
     for pair, columns in enumerate(pair_columns(acts.shape[-1])):
         fetches[pair].wait()
         product = transposed_dot(acts_here[:, columns], masked)
         for i in range(2):
-            apart = jnp.bitwise_xor(2 * pair + i, x)
-            slot = jnp.where(
-                apart == 0, 0, jnp.where(apart == 2, 3, jnp.where(apart == first, 2, 1))
-            )
             for j in range(NY):
                 start = (i * NY + j) * 2 * rows
                 halves = [product[start + k * rows : start + (k + 1) * rows] for k in range(2)]
-                part[slot, jnp.bitwise_xor(j, y)] = jnp.concatenate(halves, axis=1)
+                part[x_places[2 * pair + i] + y_places[j]] = jnp.concatenate(halves, axis=1)
 
 
 def in_hbm(array):
@@ -106,7 +108,7 @@
                 pltpu.SemaphoreType.DMA((NX // 2,)),
             ],
         ),
-        out_shape=jax.ShapeDtypeStruct((NX, NY, rows // (2 * NX * NY), 2 * width), jnp.float32),
+        out_shape=jax.ShapeDtypeStruct((NX * NY, rows // (2 * NX * NY), 2 * width), jnp.float32),
         compiler_params=pltpu.CompilerParams(vmem_limit_bytes=VMEM_BYTES),
         cost_estimate=cost(2 * slots * rows * width, 6 << 20),
     )(counts, in_hbm(activations), grads)
@@ -129,25 +131,23 @@
     grads = lax.all_gather(out_grads[0, 0], "expert")
 
     other = multiply_span(1, live, activations, grads)
-    other_out = narrow(other[2:], X_SCALE)
-    other_in = send(other_out, over_x(0))
+    other_out = narrow(other[8:], SCALES[0])
+    other_in = send(other_out, step(1, 0))
     own = multiply_span(0, live, activations, after(grads, other_out))
-    own_out = narrow(own[2:], X_SCALE)
-    own_in = send(own_out, over_x(0))
-    other_pass = narrow(after(other[1], own_out) + widen(other_in[1], X_SCALE), X_SCALE)
-    other_last = send(other_pass, over_x(1))
-    own_pass = narrow(after(own[1], other_pass) + widen(own_in[1], X_SCALE), X_SCALE)
-    own_last = send(own_pass, over_x(1))
+    own_out = narrow(own[8:], SCALES[0])
+    own_in = send(own_out, step(0, 0))
+    for number, kept in ((1, 8), (2, 4), (3, 2)):
+        scale = SCALES[number - 1]
+        other = after(other[:kept], own_out) + widen(other_in, scale)
+        other_out = narrow(other[kept // 2 :], SCALES[number])
+        other_in = send(other_out, step(1, number))
+        own = after(own[:kept], other_out) + widen(own_in, scale)
+        own_out = narrow(own[kept // 2 :], SCALES[number])
+        own_in = send(own_out, step(0, number))
 
-    other = after(other[0], own_pass) + widen(other_in[0], X_SCALE) + widen(other_last, X_SCALE)
-    other_out = [narrow(other[k], Y_SCALE) for k in range(1, NY)]
-    other_in = [send(block, over_y(k)) for k, block in enumerate(other_out, 1)]
-    own = after(own[0], *other_out) + widen(own_in[0], X_SCALE) + widen(own_last, X_SCALE)
-    own_out = [narrow(own[k], Y_SCALE) for k in range(1, NY)]
-    own_in = [send(block, over_y(k)) for k, block in enumerate(own_out, 1)]
-    other = after(other[0], *own_out) + sum(widen(block, Y_SCALE) for block in other_in)
-    from_mirror = send(narrow(other, Z_SCALE), mirrored)
-    grad = own[0] + sum(widen(block, Y_SCALE) for block in own_in) + widen(from_mirror, Z_SCALE)
+    other = after(other[:1], own_out) + widen(other_in, SCALES[3])
+    from_mirror = send(narrow(other, SCALES[4]), mirrored)
+    grad = (own[:1] + widen(own_in, SCALES[3]) + widen(from_mirror, SCALES[4]))[0]
     width = out_grads.shape[-1]
     grad = jnp.concatenate([grad[:, :width], grad[:, width:]])[None, None]
     new_first = 0.9 * first_moment + 0.1 * grad

time: 100 us -> 96.7 us (0.967)
  the two profiles are of different devices: /device:TPU:61 before, /device:TPU:6 now
where the time goes in v5:
time: 96.7 us; the launch traced here: 95.6 us
  starting transfers between devices  43.8 us (45%)
  waiting for transfers between devices  23.9 us (25%)
  blocking collectives  16.5 us (17%)
  Pallas kernels  7.5 us (8%)
  other arithmetic  2.97 us (3%)
    ppermute x9, starting transfers between devices, send(): return lax.ppermute(block, AXES, pairs)  43.8 us
    ppermute x9, waiting for transfers between devices, send(): return lax.ppermute(block, AXES, pairs)  23.9 us
    all_gather x1, blocking collectives, local(): grads = lax.all_gather(out_grads[0, 0], 'expert')  16.5 us
    pallas_call x2, Pallas kernels, multiply_span(): pl.pallas_call(functools.partial(span_kernel, span), grid_spec=pltpu.Pref...  7.5 us
  transfers between devices with their start and end apart: 9, of which 6 were waited for; matrix products, arithmetic and copies ran while one was open for 2% of the time, Pallas kernels for 4%

profile of v5, /device:TPU:6, one launch (start us, length us, event | category | flops | bytes accessed | tf_op | source)
XLA Modules:
  0.0 95.6 jit_solution(16036811124130694761)
XLA Ops:
  0.6 16.5 %all-gather = bf16[4,1,2,96,576]{4,3,2,1,0:T(8,128)(2,1)S(1)} all-gather(bf16[1,1,2,96,576]{4,3,2,1,0:T(8,128)(2,1)} %param.6), channel_id=2, replica_groups=mesh['dp'=16,'pipe'=8,'expert'=4] {'expert'}, dimensions={0}, use_global_device_ids=true | all-gather | bytes 1105920 | tf_op jit(solution)/shard_map/all_gather | solution.py:131
  17.1 3.7 %shard_map.76 = f32[16,56,1152]{2,1,0:T(8,128)S(1)} custom-call(s32[2]{0:T(128)} %bitcast.10, bf16[1,1,2,384,1792]{4,3,2,1,0:T(8,128)(2,1)} %acts.3, bf16[4,2,96,576]{3,2,1,0:T(8,128)(2,1)S(1)} %bitcast.8), custom_call_target="tpu_custom_call" | custom-call | flops 792723456 | bytes 6291456 | tf_op jit(solution)/shard_map/pallas_call | solution.py:99
  20.9 0.2 fusion.12
  21.1 2.7 %collective-permute-start = (f16[8,56,1152]{2,1,0:T(8,128)(2,1)S(1)}, f16[8,56,1152]{2,1,0:T(8,128)(2,1)S(1)}, u32[]{:S(2)}, u32[]{:S(2)}) collective-permute-start(f16[8,56,1152]{2,1,0:T(8,128)(2,1)S(1)} %get-tuple-element.25), channel_id=1, source_target_pairs={{0,128},{1,385},{2,130},{3,387},{4,132},{5,389},{6,134},{7,391},{8... | collective-permute-start | bytes 3096584 | tf_op jit(solution)/shard_map/ppermute | solution.py:43
  23.9 3.8 %shard_map.77 = f32[16,56,1152]{2,1,0:T(8,128)S(1)} custom-call(s32[2]{0:T(128)} %bitcast.11, bf16[1,1,2,384,1792]{4,3,2,1,0:T(8,128)(2,1)} %acts.3, bf16[4,2,96,576]{3,2,1,0:T(8,128)(2,1)S(1)} %bitcast.9), custom_call_target="tpu_custom_call" | custom-call | flops 792723456 | bytes 6291456 | tf_op jit(solution)/shard_map/pallas_call | solution.py:99
  27.6 0.2 fusion
  27.9 5.5 %collective-permute-start.1 = (f16[8,56,1152]{2,1,0:T(8,128)(2,1)S(1)}, f16[8,56,1152]{2,1,0:T(8,128)(2,1)S(1)}, u32[]{:S(2)}, u32[]{:S(2)}) collective-permute-start(f16[8,56,1152]{2,1,0:T(8,128)(2,1)S(1)} %get-tuple-element.22), channel_id=1, source_target_pairs={{0,384},{1,33},{2,386},{3,35},{4,388},{5,37},{6,390},{7,39},{8,392... | collective-permute-start | bytes 3096584 | tf_op jit(solution)/shard_map/ppermute | solution.py:43
  33.4 4.2 %collective-permute-done = f16[8,56,1152]{2,1,0:T(8,128)(2,1)S(1)} collective-permute-done((f16[8,56,1152]{2,1,0:T(8,128)(2,1)S(1)}, f16[8,56,1152]{2,1,0:T(8,128)(2,1)S(1)}, u32[]{:S(2)}, u32[]{:S(2)}) %collective-permute-start) | collective-permute-done | bytes 1032224 | tf_op jit(solution)/shard_map/ppermute | solution.py:43
  37.6 0.2 multiply_add_fusion.1
  37.9 0.1 fusion.13
  38.0 5.6 %collective-permute-start.2 = (f16[4,56,1152]{2,1,0:T(8,128)(2,1)S(1)}, f16[4,56,1152]{2,1,0:T(8,128)(2,1)S(1)}, u32[]{:S(2)}, u32[]{:S(2)}) collective-permute-start(f16[4,56,1152]{2,1,0:T(8,128)(2,1)S(1)} %get-tuple-element.29), channel_id=1, source_target_pairs={{0,32},{1,129},{2,34},{3,131},{4,36},{5,133},{6,38},{7,135},{8,40}... | collective-permute-start | bytes 1548296 | tf_op jit(solution)/shard_map/ppermute | solution.py:43
  43.6 7.1 %collective-permute-done.1 = f16[8,56,1152]{2,1,0:T(8,128)(2,1)S(1)} collective-permute-done((f16[8,56,1152]{2,1,0:T(8,128)(2,1)S(1)}, f16[8,56,1152]{2,1,0:T(8,128)(2,1)S(1)}, u32[]{:S(2)}, u32[]{:S(2)}) %collective-permute-start.1) | collective-permute-done | bytes 1032224 | tf_op jit(solution)/shard_map/ppermute | solution.py:43
  50.8 0.3 multiply_add_fusion
  51.1 0.1 fusion.2
  51.2 4.1 %collective-permute-start.3 = (f16[4,56,1152]{2,1,0:T(8,128)(2,1)S(1)}, f16[4,56,1152]{2,1,0:T(8,128)(2,1)S(1)}, u32[]{:S(2)}, u32[]{:S(2)}) collective-permute-start(f16[4,56,1152]{2,1,0:T(8,128)(2,1)S(1)} %get-tuple-element.26), channel_id=1, source_target_pairs={{0,32},{1,129},{2,34},{3,131},{4,36},{5,133},{6,38},{7,135},{8,40}... | collective-permute-start | bytes 1548296 | tf_op jit(solution)/shard_map/ppermute | solution.py:43
  55.3 0.0 collective-permute-done.2
  55.3 0.1 multiply_add_fusion.3
  55.5 0.1 fusion.14
  55.6 2.6 %collective-permute-start.4 = (f16[2,56,1152]{2,1,0:T(8,128)(2,1)S(1)}, f16[2,56,1152]{2,1,0:T(8,128)(2,1)S(1)}, u32[]{:S(2)}, u32[]{:S(2)}) collective-permute-start(f16[2,56,1152]{2,1,0:T(8,128)(2,1)S(1)} %get-tuple-element.33), channel_id=1, source_target_pairs={{0,384},{1,33},{2,386},{3,35},{4,388},{5,37},{6,390},{7,39},{8,392... | collective-permute-start | bytes 774152 | tf_op jit(solution)/shard_map/ppermute | solution.py:43
  58.2 7.0 %collective-permute-done.3 = f16[4,56,1152]{2,1,0:T(8,128)(2,1)S(1)} collective-permute-done((f16[4,56,1152]{2,1,0:T(8,128)(2,1)S(1)}, f16[4,56,1152]{2,1,0:T(8,128)(2,1)S(1)}, u32[]{:S(2)}, u32[]{:S(2)}) %collective-permute-start.3) | collective-permute-done | bytes 516128 | tf_op jit(solution)/shard_map/ppermute | solution.py:43
  65.2 0.1 multiply_add_fusion.2
  65.3 0.1 fusion.4
  65.4 1.9 %collective-permute-start.5 = (f16[2,56,1152]{2,1,0:T(8,128)(2,1)S(1)}, f16[2,56,1152]{2,1,0:T(8,128)(2,1)S(1)}, u32[]{:S(2)}, u32[]{:S(2)}) collective-permute-start(f16[2,56,1152]{2,1,0:T(8,128)(2,1)S(1)} %get-tuple-element.30), channel_id=1, source_target_pairs={{0,128},{1,385},{2,130},{3,387},{4,132},{5,389},{6,134},{7,391},{8... | collective-permute-start | bytes 774152 | tf_op jit(solution)/shard_map/ppermute | solution.py:43
  67.3 0.0 collective-permute-done.4
  67.3 0.1 multiply_add_fusion.5
  67.4 0.0 copy-start
  67.4 0.0 copy-start.1
  67.5 5.2 %collective-permute-start.7 = (f16[1,56,1152]{2,1,0:T(8,128)(2,1)S(1)}, f16[1,56,1152]{2,1,0:T(8,128)(2,1)S(1)}, u32[]{:S(2)}, u32[]{:S(2)}) collective-permute-start(f16[1,56,1152]{2,1,0:T(8,128)(2,1)S(1)} %get-tuple-element.35), channel_id=1, source_target_pairs={{0,64},{1,65},{2,66},{3,67},{4,68},{5,69},{6,70},{7,71},{8,72},{9,... | collective-permute-start | bytes 387080 | tf_op jit(solution)/shard_map/ppermute | solution.py:43
  72.7 0.9 collective-permute-done.5
  73.6 0.1 multiply_add_fusion.4
  73.7 5.1 %collective-permute-start.6 = (f16[1,56,1152]{2,1,0:T(8,128)(2,1)S(1)}, f16[1,56,1152]{2,1,0:T(8,128)(2,1)S(1)}, u32[]{:S(2)}, u32[]{:S(2)}) collective-permute-start(f16[1,56,1152]{2,1,0:T(8,128)(2,1)S(1)} %fusion.7), channel_id=1, source_target_pairs={{0,64},{1,65},{2,66},{3,67},{4,68},{5,69},{6,70},{7,71},{8,72},{9,... | collective-permute-start | bytes 387080 | tf_op jit(solution)/shard_map/ppermute | solution.py:43
  78.8 0.3 collective-permute-done.7
  79.1 0.1 multiply_convert_fusion
  79.2 10.9 %collective-permute-start.8 = (f16[1,56,1152]{2,1,0:T(8,128)(2,1)S(1)}, f16[1,56,1152]{2,1,0:T(8,128)(2,1)S(1)}, u32[]{:S(2)}, u32[]{:S(2)}) collective-permute-start(f16[1,56,1152]{2,1,0:T(8,128)(2,1)S(1)} %multiply_convert_fusion), channel_id=1, source_target_pairs={{0,28},{1,29},{2,30},{3,31},{4,24},{5,25},{6,26},{7,27},{8,20},{9,... | collective-permute-start | bytes 387080 | tf_op jit(solution)/shard_map/ppermute | solution.py:43
  90.1 0.0 collective-permute-done.6
  90.1 4.3 %collective-permute-done.8 = f16[1,56,1152]{2,1,0:T(8,128)(2,1)S(1)} collective-permute-done((f16[1,56,1152]{2,1,0:T(8,128)(2,1)S(1)}, f16[1,56,1152]{2,1,0:T(8,128)(2,1)S(1)}, u32[]{:S(2)}, u32[]{:S(2)}) %collective-permute-start.8) | collective-permute-done | bytes 129056 | tf_op jit(solution)/shard_map/ppermute | solution.py:43
  94.4 0.1 fusion.9
  94.5 0.1 slice_bitcast_fusion.1
  94.6 0.0 copy-done
  94.6 0.0 copy-done.1
  94.6 1.0 %add_divide_fusion = (f32[1,1,112,576]{3,2,1,0:T(8,128)}, f32[1,1,112,576]{3,2,1,0:T(8,128)}, f32[1,1,112,576]{3,2,1,0:T(8,128)}) fusion(f32[1,1,56,576]{3,2,1,0:T(8,128)S(1)} %get-tuple-element.37, f32[1,1,56,576]{3,2,1,0:T(8,128)S(1)} %get-tuple-element.36, f32[1,1,112,576]{3,2,1,0:T(8,128)S(1)} %copy-done, f32[1,1,112,576]{3,2,1,0:T(8,128)S(1)} %copy-done.1), kind=kLoop, calls=%fused_computation.21 | loop fusion | flops 645120 | bytes 1548288 | tf_op jit(solution)/shard_map/div | solution.py:155
  (2 shorter events, 0.1 us)
Async XLA Ops:
  21.1 16.5 %collective-permute-start = (f16[8,56,1152]{2,1,0:T(8,128)(2,1)S(1)}, f16[8,56,1152]{2,1,0:T(8,128)(2,1)S(1)}, u32[]{:S(2)}, u32[]{:S(2)}) collective-permute-start(f16[8,56,1152]{2,1,0:T(8,128)(2,1)S(1)} %get-tuple-element.25), channel_id=1, source_target_pairs={{0,128},{1,385},{2,130},{3,387},{4,132},{5,389},{6,134},{7,391},{8... | collective-permute-start | bytes 3096584 | tf_op jit(solution)/shard_map/ppermute | solution.py:43
  27.9 22.9 %collective-permute-start.1 = (f16[8,56,1152]{2,1,0:T(8,128)(2,1)S(1)}, f16[8,56,1152]{2,1,0:T(8,128)(2,1)S(1)}, u32[]{:S(2)}, u32[]{:S(2)}) collective-permute-start(f16[8,56,1152]{2,1,0:T(8,128)(2,1)S(1)} %get-tuple-element.22), channel_id=1, source_target_pairs={{0,384},{1,33},{2,386},{3,35},{4,388},{5,37},{6,390},{7,39},{8,392... | collective-permute-start | bytes 3096584 | tf_op jit(solution)/shard_map/ppermute | solution.py:43
  38.0 17.3 %collective-permute-start.2 = (f16[4,56,1152]{2,1,0:T(8,128)(2,1)S(1)}, f16[4,56,1152]{2,1,0:T(8,128)(2,1)S(1)}, u32[]{:S(2)}, u32[]{:S(2)}) collective-permute-start(f16[4,56,1152]{2,1,0:T(8,128)(2,1)S(1)} %get-tuple-element.29), channel_id=1, source_target_pairs={{0,32},{1,129},{2,34},{3,131},{4,36},{5,133},{6,38},{7,135},{8,40}... | collective-permute-start | bytes 1548296 | tf_op jit(solution)/shard_map/ppermute | solution.py:43
  51.2 14.0 %collective-permute-start.3 = (f16[4,56,1152]{2,1,0:T(8,128)(2,1)S(1)}, f16[4,56,1152]{2,1,0:T(8,128)(2,1)S(1)}, u32[]{:S(2)}, u32[]{:S(2)}) collective-permute-start(f16[4,56,1152]{2,1,0:T(8,128)(2,1)S(1)} %get-tuple-element.26), channel_id=1, source_target_pairs={{0,32},{1,129},{2,34},{3,131},{4,36},{5,133},{6,38},{7,135},{8,40}... | collective-permute-start | bytes 1548296 | tf_op jit(solution)/shard_map/ppermute | solution.py:43
  55.6 11.8 %collective-permute-start.4 = (f16[2,56,1152]{2,1,0:T(8,128)(2,1)S(1)}, f16[2,56,1152]{2,1,0:T(8,128)(2,1)S(1)}, u32[]{:S(2)}, u32[]{:S(2)}) collective-permute-start(f16[2,56,1152]{2,1,0:T(8,128)(2,1)S(1)} %get-tuple-element.33), channel_id=1, source_target_pairs={{0,384},{1,33},{2,386},{3,35},{4,388},{5,37},{6,390},{7,39},{8,392... | collective-permute-start | bytes 774152 | tf_op jit(solution)/shard_map/ppermute | solution.py:43
  65.4 8.2 %collective-permute-start.5 = (f16[2,56,1152]{2,1,0:T(8,128)(2,1)S(1)}, f16[2,56,1152]{2,1,0:T(8,128)(2,1)S(1)}, u32[]{:S(2)}, u32[]{:S(2)}) collective-permute-start(f16[2,56,1152]{2,1,0:T(8,128)(2,1)S(1)} %get-tuple-element.30), channel_id=1, source_target_pairs={{0,128},{1,385},{2,130},{3,387},{4,132},{5,389},{6,134},{7,391},{8... | collective-permute-start | bytes 774152 | tf_op jit(solution)/shard_map/ppermute | solution.py:43
  67.4 27.2 %copy-start = (f32[1,1,112,576]{3,2,1,0:T(8,128)S(1)}, f32[1,1,112,576]{3,2,1,0:T(8,128)}, u32[]{:S(2)}) copy-start(f32[1,1,112,576]{3,2,1,0:T(8,128)} %param.9) | copy-start | bytes 774148
  67.4 27.2 %copy-start.1 = (f32[1,1,112,576]{3,2,1,0:T(8,128)S(1)}, f32[1,1,112,576]{3,2,1,0:T(8,128)}, u32[]{:S(2)}) copy-start(f32[1,1,112,576]{3,2,1,0:T(8,128)} %param.8) | copy-start | bytes 774148
  67.5 11.7 %collective-permute-start.7 = (f16[1,56,1152]{2,1,0:T(8,128)(2,1)S(1)}, f16[1,56,1152]{2,1,0:T(8,128)(2,1)S(1)}, u32[]{:S(2)}, u32[]{:S(2)}) collective-permute-start(f16[1,56,1152]{2,1,0:T(8,128)(2,1)S(1)} %get-tuple-element.35), channel_id=1, source_target_pairs={{0,64},{1,65},{2,66},{3,67},{4,68},{5,69},{6,70},{7,71},{8,72},{9,... | collective-permute-start | bytes 387080 | tf_op jit(solution)/shard_map/ppermute | solution.py:43
  73.7 16.4 %collective-permute-start.6 = (f16[1,56,1152]{2,1,0:T(8,128)(2,1)S(1)}, f16[1,56,1152]{2,1,0:T(8,128)(2,1)S(1)}, u32[]{:S(2)}, u32[]{:S(2)}) collective-permute-start(f16[1,56,1152]{2,1,0:T(8,128)(2,1)S(1)} %fusion.7), channel_id=1, source_target_pairs={{0,64},{1,65},{2,66},{3,67},{4,68},{5,69},{6,70},{7,71},{8,72},{9,... | collective-permute-start | bytes 387080 | tf_op jit(solution)/shard_map/ppermute | solution.py:43
  79.2 15.2 %collective-permute-start.8 = (f16[1,56,1152]{2,1,0:T(8,128)(2,1)S(1)}, f16[1,56,1152]{2,1,0:T(8,128)(2,1)S(1)}, u32[]{:S(2)}, u32[]{:S(2)}) collective-permute-start(f16[1,56,1152]{2,1,0:T(8,128)(2,1)S(1)} %multiply_convert_fusion), channel_id=1, source_target_pairs={{0,28},{1,29},{2,30},{3,31},{4,24},{5,25},{6,26},{7,27},{8,20},{9,... | collective-permute-start | bytes 387080 | tf_op jit(solution)/shard_map/ppermute | solution.py:43

commit v6 on v5

--- a/solution.py
+++ b/solution.py
@@ -13,13 +13,18 @@
 VMEM_BYTES = 32 << 20
 
 
-X_1, X_3, Y_1, LAST = 1 * NY, 3 * NY, 1, 2
-ORDERS = (((X_3, Y_1, X_1), (Y_1, X_1, X_3)), ((X_1, Y_1, X_3), (X_3, X_1, Y_1)))
+X_1, X_3, Y_1, Y_2 = 1 * NY, 3 * NY, 1, 2
+ORDERS = (
+    ((X_3, X_1, Y_1, Y_2), (Y_1, X_3, X_1, Y_2)),
+    ((X_1, Y_1, X_3, Y_2), (X_3, X_1, Y_1, Y_2)),
+)
 
 
-def step(span, number):
+def step(span, *numbers):
     def to(dp, pipe, expert):
-        return dp ^ (*ORDERS[span][expert % 2], LAST)[number], pipe, expert
+        for number in numbers:
+            dp ^= ORDERS[span][expert % 2][number]
+        return dp, pipe, expert
 
     return to
 
@@ -68,15 +73,16 @@
     masked = jnp.where(live, mine.astype(jnp.float32), 0.0).astype(mine.dtype)
     dp, expert = lax.axis_index("dp"), lax.axis_index("expert")
     x, y = dp // NY, lax.rem(dp, NY)
-    core_0, core_1 = ([8 >> order.index(part) for part in (X_1, X_3, Y_1)] for order in ORDERS[span])
-    x_1, x_3, y_1 = (jnp.where(lax.rem(expert, 2) == 0, p, q) for p, q in zip(core_0, core_1))
+    places = ([8 >> order.index(part) for part in (X_1, X_3, Y_1, Y_2)] for order in ORDERS[span])
+    is_0 = lax.rem(expert, 2) == 0
+    x_1, x_3, y_1, y_2 = (jnp.where(is_0, p, q) for p, q in zip(*places))
     x_places, y_places = [], []
     for i in range(NX):
         apart = jnp.bitwise_xor(i, x)
         x_place = jnp.where((apart == 1) | (apart == 2), x_1, 0)
         x_places.append(x_place + jnp.where((apart == 3) | (apart == 2), x_3, 0))
         apart = jnp.bitwise_xor(i, y)
-        y_places.append(lax.rem(apart, 2) * y_1 + apart // 2)
+        y_places.append(lax.rem(apart, 2) * y_1 + apart // 2 * y_2)
     rows = part.shape[1]
     for pair, columns in enumerate(pair_columns(acts.shape[-1])):
         fetches[pair].wait()
@@ -130,24 +136,35 @@
     live = in_hbm(counts[0, 0])
     grads = lax.all_gather(out_grads[0, 0], "expert")
 
+    def direct(part, span, *earlier):
+        part = after(part, *earlier)
+        out = [narrow(part[k], SCALES[2]) for k in (1, 2, 3)]
+        partners = (3,), (2,), (2, 3)
+        return out, part[0], [send(block, step(span, *to)) for block, to in zip(out, partners)]
+
+    def total(kept, blocks):
+        return kept + sum(widen(block, SCALES[2]) for block in blocks)
+
     other = multiply_span(1, live, activations, grads)
     other_out = narrow(other[8:], SCALES[0])
     other_in = send(other_out, step(1, 0))
     own = multiply_span(0, live, activations, after(grads, other_out))
     own_out = narrow(own[8:], SCALES[0])
     own_in = send(own_out, step(0, 0))
-    for number, kept in ((1, 8), (2, 4), (3, 2)):
-        scale = SCALES[number - 1]
-        other = after(other[:kept], own_out) + widen(other_in, scale)
-        other_out = narrow(other[kept // 2 :], SCALES[number])
-        other_in = send(other_out, step(1, number))
-        own = after(own[:kept], other_out) + widen(own_in, scale)
-        own_out = narrow(own[kept // 2 :], SCALES[number])
-        own_in = send(own_out, step(0, number))
+    other = after(other[:8], own_out) + widen(other_in, SCALES[0])
+    other_out = narrow(other[4:], SCALES[1])
+    other_in = send(other_out, step(1, 1))
+    own = after(own[:8], other_out) + widen(own_in, SCALES[0])
+    own_out = narrow(own[4:], SCALES[1])
+    own_in = send(own_out, step(0, 1))
+    other = after(other[:4], own_out) + widen(other_in, SCALES[1])
+    other_out, other, other_in = direct(other, 1)
+    own = after(own[:4], *other_out) + widen(own_in, SCALES[1])
+    own_out, own, own_in = direct(own, 0)
 
-    other = after(other[:1], own_out) + widen(other_in, SCALES[3])
+    other = total(after(other, *own_out), other_in)
     from_mirror = send(narrow(other, SCALES[4]), mirrored)
-    grad = (own[:1] + widen(own_in, SCALES[3]) + widen(from_mirror, SCALES[4]))[0]
+    grad = total(own, own_in) + widen(from_mirror, SCALES[4])
     width = out_grads.shape[-1]
     grad = jnp.concatenate([grad[:, :width], grad[:, width:]])[None, None]
     new_first = 0.9 * first_moment + 0.1 * grad

time: 96.7 us -> 93.4 us (0.966)
  waiting for transfers between devices: 23.9 us -> 16.3 us
  starting transfers between devices: 43.8 us -> 48.8 us
    ppermute x9 -> x11, waiting for transfers between devices: 23.9 us -> 16.3 us  [send(): return lax.ppermute(block, AXES, pairs)]
    ppermute x9 -> x11, starting transfers between devices: 43.8 us -> 48.8 us  [send(): return lax.ppermute(block, AXES, pairs)]
  transfers between devices with their start and end apart: 9 -> 11, of which waited for: 6 -> 4; matrix products, arithmetic and copies ran while one was open for 2% -> 2% of each run, Pallas kernels for 4% -> 4%
where the time goes in v6:
time: 93.4 us; the launch traced here: 92.9 us
  starting transfers between devices  48.8 us (52%)
  blocking collectives  16.5 us (18%)
  waiting for transfers between devices  16.3 us (17%)
  Pallas kernels  7.5 us (8%)
  other arithmetic  2.84 us (3%)
    ppermute x11, starting transfers between devices, send(): return lax.ppermute(block, AXES, pairs)  48.8 us
    all_gather x1, blocking collectives, local(): grads = lax.all_gather(out_grads[0, 0], 'expert')  16.5 us
    ppermute x11, waiting for transfers between devices, send(): return lax.ppermute(block, AXES, pairs)  16.3 us
    pallas_call x2, Pallas kernels, multiply_span(): pl.pallas_call(functools.partial(span_kernel, span), grid_spec=pltpu.Pref...  7.5 us
  transfers between devices with their start and end apart: 11, of which 4 were waited for; matrix products, arithmetic and copies ran while one was open for 2% of the time, Pallas kernels for 4%

profile of v6, /device:TPU:6, one launch (start us, length us, event | category | flops | bytes accessed | tf_op | source)
XLA Modules:
  0.0 92.9 jit_solution(17642474396377228393)
XLA Ops:
  0.6 16.5 %all-gather = bf16[4,1,2,96,576]{4,3,2,1,0:T(8,128)(2,1)S(1)} all-gather(bf16[1,1,2,96,576]{4,3,2,1,0:T(8,128)(2,1)} %param.6), channel_id=2, replica_groups=mesh['dp'=16,'pipe'=8,'expert'=4] {'expert'}, dimensions={0}, use_global_device_ids=true | all-gather | bytes 1105920 | tf_op jit(solution)/shard_map/all_gather | solution.py:137
  17.1 3.7 %shard_map.76 = f32[16,56,1152]{2,1,0:T(8,128)S(1)} custom-call(s32[2]{0:T(128)} %bitcast.28, bf16[1,1,2,384,1792]{4,3,2,1,0:T(8,128)(2,1)} %acts.3, bf16[4,2,96,576]{3,2,1,0:T(8,128)(2,1)S(1)} %bitcast.26), custom_call_target="tpu_custom_call" | custom-call | flops 792723456 | bytes 6291456 | tf_op jit(solution)/shard_map/pallas_call | solution.py:105
  20.9 0.2 fusion.20
  21.1 2.7 %collective-permute-start = (f16[8,56,1152]{2,1,0:T(8,128)(2,1)S(1)}, f16[8,56,1152]{2,1,0:T(8,128)(2,1)S(1)}, u32[]{:S(2)}, u32[]{:S(2)}) collective-permute-start(f16[8,56,1152]{2,1,0:T(8,128)(2,1)S(1)} %get-tuple-element.21), channel_id=1, source_target_pairs={{0,128},{1,385},{2,130},{3,387},{4,132},{5,389},{6,134},{7,391},{8... | collective-permute-start | bytes 3096584 | tf_op jit(solution)/shard_map/ppermute | solution.py:48
  23.9 3.8 %shard_map.77 = f32[16,56,1152]{2,1,0:T(8,128)S(1)} custom-call(s32[2]{0:T(128)} %bitcast.29, bf16[1,1,2,384,1792]{4,3,2,1,0:T(8,128)(2,1)} %acts.3, bf16[4,2,96,576]{3,2,1,0:T(8,128)(2,1)S(1)} %bitcast.27), custom_call_target="tpu_custom_call" | custom-call | flops 792723456 | bytes 6291456 | tf_op jit(solution)/shard_map/pallas_call | solution.py:105
  27.6 0.2 fusion
  27.9 5.5 %collective-permute-start.1 = (f16[8,56,1152]{2,1,0:T(8,128)(2,1)S(1)}, f16[8,56,1152]{2,1,0:T(8,128)(2,1)S(1)}, u32[]{:S(2)}, u32[]{:S(2)}) collective-permute-start(f16[8,56,1152]{2,1,0:T(8,128)(2,1)S(1)} %get-tuple-element.18), channel_id=1, source_target_pairs={{0,384},{1,33},{2,386},{3,35},{4,388},{5,37},{6,390},{7,39},{8,392... | collective-permute-start | bytes 3096584 | tf_op jit(solution)/shard_map/ppermute | solution.py:48
  33.4 4.2 %collective-permute-done = f16[8,56,1152]{2,1,0:T(8,128)(2,1)S(1)} collective-permute-done((f16[8,56,1152]{2,1,0:T(8,128)(2,1)S(1)}, f16[8,56,1152]{2,1,0:T(8,128)(2,1)S(1)}, u32[]{:S(2)}, u32[]{:S(2)}) %collective-permute-start) | collective-permute-done | bytes 1032224 | tf_op jit(solution)/shard_map/ppermute | solution.py:48
  37.6 0.2 multiply_add_fusion.1
  37.9 0.1 fusion.21
  38.0 5.6 %collective-permute-start.2 = (f16[4,56,1152]{2,1,0:T(8,128)(2,1)S(1)}, f16[4,56,1152]{2,1,0:T(8,128)(2,1)S(1)}, u32[]{:S(2)}, u32[]{:S(2)}) collective-permute-start(f16[4,56,1152]{2,1,0:T(8,128)(2,1)S(1)} %get-tuple-element.25), channel_id=1, source_target_pairs={{0,32},{1,129},{2,34},{3,131},{4,36},{5,133},{6,38},{7,135},{8,40}... | collective-permute-start | bytes 1548296 | tf_op jit(solution)/shard_map/ppermute | solution.py:48
  43.6 7.1 %collective-permute-done.1 = f16[8,56,1152]{2,1,0:T(8,128)(2,1)S(1)} collective-permute-done((f16[8,56,1152]{2,1,0:T(8,128)(2,1)S(1)}, f16[8,56,1152]{2,1,0:T(8,128)(2,1)S(1)}, u32[]{:S(2)}, u32[]{:S(2)}) %collective-permute-start.1) | collective-permute-done | bytes 1032224 | tf_op jit(solution)/shard_map/ppermute | solution.py:48
  50.8 0.3 multiply_add_fusion
  51.1 0.1 fusion.2
  51.2 1.9 %collective-permute-start.3 = (f16[4,56,1152]{2,1,0:T(8,128)(2,1)S(1)}, f16[4,56,1152]{2,1,0:T(8,128)(2,1)S(1)}, u32[]{:S(2)}, u32[]{:S(2)}) collective-permute-start(f16[4,56,1152]{2,1,0:T(8,128)(2,1)S(1)} %get-tuple-element.22), channel_id=1, source_target_pairs={{0,128},{1,385},{2,130},{3,387},{4,132},{5,389},{6,134},{7,391},{8... | collective-permute-start | bytes 1548296 | tf_op jit(solution)/shard_map/ppermute | solution.py:48
  53.1 0.0 collective-permute-done.2
  53.1 0.1 multiply_add_fusion.3
  53.3 0.1 slice_bitcast_fusion
  53.3 5.5 %collective-permute-start.9 = (f16[56,1152]{1,0:T(8,128)(2,1)S(1)}, f16[56,1152]{1,0:T(8,128)(2,1)S(1)}, u32[]{:S(2)}, u32[]{:S(2)}) collective-permute-start(f16[56,1152]{1,0:T(8,128)(2,1)S(1)} %get-tuple-element.30), channel_id=1, source_target_pairs={{0,448},{1,97},{2,450},{3,99},{4,452},{5,101},{6,454},{7,103},{8,4... | collective-permute-start | bytes 387080 | tf_op jit(solution)/shard_map/ppermute | solution.py:48
  58.8 4.4 %collective-permute-start.8 = (f16[56,1152]{1,0:T(8,128)(2,1)S(1)}, f16[56,1152]{1,0:T(8,128)(2,1)S(1)}, u32[]{:S(2)}, u32[]{:S(2)}) collective-permute-start(f16[56,1152]{1,0:T(8,128)(2,1)S(1)} %get-tuple-element.31), channel_id=1, source_target_pairs={{0,384},{1,33},{2,386},{3,35},{4,388},{5,37},{6,390},{7,39},{8,392... | collective-permute-start | bytes 387080 | tf_op jit(solution)/shard_map/ppermute | solution.py:48
  63.2 1.9 %collective-permute-start.7 = (f16[56,1152]{1,0:T(8,128)(2,1)S(1)}, f16[56,1152]{1,0:T(8,128)(2,1)S(1)}, u32[]{:S(2)}, u32[]{:S(2)}) collective-permute-start(f16[56,1152]{1,0:T(8,128)(2,1)S(1)} %get-tuple-element.32), channel_id=1, source_target_pairs={{0,64},{1,65},{2,66},{3,67},{4,68},{5,69},{6,70},{7,71},{8,72},{9,... | collective-permute-start | bytes 387080 | tf_op jit(solution)/shard_map/ppermute | solution.py:48
  65.2 0.0 collective-permute-done.3
  65.2 0.1 multiply_add_fusion.2
  65.3 0.0 copy-start
  65.3 0.0 copy-start.1
  65.3 0.1 fusion.18
  65.4 5.5 %collective-permute-start.6 = (f16[56,1152]{1,0:T(8,128)(2,1)S(1)}, f16[56,1152]{1,0:T(8,128)(2,1)S(1)}, u32[]{:S(2)}, u32[]{:S(2)}) collective-permute-start(f16[56,1152]{1,0:T(8,128)(2,1)S(1)} %get-tuple-element.26), channel_id=1, source_target_pairs={{0,96},{1,193},{2,98},{3,195},{4,100},{5,197},{6,102},{7,199},{8,1... | collective-permute-start | bytes 387080 | tf_op jit(solution)/shard_map/ppermute | solution.py:48
  70.9 2.0 %collective-permute-start.5 = (f16[56,1152]{1,0:T(8,128)(2,1)S(1)}, f16[56,1152]{1,0:T(8,128)(2,1)S(1)}, u32[]{:S(2)}, u32[]{:S(2)}) collective-permute-start(f16[56,1152]{1,0:T(8,128)(2,1)S(1)} %get-tuple-element.27), channel_id=1, source_target_pairs={{0,32},{1,129},{2,34},{3,131},{4,36},{5,133},{6,38},{7,135},{8,40}... | collective-permute-start | bytes 387080 | tf_op jit(solution)/shard_map/ppermute | solution.py:48
  72.9 0.0 collective-permute-done.9
  72.9 2.8 %collective-permute-start.4 = (f16[56,1152]{1,0:T(8,128)(2,1)S(1)}, f16[56,1152]{1,0:T(8,128)(2,1)S(1)}, u32[]{:S(2)}, u32[]{:S(2)}) collective-permute-start(f16[56,1152]{1,0:T(8,128)(2,1)S(1)} %get-tuple-element.28), channel_id=1, source_target_pairs={{0,64},{1,65},{2,66},{3,67},{4,68},{5,69},{6,70},{7,71},{8,72},{9,... | collective-permute-start | bytes 387080 | tf_op jit(solution)/shard_map/ppermute | solution.py:48
  75.7 0.0 collective-permute-done.8
  75.7 0.6 collective-permute-done.7
  76.3 0.1 multiply_convert_fusion
  76.4 11.0 %collective-permute-start.10 = (f16[56,1152]{1,0:T(8,128)(2,1)S(1)}, f16[56,1152]{1,0:T(8,128)(2,1)S(1)}, u32[]{:S(2)}, u32[]{:S(2)}) collective-permute-start(f16[56,1152]{1,0:T(8,128)(2,1)S(1)} %multiply_convert_fusion), channel_id=1, source_target_pairs={{0,28},{1,29},{2,30},{3,31},{4,24},{5,25},{6,26},{7,27},{8,20},{9,... | collective-permute-start | bytes 387080 | tf_op jit(solution)/shard_map/ppermute | solution.py:48
  87.4 0.0 collective-permute-done.6
  87.4 0.0 collective-permute-done.5
  87.5 0.0 collective-permute-done.4
  87.5 4.2 %collective-permute-done.10 = f16[56,1152]{1,0:T(8,128)(2,1)S(1)} collective-permute-done((f16[56,1152]{1,0:T(8,128)(2,1)S(1)}, f16[56,1152]{1,0:T(8,128)(2,1)S(1)}, u32[]{:S(2)}, u32[]{:S(2)}) %collective-permute-start.10) | collective-permute-done | bytes 129056 | tf_op jit(solution)/shard_map/ppermute | solution.py:48
  91.7 0.1 fusion.9
  91.8 0.1 slice_bitcast_fusion.3
  91.9 0.0 copy-done
  91.9 0.0 copy-done.1
  91.9 1.0 %add_divide_fusion = (f32[1,1,112,576]{3,2,1,0:T(8,128)}, f32[1,1,112,576]{3,2,1,0:T(8,128)}, f32[1,1,112,576]{3,2,1,0:T(8,128)}) fusion(f32[1,1,56,576]{3,2,1,0:T(8,128)S(1)} %get-tuple-element.34, f32[1,1,56,576]{3,2,1,0:T(8,128)S(1)} %get-tuple-element.33, f32[1,1,112,576]{3,2,1,0:T(8,128)S(1)} %copy-done, f32[1,1,112,576]{3,2,1,0:T(8,128)S(1)} %copy-done.1), kind=kLoop, calls=%fused_computation.15 | loop fusion | flops 645120 | bytes 1548288 | tf_op jit(solution)/shard_map/div | solution.py:172
Async XLA Ops:
  21.1 16.5 %collective-permute-start = (f16[8,56,1152]{2,1,0:T(8,128)(2,1)S(1)}, f16[8,56,1152]{2,1,0:T(8,128)(2,1)S(1)}, u32[]{:S(2)}, u32[]{:S(2)}) collective-permute-start(f16[8,56,1152]{2,1,0:T(8,128)(2,1)S(1)} %get-tuple-element.21), channel_id=1, source_target_pairs={{0,128},{1,385},{2,130},{3,387},{4,132},{5,389},{6,134},{7,391},{8... | collective-permute-start | bytes 3096584 | tf_op jit(solution)/shard_map/ppermute | solution.py:48
  27.9 22.9 %collective-permute-start.1 = (f16[8,56,1152]{2,1,0:T(8,128)(2,1)S(1)}, f16[8,56,1152]{2,1,0:T(8,128)(2,1)S(1)}, u32[]{:S(2)}, u32[]{:S(2)}) collective-permute-start(f16[8,56,1152]{2,1,0:T(8,128)(2,1)S(1)} %get-tuple-element.18), channel_id=1, source_target_pairs={{0,384},{1,33},{2,386},{3,35},{4,388},{5,37},{6,390},{7,39},{8,392... | collective-permute-start | bytes 3096584 | tf_op jit(solution)/shard_map/ppermute | solution.py:48
  38.0 15.1 %collective-permute-start.2 = (f16[4,56,1152]{2,1,0:T(8,128)(2,1)S(1)}, f16[4,56,1152]{2,1,0:T(8,128)(2,1)S(1)}, u32[]{:S(2)}, u32[]{:S(2)}) collective-permute-start(f16[4,56,1152]{2,1,0:T(8,128)(2,1)S(1)} %get-tuple-element.25), channel_id=1, source_target_pairs={{0,32},{1,129},{2,34},{3,131},{4,36},{5,133},{6,38},{7,135},{8,40}... | collective-permute-start | bytes 1548296 | tf_op jit(solution)/shard_map/ppermute | solution.py:48
  51.2 14.0 %collective-permute-start.3 = (f16[4,56,1152]{2,1,0:T(8,128)(2,1)S(1)}, f16[4,56,1152]{2,1,0:T(8,128)(2,1)S(1)}, u32[]{:S(2)}, u32[]{:S(2)}) collective-permute-start(f16[4,56,1152]{2,1,0:T(8,128)(2,1)S(1)} %get-tuple-element.22), channel_id=1, source_target_pairs={{0,128},{1,385},{2,130},{3,387},{4,132},{5,389},{6,134},{7,391},{8... | collective-permute-start | bytes 1548296 | tf_op jit(solution)/shard_map/ppermute | solution.py:48
  53.3 19.5 %collective-permute-start.9 = (f16[56,1152]{1,0:T(8,128)(2,1)S(1)}, f16[56,1152]{1,0:T(8,128)(2,1)S(1)}, u32[]{:S(2)}, u32[]{:S(2)}) collective-permute-start(f16[56,1152]{1,0:T(8,128)(2,1)S(1)} %get-tuple-element.30), channel_id=1, source_target_pairs={{0,448},{1,97},{2,450},{3,99},{4,452},{5,101},{6,454},{7,103},{8,4... | collective-permute-start | bytes 387080 | tf_op jit(solution)/shard_map/ppermute | solution.py:48
  58.8 16.9 %collective-permute-start.8 = (f16[56,1152]{1,0:T(8,128)(2,1)S(1)}, f16[56,1152]{1,0:T(8,128)(2,1)S(1)}, u32[]{:S(2)}, u32[]{:S(2)}) collective-permute-start(f16[56,1152]{1,0:T(8,128)(2,1)S(1)} %get-tuple-element.31), channel_id=1, source_target_pairs={{0,384},{1,33},{2,386},{3,35},{4,388},{5,37},{6,390},{7,39},{8,392... | collective-permute-start | bytes 387080 | tf_op jit(solution)/shard_map/ppermute | solution.py:48
  63.2 13.1 %collective-permute-start.7 = (f16[56,1152]{1,0:T(8,128)(2,1)S(1)}, f16[56,1152]{1,0:T(8,128)(2,1)S(1)}, u32[]{:S(2)}, u32[]{:S(2)}) collective-permute-start(f16[56,1152]{1,0:T(8,128)(2,1)S(1)} %get-tuple-element.32), channel_id=1, source_target_pairs={{0,64},{1,65},{2,66},{3,67},{4,68},{5,69},{6,70},{7,71},{8,72},{9,... | collective-permute-start | bytes 387080 | tf_op jit(solution)/shard_map/ppermute | solution.py:48
  65.3 26.6 %copy-start = (f32[1,1,112,576]{3,2,1,0:T(8,128)S(1)}, f32[1,1,112,576]{3,2,1,0:T(8,128)}, u32[]{:S(2)}) copy-start(f32[1,1,112,576]{3,2,1,0:T(8,128)} %param.9) | copy-start | bytes 774148
  65.3 26.6 %copy-start.1 = (f32[1,1,112,576]{3,2,1,0:T(8,128)S(1)}, f32[1,1,112,576]{3,2,1,0:T(8,128)}, u32[]{:S(2)}) copy-start(f32[1,1,112,576]{3,2,1,0:T(8,128)} %param.8) | copy-start | bytes 774148
  65.4 22.0 %collective-permute-start.6 = (f16[56,1152]{1,0:T(8,128)(2,1)S(1)}, f16[56,1152]{1,0:T(8,128)(2,1)S(1)}, u32[]{:S(2)}, u32[]{:S(2)}) collective-permute-start(f16[56,1152]{1,0:T(8,128)(2,1)S(1)} %get-tuple-element.26), channel_id=1, source_target_pairs={{0,96},{1,193},{2,98},{3,195},{4,100},{5,197},{6,102},{7,199},{8,1... | collective-permute-start | bytes 387080 | tf_op jit(solution)/shard_map/ppermute | solution.py:48
  70.9 16.6 %collective-permute-start.5 = (f16[56,1152]{1,0:T(8,128)(2,1)S(1)}, f16[56,1152]{1,0:T(8,128)(2,1)S(1)}, u32[]{:S(2)}, u32[]{:S(2)}) collective-permute-start(f16[56,1152]{1,0:T(8,128)(2,1)S(1)} %get-tuple-element.27), channel_id=1, source_target_pairs={{0,32},{1,129},{2,34},{3,131},{4,36},{5,133},{6,38},{7,135},{8,40}... | collective-permute-start | bytes 387080 | tf_op jit(solution)/shard_map/ppermute | solution.py:48
  72.9 14.6 %collective-permute-start.4 = (f16[56,1152]{1,0:T(8,128)(2,1)S(1)}, f16[56,1152]{1,0:T(8,128)(2,1)S(1)}, u32[]{:S(2)}, u32[]{:S(2)}) collective-permute-start(f16[56,1152]{1,0:T(8,128)(2,1)S(1)} %get-tuple-element.28), channel_id=1, source_target_pairs={{0,64},{1,65},{2,66},{3,67},{4,68},{5,69},{6,70},{7,71},{8,72},{9,... | collective-permute-start | bytes 387080 | tf_op jit(solution)/shard_map/ppermute | solution.py:48
  76.4 15.3 %collective-permute-start.10 = (f16[56,1152]{1,0:T(8,128)(2,1)S(1)}, f16[56,1152]{1,0:T(8,128)(2,1)S(1)}, u32[]{:S(2)}, u32[]{:S(2)}) collective-permute-start(f16[56,1152]{1,0:T(8,128)(2,1)S(1)} %multiply_convert_fusion), channel_id=1, source_target_pairs={{0,28},{1,29},{2,30},{3,31},{4,24},{5,25},{6,26},{7,27},{8,20},{9,... | collective-permute-start | bytes 387080 | tf_op jit(solution)/shard_map/ppermute | solution.py:48

commit v7 on v6

--- a/solution.py
+++ b/solution.py
@@ -16,7 +16,7 @@
 X_1, X_3, Y_1, Y_2 = 1 * NY, 3 * NY, 1, 2
 ORDERS = (
     ((X_3, X_1, Y_1, Y_2), (Y_1, X_3, X_1, Y_2)),
-    ((X_1, Y_1, X_3, Y_2), (X_3, X_1, Y_1, Y_2)),
+    ((X_1, Y_1, X_3, Y_2), (X_3, X_1, Y_2, Y_1)),
 )
 
 
@@ -164,7 +164,8 @@
 
     other = total(after(other, *own_out), other_in)
     from_mirror = send(narrow(other, SCALES[4]), mirrored)
-    grad = total(own, own_in) + widen(from_mirror, SCALES[4])
+    own = lax.optimization_barrier(total(own, own_in))
+    grad = own + widen(from_mirror, SCALES[4])
     width = out_grads.shape[-1]
     grad = jnp.concatenate([grad[:, :width], grad[:, width:]])[None, None]
     new_first = 0.9 * first_moment + 0.1 * grad

time: 93.4 us -> 96.2 us (1.030)
  starting transfers between devices: 48.8 us -> 50.3 us
  waiting for transfers between devices: 16.3 us -> 17.6 us
    ppermute x11, starting transfers between devices: 48.8 us -> 50.3 us  [send(): return lax.ppermute(block, AXES, pairs)]
    ppermute x11, waiting for transfers between devices: 16.3 us -> 17.6 us  [send(): return lax.ppermute(block, AXES, pairs)]
where the time goes in v7:
time: 96.2 us; the launch traced here: 95.8 us
  starting transfers between devices  50.3 us (52%)
  waiting for transfers between devices  17.6 us (18%)
  blocking collectives  16.5 us (17%)
  Pallas kernels  7.5 us (8%)
  other arithmetic  2.86 us (3%)
    ppermute x11, starting transfers between devices, send(): return lax.ppermute(block, AXES, pairs)  50.3 us
    ppermute x11, waiting for transfers between devices, send(): return lax.ppermute(block, AXES, pairs)  17.6 us
    all_gather x1, blocking collectives, local(): grads = lax.all_gather(out_grads[0, 0], 'expert')  16.5 us
    pallas_call x2, Pallas kernels, multiply_span(): pl.pallas_call(functools.partial(span_kernel, span), grid_spec=pltpu.Pref...  7.5 us
  transfers between devices with their start and end apart: 11, of which 4 were waited for; matrix products, arithmetic and copies ran while one was open for 2% of the time, Pallas kernels for 4%

profile of v7, /device:TPU:6, one launch (start us, length us, event | category | flops | bytes accessed | tf_op | source)
XLA Modules:
  0.0 95.8 jit_solution(7154779800588740818)
XLA Ops:
  0.6 16.5 %all-gather = bf16[4,1,2,96,576]{4,3,2,1,0:T(8,128)(2,1)S(1)} all-gather(bf16[1,1,2,96,576]{4,3,2,1,0:T(8,128)(2,1)} %param.6), channel_id=2, replica_groups=mesh['dp'=16,'pipe'=8,'expert'=4] {'expert'}, dimensions={0}, use_global_device_ids=true | all-gather | bytes 1105920 | tf_op jit(solution)/shard_map/all_gather | solution.py:137
  17.1 3.7 %shard_map.76 = f32[16,56,1152]{2,1,0:T(8,128)S(1)} custom-call(s32[2]{0:T(128)} %bitcast.26, bf16[1,1,2,384,1792]{4,3,2,1,0:T(8,128)(2,1)} %acts.3, bf16[4,2,96,576]{3,2,1,0:T(8,128)(2,1)S(1)} %bitcast.24), custom_call_target="tpu_custom_call" | custom-call | flops 792723456 | bytes 6291456 | tf_op jit(solution)/shard_map/pallas_call | solution.py:105
  20.9 0.2 fusion.19
  21.1 2.7 %collective-permute-start = (f16[8,56,1152]{2,1,0:T(8,128)(2,1)S(1)}, f16[8,56,1152]{2,1,0:T(8,128)(2,1)S(1)}, u32[]{:S(2)}, u32[]{:S(2)}) collective-permute-start(f16[8,56,1152]{2,1,0:T(8,128)(2,1)S(1)} %get-tuple-element.21), channel_id=1, source_target_pairs={{0,128},{1,385},{2,130},{3,387},{4,132},{5,389},{6,134},{7,391},{8... | collective-permute-start | bytes 3096584 | tf_op jit(solution)/shard_map/ppermute | solution.py:48
  23.9 3.8 %shard_map.77 = f32[16,56,1152]{2,1,0:T(8,128)S(1)} custom-call(s32[2]{0:T(128)} %bitcast.27, bf16[1,1,2,384,1792]{4,3,2,1,0:T(8,128)(2,1)} %acts.3, bf16[4,2,96,576]{3,2,1,0:T(8,128)(2,1)S(1)} %bitcast.25), custom_call_target="tpu_custom_call" | custom-call | flops 792723456 | bytes 6291456 | tf_op jit(solution)/shard_map/pallas_call | solution.py:105
  27.6 0.2 fusion
  27.9 5.5 %collective-permute-start.1 = (f16[8,56,1152]{2,1,0:T(8,128)(2,1)S(1)}, f16[8,56,1152]{2,1,0:T(8,128)(2,1)S(1)}, u32[]{:S(2)}, u32[]{:S(2)}) collective-permute-start(f16[8,56,1152]{2,1,0:T(8,128)(2,1)S(1)} %get-tuple-element.18), channel_id=1, source_target_pairs={{0,384},{1,33},{2,386},{3,35},{4,388},{5,37},{6,390},{7,39},{8,392... | collective-permute-start | bytes 3096584 | tf_op jit(solution)/shard_map/ppermute | solution.py:48
  33.4 4.2 %collective-permute-done = f16[8,56,1152]{2,1,0:T(8,128)(2,1)S(1)} collective-permute-done((f16[8,56,1152]{2,1,0:T(8,128)(2,1)S(1)}, f16[8,56,1152]{2,1,0:T(8,128)(2,1)S(1)}, u32[]{:S(2)}, u32[]{:S(2)}) %collective-permute-start) | collective-permute-done | bytes 1032224 | tf_op jit(solution)/shard_map/ppermute | solution.py:48
  37.6 0.2 multiply_add_fusion.1
  37.9 0.1 fusion.20
  38.0 5.6 %collective-permute-start.2 = (f16[4,56,1152]{2,1,0:T(8,128)(2,1)S(1)}, f16[4,56,1152]{2,1,0:T(8,128)(2,1)S(1)}, u32[]{:S(2)}, u32[]{:S(2)}) collective-permute-start(f16[4,56,1152]{2,1,0:T(8,128)(2,1)S(1)} %get-tuple-element.25), channel_id=1, source_target_pairs={{0,32},{1,129},{2,34},{3,131},{4,36},{5,133},{6,38},{7,135},{8,40}... | collective-permute-start | bytes 1548296 | tf_op jit(solution)/shard_map/ppermute | solution.py:48
  43.6 7.1 %collective-permute-done.1 = f16[8,56,1152]{2,1,0:T(8,128)(2,1)S(1)} collective-permute-done((f16[8,56,1152]{2,1,0:T(8,128)(2,1)S(1)}, f16[8,56,1152]{2,1,0:T(8,128)(2,1)S(1)}, u32[]{:S(2)}, u32[]{:S(2)}) %collective-permute-start.1) | collective-permute-done | bytes 1032224 | tf_op jit(solution)/shard_map/ppermute | solution.py:48
  50.8 0.3 multiply_add_fusion
  51.1 0.1 fusion.2
  51.2 1.9 %collective-permute-start.3 = (f16[4,56,1152]{2,1,0:T(8,128)(2,1)S(1)}, f16[4,56,1152]{2,1,0:T(8,128)(2,1)S(1)}, u32[]{:S(2)}, u32[]{:S(2)}) collective-permute-start(f16[4,56,1152]{2,1,0:T(8,128)(2,1)S(1)} %get-tuple-element.22), channel_id=1, source_target_pairs={{0,128},{1,385},{2,130},{3,387},{4,132},{5,389},{6,134},{7,391},{8... | collective-permute-start | bytes 1548296 | tf_op jit(solution)/shard_map/ppermute | solution.py:48
  53.1 0.0 collective-permute-done.2
  53.1 0.1 multiply_add_fusion.3
  53.3 0.1 slice_bitcast_fusion
  53.3 5.5 %collective-permute-start.9 = (f16[56,1152]{1,0:T(8,128)(2,1)S(1)}, f16[56,1152]{1,0:T(8,128)(2,1)S(1)}, u32[]{:S(2)}, u32[]{:S(2)}) collective-permute-start(f16[56,1152]{1,0:T(8,128)(2,1)S(1)} %get-tuple-element.27), channel_id=1, source_target_pairs={{0,448},{1,97},{2,450},{3,99},{4,452},{5,101},{6,454},{7,103},{8,4... | collective-permute-start | bytes 387080 | tf_op jit(solution)/shard_map/ppermute | solution.py:48
  58.8 4.4 %collective-permute-start.8 = (f16[56,1152]{1,0:T(8,128)(2,1)S(1)}, f16[56,1152]{1,0:T(8,128)(2,1)S(1)}, u32[]{:S(2)}, u32[]{:S(2)}) collective-permute-start(f16[56,1152]{1,0:T(8,128)(2,1)S(1)} %get-tuple-element.28), channel_id=1, source_target_pairs={{0,384},{1,65},{2,386},{3,67},{4,388},{5,69},{6,390},{7,71},{8,392... | collective-permute-start | bytes 387080 | tf_op jit(solution)/shard_map/ppermute | solution.py:48
  63.2 1.9 %collective-permute-start.7 = (f16[56,1152]{1,0:T(8,128)(2,1)S(1)}, f16[56,1152]{1,0:T(8,128)(2,1)S(1)}, u32[]{:S(2)}, u32[]{:S(2)}) collective-permute-start(f16[56,1152]{1,0:T(8,128)(2,1)S(1)} %get-tuple-element.29), channel_id=1, source_target_pairs={{0,64},{1,33},{2,66},{3,35},{4,68},{5,37},{6,70},{7,39},{8,72},{9,... | collective-permute-start | bytes 387080 | tf_op jit(solution)/shard_map/ppermute | solution.py:48
  65.2 0.0 collective-permute-done.3
  65.2 0.1 multiply_add_fusion.2
  65.3 0.0 copy-start
  65.3 0.0 copy-start.1
  65.3 0.1 fusion.15
  65.4 5.0 %collective-permute-start.4 = (f16[56,1152]{1,0:T(8,128)(2,1)S(1)}, f16[56,1152]{1,0:T(8,128)(2,1)S(1)}, u32[]{:S(2)}, u32[]{:S(2)}) collective-permute-start(f16[56,1152]{1,0:T(8,128)(2,1)S(1)} %get-tuple-element.30), channel_id=1, source_target_pairs={{0,64},{1,65},{2,66},{3,67},{4,68},{5,69},{6,70},{7,71},{8,72},{9,... | collective-permute-start | bytes 387080 | tf_op jit(solution)/shard_map/ppermute | solution.py:48
  70.4 3.1 %collective-permute-start.6 = (f16[56,1152]{1,0:T(8,128)(2,1)S(1)}, f16[56,1152]{1,0:T(8,128)(2,1)S(1)}, u32[]{:S(2)}, u32[]{:S(2)}) collective-permute-start(f16[56,1152]{1,0:T(8,128)(2,1)S(1)} %get-tuple-element.31), channel_id=1, source_target_pairs={{0,96},{1,193},{2,98},{3,195},{4,100},{5,197},{6,102},{7,199},{8,1... | collective-permute-start | bytes 387080 | tf_op jit(solution)/shard_map/ppermute | solution.py:48
  73.5 0.0 collective-permute-done.9
  73.5 1.9 %collective-permute-start.5 = (f16[56,1152]{1,0:T(8,128)(2,1)S(1)}, f16[56,1152]{1,0:T(8,128)(2,1)S(1)}, u32[]{:S(2)}, u32[]{:S(2)}) collective-permute-start(f16[56,1152]{1,0:T(8,128)(2,1)S(1)} %get-tuple-element.32), channel_id=1, source_target_pairs={{0,32},{1,129},{2,34},{3,131},{4,36},{5,133},{6,38},{7,135},{8,40}... | collective-permute-start | bytes 387080 | tf_op jit(solution)/shard_map/ppermute | solution.py:48
  75.4 0.0 collective-permute-done.8
  75.5 2.0 %collective-permute-done.7 = f16[56,1152]{1,0:T(8,128)(2,1)S(1)} collective-permute-done((f16[56,1152]{1,0:T(8,128)(2,1)S(1)}, f16[56,1152]{1,0:T(8,128)(2,1)S(1)}, u32[]{:S(2)}, u32[]{:S(2)}) %collective-permute-start.7) | collective-permute-done | bytes 129056 | tf_op jit(solution)/shard_map/ppermute | solution.py:48
  77.5 0.1 multiply_convert_fusion
  77.6 12.7 %collective-permute-start.10 = (f16[56,1152]{1,0:T(8,128)(2,1)S(1)}, f16[56,1152]{1,0:T(8,128)(2,1)S(1)}, u32[]{:S(2)}, u32[]{:S(2)}) collective-permute-start(f16[56,1152]{1,0:T(8,128)(2,1)S(1)} %multiply_convert_fusion), channel_id=1, source_target_pairs={{0,28},{1,29},{2,30},{3,31},{4,24},{5,25},{6,26},{7,27},{8,20},{9,... | collective-permute-start | bytes 387080 | tf_op jit(solution)/shard_map/ppermute | solution.py:48
  90.3 0.0 collective-permute-done.4
  90.3 0.0 collective-permute-done.6
  90.4 0.0 collective-permute-done.5
  90.4 0.1 fusion.8
  90.4 4.2 %collective-permute-done.10 = f16[56,1152]{1,0:T(8,128)(2,1)S(1)} collective-permute-done((f16[56,1152]{1,0:T(8,128)(2,1)S(1)}, f16[56,1152]{1,0:T(8,128)(2,1)S(1)}, u32[]{:S(2)}, u32[]{:S(2)}) %collective-permute-start.10) | collective-permute-done | bytes 129056 | tf_op jit(solution)/shard_map/ppermute | solution.py:48
  94.7 0.1 slice_bitcast_fusion.3
  94.8 0.0 copy-done
  94.8 0.0 copy-done.1
  94.8 1.0 %add_divide_fusion = (f32[1,1,112,576]{3,2,1,0:T(8,128)}, f32[1,1,112,576]{3,2,1,0:T(8,128)}, f32[1,1,112,576]{3,2,1,0:T(8,128)}) fusion(f32[1,1,56,576]{3,2,1,0:T(8,128)S(1)} %get-tuple-element.34, f32[1,1,56,576]{3,2,1,0:T(8,128)S(1)} %get-tuple-element.33, f32[1,1,112,576]{3,2,1,0:T(8,128)S(1)} %copy-done, f32[1,1,112,576]{3,2,1,0:T(8,128)S(1)} %copy-done.1), kind=kLoop, calls=%fused_computation.15 | loop fusion | flops 645120 | bytes 1548288 | tf_op jit(solution)/shard_map/div | solution.py:173
  (1 shorter events, 0.0 us)
Async XLA Ops:
  21.1 16.5 %collective-permute-start = (f16[8,56,1152]{2,1,0:T(8,128)(2,1)S(1)}, f16[8,56,1152]{2,1,0:T(8,128)(2,1)S(1)}, u32[]{:S(2)}, u32[]{:S(2)}) collective-permute-start(f16[8,56,1152]{2,1,0:T(8,128)(2,1)S(1)} %get-tuple-element.21), channel_id=1, source_target_pairs={{0,128},{1,385},{2,130},{3,387},{4,132},{5,389},{6,134},{7,391},{8... | collective-permute-start | bytes 3096584 | tf_op jit(solution)/shard_map/ppermute | solution.py:48
  27.9 22.9 %collective-permute-start.1 = (f16[8,56,1152]{2,1,0:T(8,128)(2,1)S(1)}, f16[8,56,1152]{2,1,0:T(8,128)(2,1)S(1)}, u32[]{:S(2)}, u32[]{:S(2)}) collective-permute-start(f16[8,56,1152]{2,1,0:T(8,128)(2,1)S(1)} %get-tuple-element.18), channel_id=1, source_target_pairs={{0,384},{1,33},{2,386},{3,35},{4,388},{5,37},{6,390},{7,39},{8,392... | collective-permute-start | bytes 3096584 | tf_op jit(solution)/shard_map/ppermute | solution.py:48
  38.0 15.1 %collective-permute-start.2 = (f16[4,56,1152]{2,1,0:T(8,128)(2,1)S(1)}, f16[4,56,1152]{2,1,0:T(8,128)(2,1)S(1)}, u32[]{:S(2)}, u32[]{:S(2)}) collective-permute-start(f16[4,56,1152]{2,1,0:T(8,128)(2,1)S(1)} %get-tuple-element.25), channel_id=1, source_target_pairs={{0,32},{1,129},{2,34},{3,131},{4,36},{5,133},{6,38},{7,135},{8,40}... | collective-permute-start | bytes 1548296 | tf_op jit(solution)/shard_map/ppermute | solution.py:48
  51.2 14.0 %collective-permute-start.3 = (f16[4,56,1152]{2,1,0:T(8,128)(2,1)S(1)}, f16[4,56,1152]{2,1,0:T(8,128)(2,1)S(1)}, u32[]{:S(2)}, u32[]{:S(2)}) collective-permute-start(f16[4,56,1152]{2,1,0:T(8,128)(2,1)S(1)} %get-tuple-element.22), channel_id=1, source_target_pairs={{0,128},{1,385},{2,130},{3,387},{4,132},{5,389},{6,134},{7,391},{8... | collective-permute-start | bytes 1548296 | tf_op jit(solution)/shard_map/ppermute | solution.py:48
  53.3 20.2 %collective-permute-start.9 = (f16[56,1152]{1,0:T(8,128)(2,1)S(1)}, f16[56,1152]{1,0:T(8,128)(2,1)S(1)}, u32[]{:S(2)}, u32[]{:S(2)}) collective-permute-start(f16[56,1152]{1,0:T(8,128)(2,1)S(1)} %get-tuple-element.27), channel_id=1, source_target_pairs={{0,448},{1,97},{2,450},{3,99},{4,452},{5,101},{6,454},{7,103},{8,4... | collective-permute-start | bytes 387080 | tf_op jit(solution)/shard_map/ppermute | solution.py:48
  58.8 16.6 %collective-permute-start.8 = (f16[56,1152]{1,0:T(8,128)(2,1)S(1)}, f16[56,1152]{1,0:T(8,128)(2,1)S(1)}, u32[]{:S(2)}, u32[]{:S(2)}) collective-permute-start(f16[56,1152]{1,0:T(8,128)(2,1)S(1)} %get-tuple-element.28), channel_id=1, source_target_pairs={{0,384},{1,65},{2,386},{3,67},{4,388},{5,69},{6,390},{7,71},{8,392... | collective-permute-start | bytes 387080 | tf_op jit(solution)/shard_map/ppermute | solution.py:48
  63.2 14.3 %collective-permute-start.7 = (f16[56,1152]{1,0:T(8,128)(2,1)S(1)}, f16[56,1152]{1,0:T(8,128)(2,1)S(1)}, u32[]{:S(2)}, u32[]{:S(2)}) collective-permute-start(f16[56,1152]{1,0:T(8,128)(2,1)S(1)} %get-tuple-element.29), channel_id=1, source_target_pairs={{0,64},{1,33},{2,66},{3,35},{4,68},{5,37},{6,70},{7,39},{8,72},{9,... | collective-permute-start | bytes 387080 | tf_op jit(solution)/shard_map/ppermute | solution.py:48
  65.3 29.5 %copy-start = (f32[1,1,112,576]{3,2,1,0:T(8,128)S(1)}, f32[1,1,112,576]{3,2,1,0:T(8,128)}, u32[]{:S(2)}) copy-start(f32[1,1,112,576]{3,2,1,0:T(8,128)} %param.9) | copy-start | bytes 774148
  65.3 29.4 %copy-start.1 = (f32[1,1,112,576]{3,2,1,0:T(8,128)S(1)}, f32[1,1,112,576]{3,2,1,0:T(8,128)}, u32[]{:S(2)}) copy-start(f32[1,1,112,576]{3,2,1,0:T(8,128)} %param.8) | copy-start | bytes 774148
  65.4 24.9 %collective-permute-start.4 = (f16[56,1152]{1,0:T(8,128)(2,1)S(1)}, f16[56,1152]{1,0:T(8,128)(2,1)S(1)}, u32[]{:S(2)}, u32[]{:S(2)}) collective-permute-start(f16[56,1152]{1,0:T(8,128)(2,1)S(1)} %get-tuple-element.30), channel_id=1, source_target_pairs={{0,64},{1,65},{2,66},{3,67},{4,68},{5,69},{6,70},{7,71},{8,72},{9,... | collective-permute-start | bytes 387080 | tf_op jit(solution)/shard_map/ppermute | solution.py:48
  70.4 20.0 %collective-permute-start.6 = (f16[56,1152]{1,0:T(8,128)(2,1)S(1)}, f16[56,1152]{1,0:T(8,128)(2,1)S(1)}, u32[]{:S(2)}, u32[]{:S(2)}) collective-permute-start(f16[56,1152]{1,0:T(8,128)(2,1)S(1)} %get-tuple-element.31), channel_id=1, source_target_pairs={{0,96},{1,193},{2,98},{3,195},{4,100},{5,197},{6,102},{7,199},{8,1... | collective-permute-start | bytes 387080 | tf_op jit(solution)/shard_map/ppermute | solution.py:48
  73.5 16.8 %collective-permute-start.5 = (f16[56,1152]{1,0:T(8,128)(2,1)S(1)}, f16[56,1152]{1,0:T(8,128)(2,1)S(1)}, u32[]{:S(2)}, u32[]{:S(2)}) collective-permute-start(f16[56,1152]{1,0:T(8,128)(2,1)S(1)} %get-tuple-element.32), channel_id=1, source_target_pairs={{0,32},{1,129},{2,34},{3,131},{4,36},{5,133},{6,38},{7,135},{8,40}... | collective-permute-start | bytes 387080 | tf_op jit(solution)/shard_map/ppermute | solution.py:48
  77.6 17.0 %collective-permute-start.10 = (f16[56,1152]{1,0:T(8,128)(2,1)S(1)}, f16[56,1152]{1,0:T(8,128)(2,1)S(1)}, u32[]{:S(2)}, u32[]{:S(2)}) collective-permute-start(f16[56,1152]{1,0:T(8,128)(2,1)S(1)} %multiply_convert_fusion), channel_id=1, source_target_pairs={{0,28},{1,29},{2,30},{3,31},{4,24},{5,25},{6,26},{7,27},{8,20},{9,... | collective-permute-start | bytes 387080 | tf_op jit(solution)/shard_map/ppermute | solution.py:48
